TPU v7x, 256 devices: a whole 4x4x8 slice. The times are simulated.
256 devices in a mesh: seq: 16 (over z_lo, x, core), head: 16 (over z_hi, y).
Axes of the slice: x: 4, y: 4, z: 8 (z_hi: 4, z_lo: 2; z = z_hi * 2 + z_lo), core: 2. Of those that a mesh axis runs over, the one named last changes fastest.
Arguments:
- queries: bfloat16 [32768, 4096], P(('seq', 'head')), may hold values from -6 to 6
- outputs: bfloat16 [32768, 4096], P(('seq', 'head')), may hold values from -6 to 6
- out_grads: bfloat16 [32768, 4096], P(('seq', 'head')), may hold values from -0.5 to 0.5
- log_norms: bfloat16 [32768, 32], P(('seq', 'head')), may hold values from 2 to 5
- keys: bfloat16 [32768, 512], P(('seq', 'head')), may hold values from -6 to 6
- values: bfloat16 [32768, 512], P(('seq', 'head')), may hold values from -6 to 6
- doc_start: int32 [256], P('seq'), may hold values from 0 to 255, as said below
Outputs:
- query_grads: bfloat16 [32768, 4096], P(('seq', 'head'))
- key_grads: bfloat16 [32768, 512], P(('seq', 'head'))
- value_grads: bfloat16 [32768, 512], P(('seq', 'head'))
Inputs may be any that keep to these rules, and one draw needn't show every extreme that they name: doc_start never falls, doc_start[b] <= b, and equals b exactly where a document begins; every document covers 1 to 8 blocks, one document of exactly 8 blocks has 7 of its blocks before block 16 and one at it, and the last block begins a document.
All inputs are finite; a program needn't handle non-finite values.
Results may differ from a plain program's by a relative error of at most 0.0053.
Values may be sent and summed in bfloat16 or wider, within the bound.
No kernel may reach another device: no remote copies, remote signals or barrier semaphores. Data moves between devices by JAX's collectives and lax.ppermute only.
A program may use at most 128 MiB of HBM per device.

v0:
```python
import jax
import jax.numpy as jnp
from jax import lax
from jax.sharding import PartitionSpec as P

H = 32
KVH = 4
DH = 128
BLOCK = 128
TAIL = 896


def from_behind(value, axis, by):
    length = lax.axis_size(axis)
    pairs = [(i, i + by) for i in range(length) if 0 <= i + by < length]
    return lax.ppermute(value, axis, pairs)


def core_grads(query_part, grad_part, dot_part, norm_part, key_part, value_part, visible):
    scale = DH ** (-0.5)
    scores = (
        jnp.einsum("rhgd,khd->hgrk", query_part, key_part, preferred_element_type=jnp.float32)
        * scale
    )
    norm_moved = jnp.transpose(norm_part, (1, 2, 0))[..., None]
    weights = jnp.where(visible[None, None], jnp.exp(scores - norm_moved), 0.0)
    weight_bf = weights.astype(jnp.bfloat16)
    grad_weights = jnp.einsum(
        "rhgd,khd->hgrk", grad_part, value_part, preferred_element_type=jnp.float32
    )
    dot_moved = jnp.transpose(dot_part, (1, 2, 0))[..., None]
    grad_scores = (weights * (grad_weights - dot_moved)).astype(jnp.bfloat16)
    value_grad = jnp.einsum(
        "hgrk,rhgd->khd", weight_bf, grad_part, preferred_element_type=jnp.float32
    )
    key_grad = (
        jnp.einsum("hgrk,rhgd->khd", grad_scores, query_part, preferred_element_type=jnp.float32)
        * scale
    )
    query_grad = (
        jnp.einsum("hgrk,khd->rhgd", grad_scores, key_part, preferred_element_type=jnp.float32)
        * scale
    )
    return (query_grad, key_grad, value_grad)


def sweep(query4, grad4, dot3, norm3, key_ext, value_ext, query_doc, first_pos, block_rows):
    row_count = query4.shape[0]
    tail_rows = key_ext.shape[0] - row_count
    span = block_rows + tail_rows
    zeros = jnp.zeros(key_ext.shape, jnp.float32)

    def turn(carry, number):
        key_acc, value_acc = carry
        start = number * block_rows

        def window(array, length):
            return lax.dynamic_slice_in_dim(array, start, length, 0)

        query_pos = first_pos + start + jnp.arange(block_rows, dtype=jnp.int32)
        key_pos = first_pos - tail_rows + start + jnp.arange(span, dtype=jnp.int32)
        visible = (key_pos[None, :] <= query_pos[:, None]) & (
            (key_pos // BLOCK)[None, :] >= window(query_doc, block_rows)[:, None]
        )
        query_grad, key_grad, value_grad = core_grads(
            window(query4, block_rows),
            window(grad4, block_rows),
            window(dot3, block_rows),
            window(norm3, block_rows),
            window(key_ext, span),
            window(value_ext, span),
            visible,
        )
        key_acc = lax.dynamic_update_slice_in_dim(
            key_acc, window(key_acc, span) + key_grad, start, 0
        )
        value_acc = lax.dynamic_update_slice_in_dim(
            value_acc, window(value_acc, span) + value_grad, start, 0
        )
        return ((key_acc, value_acc), query_grad)

    (key_acc, value_acc), query_grads = lax.scan(
        turn, (zeros, zeros), jnp.arange(row_count // block_rows, dtype=jnp.int32)
    )
    return (query_grads.reshape(query4.shape), key_acc, value_acc)


def per_device(queries, outputs, out_grads, log_norms, keys, values, doc_start):
    tok_rows = queries.shape[0]
    head_count = lax.axis_size("head")
    tail_rows = TAIL
    kv_rep = max(1, head_count // KVH)
    kv_wide = KVH * kv_rep
    kv_local = kv_wide // head_count
    heads_local = H // head_count
    group_local = heads_local // kv_local
    key_wide = jnp.broadcast_to(
        keys.reshape(tok_rows, KVH, 1, DH), (tok_rows, KVH, kv_rep, DH)
    ).reshape(tok_rows, kv_wide * DH)
    value_wide = jnp.broadcast_to(
        values.reshape(tok_rows, KVH, 1, DH), (tok_rows, KVH, kv_rep, DH)
    ).reshape(tok_rows, kv_wide * DH)
    query_g, output_g, grad_g, key_g, value_g, norm_g = (
        lax.all_to_all(queries, "head", split_axis=1, concat_axis=0, tiled=True),
        lax.all_to_all(outputs, "head", split_axis=1, concat_axis=0, tiled=True),
        lax.all_to_all(out_grads, "head", split_axis=1, concat_axis=0, tiled=True),
        lax.all_to_all(key_wide, "head", split_axis=1, concat_axis=0, tiled=True),
        lax.all_to_all(value_wide, "head", split_axis=1, concat_axis=0, tiled=True),
        lax.all_to_all(log_norms, "head", split_axis=1, concat_axis=0, tiled=True),
    )
    group_rows = query_g.shape[0]
    query4 = query_g.reshape(group_rows, kv_local, group_local, DH)
    grad4 = grad_g.reshape(group_rows, kv_local, group_local, DH)
    output4 = output_g.reshape(group_rows, kv_local, group_local, DH)
    dot3 = jnp.sum(grad4.astype(jnp.float32) * output4.astype(jnp.float32), axis=-1)
    norm3 = norm_g.reshape(group_rows, kv_local, group_local).astype(jnp.float32)
    key3 = key_g.reshape(group_rows, kv_local, DH)
    value3 = value_g.reshape(group_rows, kv_local, DH)
    prior_key, prior_value = from_behind(
        (key3[group_rows - tail_rows :], value3[group_rows - tail_rows :]), "seq", 1
    )
    key_ext = jnp.concatenate([prior_key, key3], axis=0)
    value_ext = jnp.concatenate([prior_value, value3], axis=0)
    query_doc = jnp.repeat(doc_start, BLOCK, total_repeat_length=group_rows)
    first_pos = lax.axis_index("seq") * group_rows
    block_rows = min(group_rows, max(512, group_rows // 16))
    query_grad, key_acc, value_acc = sweep(
        query4, grad4, dot3, norm3, key_ext, value_ext, query_doc, first_pos, block_rows
    )
    back_key, back_value = from_behind((key_acc[:tail_rows], value_acc[:tail_rows]), "seq", -1)
    own_key = key_acc[tail_rows:]
    own_value = value_acc[tail_rows:]
    cut = group_rows - tail_rows
    own_key = jnp.concatenate([own_key[:cut], own_key[cut:] + back_key], axis=0)
    own_value = jnp.concatenate([own_value[:cut], own_value[cut:] + back_value], axis=0)
    query_out = lax.all_to_all(
        query_grad.astype(jnp.bfloat16).reshape(group_rows, heads_local * DH),
        "head",
        split_axis=0,
        concat_axis=1,
        tiled=True,
    )
    key_tok, value_tok = (
        lax.all_to_all(
            own_key.reshape(group_rows, kv_local * DH),
            "head",
            split_axis=0,
            concat_axis=1,
            tiled=True,
        ),
        lax.all_to_all(
            own_value.reshape(group_rows, kv_local * DH),
            "head",
            split_axis=0,
            concat_axis=1,
            tiled=True,
        ),
    )
    key_out = (
        jnp.sum(key_tok.reshape(tok_rows, KVH, kv_rep, DH), axis=2)
        .astype(jnp.bfloat16)
        .reshape(tok_rows, KVH * DH)
    )
    value_out = (
        jnp.sum(value_tok.reshape(tok_rows, KVH, kv_rep, DH), axis=2)
        .astype(jnp.bfloat16)
        .reshape(tok_rows, KVH * DH)
    )
    return (query_out, key_out, value_out)


def solution(mesh):
    placed = (
        P(("seq", "head"), None),
        P(("seq", "head"), None),
        P(("seq", "head"), None),
        P(("seq", "head"), None),
        P(("seq", "head"), None),
        P(("seq", "head"), None),
        P("seq"),
    )
    return jax.shard_map(
        per_device,
        mesh=mesh,
        in_specs=placed,
        out_specs=(P(("seq", "head"), None), P(("seq", "head"), None), P(("seq", "head"), None)),
        check_vma=False,
    )
```

profile of v0, /device:TPU:34, one launch (start us, length us, event | category | flops | bytes accessed | tf_op | source)
XLA Modules:
  0.0 341.0 jit_solution(8349104317636208019)
XLA Ops:
  0.7 10.4 %all-to-all-start.2 = ((bf16[128,16,2]{0,2,1:T(2,128)(2,1)}), bf16[128,16,2]{0,2,1:T(2,128)(2,1)S(1)}, u32[]{:S(2)}, u32[]{:S(2)}) async-start(bf16[128,16,2]{0,2,1:T(2,128)(2,1)} %bitcast.230), calls=%async_computation.2 | async-start | bytes 16384 | tf_op jit(solution)/shard_map/all_to_all | solution.py:109
  11.1 9.8 %all-to-all-done.2 = bf16[128,16,2]{0,2,1:T(2,128)(2,1)S(1)} async-done(((bf16[128,16,2]{0,2,1:T(2,128)(2,1)}), bf16[128,16,2]{0,2,1:T(2,128)(2,1)S(1)}, u32[]{:S(2)}, u32[]{:S(2)}) %all-to-all-start.2) | async-done | bytes 8224 | tf_op jit(solution)/shard_map/all_to_all | solution.py:109
  21.9 3.6 %all-to-all-start.3 = ((bf16[128,16,128]{2,0,1:T(8,128)(2,1)}), bf16[128,16,128]{2,0,1:T(8,128)(2,1)S(1)}, u32[]{:S(2)}, u32[]{:S(2)}) async-start(bf16[128,16,128]{2,0,1:T(8,128)(2,1)} %bitcast.57), calls=%async_computation.3 | async-start | bytes 1048576 | tf_op jit(solution)/shard_map/all_to_all | solution.py:108
  26.4 15.5 %all-to-all-done.3 = bf16[128,16,128]{2,0,1:T(8,128)(2,1)S(1)} async-done(((bf16[128,16,128]{2,0,1:T(8,128)(2,1)}), bf16[128,16,128]{2,0,1:T(8,128)(2,1)S(1)}, u32[]{:S(2)}, u32[]{:S(2)}) %all-to-all-start.3) | async-done | bytes 524320 | tf_op jit(solution)/shard_map/all_to_all | solution.py:108
  42.8 4.5 %all-to-all-start.1 = ((bf16[128,16,128]{2,0,1:T(8,128)(2,1)}), bf16[128,16,128]{2,0,1:T(8,128)(2,1)S(1)}, u32[]{:S(2)}, u32[]{:S(2)}) async-start(bf16[128,16,128]{2,0,1:T(8,128)(2,1)} %bitcast.50), calls=%async_computation.1 | async-start | bytes 1048576 | tf_op jit(solution)/shard_map/all_to_all | solution.py:107
  48.6 14.0 %all-to-all-done.1 = bf16[128,16,128]{2,0,1:T(8,128)(2,1)S(1)} async-done(((bf16[128,16,128]{2,0,1:T(8,128)(2,1)}), bf16[128,16,128]{2,0,1:T(8,128)(2,1)S(1)}, u32[]{:S(2)}, u32[]{:S(2)}) %all-to-all-start.1) | async-done | bytes 524320 | tf_op jit(solution)/shard_map/all_to_all | solution.py:107
  62.6 4.5 %all-to-all-start = ((bf16[128,16,256]{0,2,1:T(8,128)(2,1)}), bf16[128,16,256]{0,2,1:T(8,128)(2,1)S(1)}, u32[]{:S(2)}, u32[]{:S(2)}) async-start(bf16[128,16,256]{0,2,1:T(8,128)(2,1)} %bitcast.27), calls=%async_computation | async-start | bytes 2097152 | tf_op jit(solution)/shard_map/all_to_all | solution.py:104
  68.5 26.3 %all-to-all-done = bf16[128,16,256]{0,2,1:T(8,128)(2,1)S(1)} async-done(((bf16[128,16,256]{0,2,1:T(8,128)(2,1)}), bf16[128,16,256]{0,2,1:T(8,128)(2,1)S(1)}, u32[]{:S(2)}, u32[]{:S(2)}) %all-to-all-start) | async-done | bytes 1048608 | tf_op jit(solution)/shard_map/all_to_all | solution.py:104
  94.7 3.8 %all-to-all-start.5 = ((bf16[128,16,256]{0,2,1:T(8,128)(2,1)}), bf16[128,16,256]{0,2,1:T(8,128)(2,1)S(1)}, u32[]{:S(2)}, u32[]{:S(2)}) async-start(bf16[128,16,256]{0,2,1:T(8,128)(2,1)} %bitcast.63), calls=%async_computation.5 | async-start | bytes 2097152 | tf_op jit(solution)/shard_map/all_to_all | solution.py:105
  98.5 2.3 copy.82
  101.5 19.4 %all-to-all-done.5 = bf16[128,16,256]{0,2,1:T(8,128)(2,1)S(1)} async-done(((bf16[128,16,256]{0,2,1:T(8,128)(2,1)}), bf16[128,16,256]{0,2,1:T(8,128)(2,1)S(1)}, u32[]{:S(2)}, u32[]{:S(2)}) %all-to-all-start.5) | async-done | bytes 1048608 | tf_op jit(solution)/shard_map/all_to_all | solution.py:105
  121.0 10.7 %all-to-all-start.4 = ((bf16[128,16,256]{0,2,1:T(8,128)(2,1)}), bf16[128,16,256]{0,2,1:T(8,128)(2,1)}, u32[]{:S(2)}, u32[]{:S(2)}) async-start(bf16[128,16,256]{0,2,1:T(8,128)(2,1)} %bitcast.61), calls=%async_computation.4 | async-start | bytes 2097152 | tf_op jit(solution)/shard_map/all_to_all | solution.py:106
  131.7 4.4 %compare_select_fusion.1 = (s32[2048,1]{0,1:T(1,128)S(1)}, s32[2048,1]{0,1:T(1,128)S(1)}) fusion(s32[]{:T(128)} %bitcast.42, s32[]{:T(128)} %bitcast.43, s32[]{:T(128)} %bitcast.44, s32[]{:T(128)} %bitcast.45, s32[]{:T(128)} %bitcast.46, s32[]{:T(128)} %bitcast.48, s32[]{:T(128)} %bitcast.47, s32[2048,1]{0,1:T(1,128)S(1)} %bitcast.229, ...), kind=kLoop, calls=%fused_computation.77 | loop fusion | flops 28672 | bytes 32796 | tf_op jit(solution)/shard_map/jit(_take)/gather | solution.py:124
  136.3 5.6 %select_select_fusion = s32[2048]{0:T(1024)S(1)} fusion(pred[2048]{0:T(1024)(128)(4,1)S(1)} %get-tuple-element.262, pred[2048]{0:T(1024)(128)(4,1)S(1)} %get-tuple-element.261, pred[2048]{0:T(1024)(128)(4,1)S(1)} %get-tuple-element.260, pred[2048]{0:T(1024)(128)(4,1)S(1)} %get-tuple-element.259, pred[2048]{0:T(1024)(128)(4,1)S(1)} %get-tuple-element.258, ...), kind=kLoop, calls=%fused_computation.85 | loop fusion | flops 36864 | bytes 34852 | tf_op jit(solution)/shard_map/jit(_take)/select_n | solution.py:124
  142.0 1.9 collective-permute-start.1
  144.0 3.7 %collective-permute-start = (bf16[896,1,128]{2,0,1:T(8,128)(2,1)S(1)}, bf16[896,1,128]{2,0,1:T(8,128)(2,1)S(1)}, u32[]{:S(2)}, u32[]{:S(2)}) collective-permute-start(bf16[896,1,128]{2,0,1:T(8,128)(2,1)S(1)} %bitcast.225), channel_id=1, source_target_pairs={{0,16},{16,32},{32,48},{48,64},{64,80},{80,96},{96,112},{112,128},... | collective-permute-start | bytes 688136 | tf_op jit(solution)/shard_map/ppermute | solution.py:16
  154.9 2.6 copy.85
  159.2 2.9 copy.83
  166.4 70.6 %while.17 = (s32[]{:T(128)}, f32[2944,1,128]{2,0,1:T(8,128)}, f32[2944,1,128]{2,0,1:T(8,128)}, bf16[4,512,1,2,128]{1,4,3,2,0:T(8,128)(2,1)}, s32[4]{0:T(128)S(1)...) while((s32[]{:T(128)}, f32[2944,1,128]{2,0,1:T(8,128)}, ...), condition=%wide.region_2.3_spmd, body=%wide.region_1.2_spmd.sunk | while | flops 1858443776 | bytes 44523868 | solution.py:82
  171.6 2.8 fusion.73
  175.5 1.9 fusion.74
  177.4 2.0 fusion.75
  179.4 2.3 fusion.77
  189.2 2.8 fusion.73
  193.1 1.9 fusion.74
  195.0 2.0 fusion.75
  197.0 2.3 fusion.77
  206.9 2.8 fusion.73
  210.8 1.9 fusion.74
  212.7 2.0 fusion.75
  214.7 2.3 fusion.77
  224.5 2.8 fusion.73
  228.4 1.9 fusion.74
  230.3 2.0 fusion.75
  232.3 2.3 fusion.77
  237.0 2.4 copy.88
  241.0 9.6 %all-to-all-start.6 = ((bf16[16,128,256]{2,1,0:T(8,128)(2,1)}), bf16[16,128,256]{2,1,0:T(8,128)(2,1)S(1)}, u32[]{:S(2)}, u32[]{:S(2)}) async-start(bf16[16,128,256]{2,1,0:T(8,128)(2,1)} %convert_element_type.89), calls=%async_computation.6 | async-start | bytes 2097152 | tf_op jit(solution)/shard_map/all_to_all | solution.py:136
  250.6 1.9 collective-permute-start.3
  252.6 5.9 %collective-permute-done.3 = f32[896,1,128]{2,0,1:T(8,128)S(1)} collective-permute-done((f32[896,1,128]{2,0,1:T(8,128)S(1)}, f32[896,1,128]{2,0,1:T(8,128)S(1)}, u32[]{:S(2)}, u32[]{:S(2)}) %collective-permute-start.3) | collective-permute-done | bytes 458784 | tf_op jit(solution)/shard_map/ppermute | solution.py:16
  259.6 2.7 copy.99
  262.3 10.0 %all-to-all-done.6 = bf16[16,128,256]{2,1,0:T(8,128)(2,1)S(1)} async-done(((bf16[16,128,256]{2,1,0:T(8,128)(2,1)}), bf16[16,128,256]{2,1,0:T(8,128)(2,1)S(1)}, u32[]{:S(2)}, u32[]{:S(2)}) %all-to-all-start.6) | async-done | bytes 1048608 | tf_op jit(solution)/shard_map/all_to_all | solution.py:136
  272.3 10.6 %all-to-all-start.8 = ((f32[16,128,128]{1,2,0:T(8,128)}), f32[16,128,128]{1,2,0:T(8,128)}, u32[]{:S(2)}, u32[]{:S(2)}) async-start(f32[16,128,128]{1,2,0:T(8,128)} %copy.99), calls=%async_computation.8 | async-start | bytes 2097152 | tf_op jit(solution)/shard_map/all_to_all | solution.py:151
  283.0 1.9 collective-permute-start.2
  285.0 5.9 %collective-permute-done.2 = f32[896,1,128]{2,0,1:T(8,128)S(1)} collective-permute-done((f32[896,1,128]{2,0,1:T(8,128)S(1)}, f32[896,1,128]{2,0,1:T(8,128)S(1)}, u32[]{:S(2)}, u32[]{:S(2)}) %collective-permute-start.2) | collective-permute-done | bytes 458784 | tf_op jit(solution)/shard_map/ppermute | solution.py:16
  292.4 7.3 %all-to-all-done.8 = f32[16,128,128]{1,2,0:T(8,128)} async-done(((f32[16,128,128]{1,2,0:T(8,128)}), f32[16,128,128]{1,2,0:T(8,128)}, u32[]{:S(2)}, u32[]{:S(2)}) %all-to-all-start.8) | async-done | bytes 1048608 | tf_op jit(solution)/shard_map/all_to_all | solution.py:151
  299.6 14.8 %all-to-all-start.7 = ((f32[16,128,128]{1,2,0:T(8,128)}), f32[16,128,128]{1,2,0:T(8,128)S(1)}, u32[]{:S(2)}, u32[]{:S(2)}) async-start(f32[16,128,128]{1,2,0:T(8,128)} %copy.93), calls=%async_computation.7 | async-start | bytes 2097152 | tf_op jit(solution)/shard_map/all_to_all | solution.py:144
  315.8 2.3 copy.102
  320.1 20.0 %all-to-all-done.7 = f32[16,128,128]{1,2,0:T(8,128)S(1)} async-done(((f32[16,128,128]{1,2,0:T(8,128)}), f32[16,128,128]{1,2,0:T(8,128)S(1)}, u32[]{:S(2)}, u32[]{:S(2)}) %all-to-all-start.7) | async-done | bytes 1048608 | tf_op jit(solution)/shard_map/all_to_all | solution.py:144
  (111 shorter events, 59.7 us)
Async XLA Ops:
  0.6 10.5 %copy-start = (bf16[128,512]{1,0:T(8,128)(2,1)S(1)}, bf16[128,512]{1,0:T(8,128)(2,1)}, u32[]{:S(2)}) copy-start(bf16[128,512]{1,0:T(8,128)(2,1)} %param.16) | copy-start | bytes 393220
  0.6 46.7 %copy-start.3 = (bf16[128,4096]{1,0:T(8,128)(2,1)S(1)}, bf16[128,4096]{1,0:T(8,128)(2,1)}, u32[]{:S(2)}) copy-start(bf16[128,4096]{1,0:T(8,128)(2,1)} %param.11) | copy-start | bytes 3145732
  0.7 20.3 %all-to-all-start.2 = ((bf16[128,16,2]{0,2,1:T(2,128)(2,1)}), bf16[128,16,2]{0,2,1:T(2,128)(2,1)S(1)}, u32[]{:S(2)}, u32[]{:S(2)}) async-start(bf16[128,16,2]{0,2,1:T(2,128)(2,1)} %bitcast.230), calls=%async_computation.2 | async-start | bytes 16384 | tf_op jit(solution)/shard_map/all_to_all | solution.py:109
  21.9 20.0 %all-to-all-start.3 = ((bf16[128,16,128]{2,0,1:T(8,128)(2,1)}), bf16[128,16,128]{2,0,1:T(8,128)(2,1)S(1)}, u32[]{:S(2)}, u32[]{:S(2)}) async-start(bf16[128,16,128]{2,0,1:T(8,128)(2,1)} %bitcast.57), calls=%async_computation.3 | async-start | bytes 1048576 | tf_op jit(solution)/shard_map/all_to_all | solution.py:108
  42.8 19.8 %all-to-all-start.1 = ((bf16[128,16,128]{2,0,1:T(8,128)(2,1)}), bf16[128,16,128]{2,0,1:T(8,128)(2,1)S(1)}, u32[]{:S(2)}, u32[]{:S(2)}) async-start(bf16[128,16,128]{2,0,1:T(8,128)(2,1)} %bitcast.50), calls=%async_computation.1 | async-start | bytes 1048576 | tf_op jit(solution)/shard_map/all_to_all | solution.py:107
  48.6 18.5 %copy-start.4 = (bf16[128,4096]{1,0:T(8,128)(2,1)S(1)}, bf16[128,4096]{1,0:T(8,128)(2,1)}, u32[]{:S(2)}) copy-start(bf16[128,4096]{1,0:T(8,128)(2,1)} %param.12) | copy-start | bytes 3145732
  62.6 32.1 %all-to-all-start = ((bf16[128,16,256]{0,2,1:T(8,128)(2,1)}), bf16[128,16,256]{0,2,1:T(8,128)(2,1)S(1)}, u32[]{:S(2)}, u32[]{:S(2)}) async-start(bf16[128,16,256]{0,2,1:T(8,128)(2,1)} %bitcast.27), calls=%async_computation | async-start | bytes 2097152 | tf_op jit(solution)/shard_map/all_to_all | solution.py:104
  94.7 6.1 %copy-start.5 = (s32[16]{0:T(128)S(1)}, s32[16]{0:T(128)}, u32[]{:S(2)}) copy-start(s32[16]{0:T(128)} %param.17) | copy-start | bytes 196
  94.7 26.2 %all-to-all-start.5 = ((bf16[128,16,256]{0,2,1:T(8,128)(2,1)}), bf16[128,16,256]{0,2,1:T(8,128)(2,1)S(1)}, u32[]{:S(2)}, u32[]{:S(2)}) async-start(bf16[128,16,256]{0,2,1:T(8,128)(2,1)} %bitcast.63), calls=%async_computation.5 | async-start | bytes 2097152 | tf_op jit(solution)/shard_map/all_to_all | solution.py:105
  121.0 38.3 %all-to-all-start.4 = ((bf16[128,16,256]{0,2,1:T(8,128)(2,1)}), bf16[128,16,256]{0,2,1:T(8,128)(2,1)}, u32[]{:S(2)}, u32[]{:S(2)}) async-start(bf16[128,16,256]{0,2,1:T(8,128)(2,1)} %bitcast.61), calls=%async_computation.4 | async-start | bytes 2097152 | tf_op jit(solution)/shard_map/all_to_all | solution.py:106
  142.0 7.3 %collective-permute-start.1 = (bf16[896,1,128]{2,0,1:T(8,128)(2,1)S(1)}, bf16[896,1,128]{2,0,1:T(8,128)(2,1)S(1)}, u32[]{:S(2)}, u32[]{:S(2)}) collective-permute-start(bf16[896,1,128]{2,0,1:T(8,128)(2,1)S(1)} %bitcast.224), channel_id=1, source_target_pairs={{0,16},{16,32},{32,48},{48,64},{64,80},{80,96},{96,112},{112,128},... | collective-permute-start | bytes 688136 | tf_op jit(solution)/shard_map/ppermute | solution.py:16
  144.0 7.8 %collective-permute-start = (bf16[896,1,128]{2,0,1:T(8,128)(2,1)S(1)}, bf16[896,1,128]{2,0,1:T(8,128)(2,1)S(1)}, u32[]{:S(2)}, u32[]{:S(2)}) collective-permute-start(bf16[896,1,128]{2,0,1:T(8,128)(2,1)S(1)} %bitcast.225), channel_id=1, source_target_pairs={{0,16},{16,32},{32,48},{48,64},{64,80},{80,96},{96,112},{112,128},... | collective-permute-start | bytes 688136 | tf_op jit(solution)/shard_map/ppermute | solution.py:16
  239.5 11.1 %copy-start.1 = (f32[2944,1,128]{2,0,1:T(8,128)S(1)}, f32[2944,1,128]{2,0,1:T(8,128)}, u32[]{:S(2)}) copy-start(f32[2944,1,128]{2,0,1:T(8,128)} %get-tuple-element.188) | copy-start | bytes 4521988
  241.0 31.3 %all-to-all-start.6 = ((bf16[16,128,256]{2,1,0:T(8,128)(2,1)}), bf16[16,128,256]{2,1,0:T(8,128)(2,1)S(1)}, u32[]{:S(2)}, u32[]{:S(2)}) async-start(bf16[16,128,256]{2,1,0:T(8,128)(2,1)} %convert_element_type.89), calls=%async_computation.6 | async-start | bytes 2097152 | tf_op jit(solution)/shard_map/all_to_all | solution.py:136
  250.6 7.9 %collective-permute-start.3 = (f32[896,1,128]{2,0,1:T(8,128)S(1)}, f32[896,1,128]{2,0,1:T(8,128)S(1)}, u32[]{:S(2)}, u32[]{:S(2)}) collective-permute-start(f32[896,1,128]{2,0,1:T(8,128)S(1)} %slice.61), channel_id=1, source_target_pairs={{16,0},{32,16},{48,32},{64,48},{80,64},{96,80},{112,96},{128,112},... | collective-permute-start | bytes 1376264 | tf_op jit(solution)/shard_map/ppermute | solution.py:16
  259.6 23.3 %copy-start.2 = (f32[2944,1,128]{2,0,1:T(8,128)S(1)}, f32[2944,1,128]{2,0,1:T(8,128)}, u32[]{:S(2)}) copy-start(f32[2944,1,128]{2,0,1:T(8,128)} %get-tuple-element.187) | copy-start | bytes 4521988
  272.3 27.4 %all-to-all-start.8 = ((f32[16,128,128]{1,2,0:T(8,128)}), f32[16,128,128]{1,2,0:T(8,128)}, u32[]{:S(2)}, u32[]{:S(2)}) async-start(f32[16,128,128]{1,2,0:T(8,128)} %copy.99), calls=%async_computation.8 | async-start | bytes 2097152 | tf_op jit(solution)/shard_map/all_to_all | solution.py:151
  283.0 7.9 %collective-permute-start.2 = (f32[896,1,128]{2,0,1:T(8,128)S(1)}, f32[896,1,128]{2,0,1:T(8,128)S(1)}, u32[]{:S(2)}, u32[]{:S(2)}) collective-permute-start(f32[896,1,128]{2,0,1:T(8,128)S(1)} %slice.58), channel_id=1, source_target_pairs={{16,0},{32,16},{48,32},{64,48},{80,64},{96,80},{112,96},{128,112},... | collective-permute-start | bytes 1376264 | tf_op jit(solution)/shard_map/ppermute | solution.py:16
  299.6 40.5 %all-to-all-start.7 = ((f32[16,128,128]{1,2,0:T(8,128)}), f32[16,128,128]{1,2,0:T(8,128)S(1)}, u32[]{:S(2)}, u32[]{:S(2)}) async-start(f32[16,128,128]{1,2,0:T(8,128)} %copy.93), calls=%async_computation.7 | async-start | bytes 2097152 | tf_op jit(solution)/shard_map/all_to_all | solution.py:144
where the time goes:
time: 343 us; the launch traced here: 341 us
  waiting for transfers between devices  137 us (40%)
  starting transfers between devices  82 us (24%)
  local copies, waits for them, and re-layouts  54.8 us (16%)
  matrix products  40.4 us (12%)
  other arithmetic  22.5 us (7%)
    all_to_all x1, waiting for transfers between devices, per_device(): lax.all_to_all(queries, 'head', split_axis=1, concat_axis=0, tiled=True)  26.3 us
    all_to_all x1, waiting for transfers between devices, per_device(): lax.all_to_all(own_key.reshape(group_rows, kv_local * DH), 'head', split_...  20 us
    all_to_all x1, waiting for transfers between devices, per_device(): lax.all_to_all(outputs, 'head', split_axis=1, concat_axis=0, tiled=True)  19.4 us
    all_to_all x1, waiting for transfers between devices, per_device(): lax.all_to_all(value_wide, 'head', split_axis=1, concat_axis=0, tiled=True)  15.5 us
    ppermute x4, waiting for transfers between devices, from_behind(): return lax.ppermute(value, axis, pairs)  15.1 us
    all_to_all x1, starting transfers between devices, per_device(): lax.all_to_all(own_key.reshape(group_rows, kv_local * DH), 'head', split_...  14.8 us
    all_to_all x1, waiting for transfers between devices, per_device(): lax.all_to_all(key_wide, 'head', split_axis=1, concat_axis=0, tiled=True)  14 us
    dot_general x4, matrix products, core_grads(): jnp.einsum('rhgd,khd->hgrk', query_part, key_part, preferred_element_type...  11.2 us
  transfers between devices with their start and end apart: 13, of which 12 were waited for; matrix products, arithmetic and copies ran while one was open for 11% of the time, Pallas kernels for 0%

commit v1 on v0

v1 whole, which is shorter than its diff:
```python
import jax
import jax.numpy as jnp
from jax import lax
from jax.experimental import pallas as pl
from jax.experimental.pallas import tpu as pltpu
from jax.sharding import PartitionSpec as P

H = 32
KVH = 4
DH = 128
BLOCK = 128
GQ = 8
ROW = 4
WIDE = GQ * DH
SCALE = DH ** (-0.5)
AXES = ("seq", "head")
STAT = 2 * BLOCK
PIECE = STAT + 16
F32 = jnp.float32
BF16 = jnp.bfloat16

VMEM = pl.BlockSpec(memory_space=pltpu.VMEM)
SMEM = pl.BlockSpec(memory_space=pltpu.SMEM)
PARAMS = pltpu.CompilerParams(vmem_limit_bytes=48 << 20)


def nt(left, right):
    return lax.dot_general(left, right, (((1,), (1,)), ((), ())), preferred_element_type=F32)


def nn(left, right):
    return jnp.dot(left, right, preferred_element_type=F32)


def pack_kv(keys, values, *pieces):
    place = lax.rem(lax.axis_index("head"), ROW)
    for shift in range(ROW):
        head = lax.rem(place + shift, ROW)
        columns = pl.ds(pl.multiple_of(head * DH, DH), DH)
        pieces[shift][:, :DH] = keys[:, columns]
        pieces[shift][:, DH:] = values[:, columns]


def pack_queries(queries, outputs, grads, norms, *pieces):
    place = lax.rem(lax.axis_index("head"), ROW)
    rows = lax.broadcasted_iota(jnp.int32, (H, H), 0)
    columns = lax.broadcasted_iota(jnp.int32, (H, H), 1)
    unit = (rows == columns).astype(BF16)
    turned = nt(unit, norms[...])
    ones = jnp.ones((16, DH), BF16)
    row_id = lax.broadcasted_iota(jnp.int32, (16, BLOCK), 0)
    head_id = lax.broadcasted_iota(jnp.int32, (H, BLOCK), 0)
    for shift in range(ROW):
        group = lax.rem(place + shift, ROW)
        span = pl.ds(pl.multiple_of(group * WIDE, WIDE), WIDE)
        pieces[shift][:BLOCK, :] = queries[:, span]
        pieces[shift][BLOCK:STAT, :] = grads[:, span]
        for head in range(GQ):
            cut = pl.ds(pl.multiple_of(group * WIDE + head * DH, DH), DH)
            product = grads[:, cut].astype(F32) * outputs[:, cut].astype(F32)
            high = product.astype(BF16)
            low = (product - high.astype(F32)).astype(BF16)
            dots = nt(ones, high) + nt(ones, low)
            first = dots.astype(BF16).astype(F32)
            second = (dots - first).astype(BF16).astype(F32)
            third = dots - first - second
            norm = jnp.sum(
                jnp.where(head_id == group * GQ + head, turned, 0.0), axis=0, keepdims=True
            )
            stats = jnp.where(
                row_id == 0,
                norm,
                jnp.where(row_id == 1, first, jnp.where(row_id == 2, second, third)),
            )
            pieces[shift][STAT:, head * DH : (head + 1) * DH] = stats.astype(BF16)


def stacked(piece, start):
    return jnp.concatenate(
        [piece[start : start + BLOCK, head * DH : (head + 1) * DH] for head in range(GQ)], axis=0
    )


def sweep(back, doc_start, pieces, kv, dq, dkv):
    head = lax.axis_index("head")
    place = lax.rem(head, ROW)
    own_row = head // ROW
    first_key = lax.axis_index("seq") * (ROW * ROW) + (own_row - back) * ROW
    dkv[...] = jnp.zeros_like(dkv)
    for slot in range(ROW):
        query_place = lax.rem(place + ROW - slot, ROW)
        start = doc_start[own_row * ROW + query_place]

        def turn(key_slot, carry):
            key_place = lax.rem(place + ROW - key_slot, ROW)
            seen = first_key + key_place >= start
            if back == 0:
                seen = seen & (key_place <= query_place)

            @pl.when(seen)
            def _():
                piece = pieces[slot]
                key = kv[key_slot, :, :DH]
                value = kv[key_slot, :, DH:]
                query = stacked(piece, 0)
                grad = stacked(piece, BLOCK)
                stats = piece[STAT:, :].astype(F32)
                norm = stats[0:1]
                dots = stats[1:2] + stats[2:3] + stats[3:4]
                weights = jnp.exp(nt(key, query) * SCALE - norm)
                if back == 0:
                    key_pos = lax.broadcasted_iota(jnp.int32, (BLOCK, WIDE), 0)
                    query_pos = lax.broadcasted_iota(jnp.int32, (BLOCK, WIDE), 1) % BLOCK
                    ahead = (query_place - key_place) * BLOCK
                    weights = jnp.where(key_pos <= query_pos + ahead, weights, 0.0)
                grad_scores = (weights * (nt(value, grad) - dots)).astype(BF16)
                dkv[key_slot, :, DH:] += nn(weights.astype(BF16), grad)
                dkv[key_slot, :, :DH] += nn(grad_scores, query)
                dq[slot] += nn(key.T, grad_scores)

            return carry

        lax.fori_loop(0, ROW, turn, 0)


def row_two(doc_start, piece0, piece1, piece2, piece3, kv, dkv_out, dq, dkv):
    dq[...] = jnp.zeros_like(dq)
    sweep(2, doc_start, (piece0, piece1, piece2, piece3), kv, dq, dkv)
    dkv_out[:, :, :DH] = (dkv[:, :, :DH] * SCALE).astype(BF16)
    dkv_out[:, :, DH:] = dkv[:, :, DH:].astype(BF16)


def row_one(doc_start, piece0, piece1, piece2, piece3, kv, dq_in, dkv_out, dq, dkv):
    dq[...] = dq_in[...]
    sweep(1, doc_start, (piece0, piece1, piece2, piece3), kv, dq, dkv)
    dkv_out[:, :, :DH] = (dkv[:, :, :DH] * SCALE).astype(BF16)
    dkv_out[:, :, DH:] = dkv[:, :, DH:].astype(BF16)


def row_own(doc_start, piece0, piece1, piece2, piece3, kv, dq_in, dkv, *rest):
    outs, dq = rest[:ROW], rest[ROW]
    dq[...] = dq_in[...]
    sweep(0, doc_start, (piece0, piece1, piece2, piece3), kv, dq, dkv)
    dkv[:, :, :DH] = dkv[:, :, :DH] * SCALE
    for slot in range(ROW):
        for head in range(GQ):
            cut = slice(head * DH, (head + 1) * DH)
            outs[slot][:, cut] = (dq[slot, :, cut].T * SCALE).astype(BF16)


def add_up(own, one, two, *pieces):
    for slot in range(ROW):
        pieces[slot][...] = (
            own[slot] + one[slot].astype(F32) + two[slot].astype(F32)
        ).astype(BF16)


def join_queries(piece0, piece1, piece2, piece3, out):
    place = lax.rem(lax.axis_index("head"), ROW)
    for shift, piece in enumerate((piece0, piece1, piece2, piece3)):
        group = lax.rem(place + shift, ROW)
        out[:, pl.ds(pl.multiple_of(group * WIDE, WIDE), WIDE)] = piece[...]


def join_kv(piece0, piece1, piece2, piece3, key_out, value_out):
    place = lax.rem(lax.axis_index("head"), ROW)
    for shift, piece in enumerate((piece0, piece1, piece2, piece3)):
        columns = pl.ds(pl.multiple_of(lax.rem(place + shift, ROW) * DH, DH), DH)
        key_out[:, columns] = piece[:, :DH]
        value_out[:, columns] = piece[:, DH:]


def kernel(body, name, in_specs, shapes, scratch=(), flops=0, size=0):
    return pl.pallas_call(
        body,
        in_specs=in_specs,
        out_specs=[VMEM] * len(shapes),
        out_shape=[jax.ShapeDtypeStruct(*shape) for shape in shapes],
        scratch_shapes=scratch,
        compiler_params=PARAMS,
        cost_estimate=pl.CostEstimate(flops=flops, bytes_accessed=size, transcendentals=0),
        name=name,
    )


def per_device(queries, outputs, out_grads, log_norms, keys, values, doc_start):
    seqs = lax.axis_size("seq")
    heads = lax.axis_size("head")
    total = seqs * heads

    def along_row(value, shift):
        if shift % ROW == 0:
            return value
        pairs = [(b, b - b % ROW + (b + shift) % ROW) for b in range(total)]
        return lax.ppermute(value, AXES, pairs)

    def along_rows(value, rows):
        by = rows * ROW
        return lax.ppermute(
            value, AXES, [(b, b + by) for b in range(total) if 0 <= b + by < total]
        )

    kv_sent = kernel(
        pack_kv, "pack_kv", [VMEM] * 2, [((BLOCK, 2 * DH), BF16)] * ROW, size=1 << 19
    )(keys, values)
    kv_own = jnp.stack([along_row(kv_sent[shift], shift) for shift in range(ROW)])
    kv_two = along_rows(kv_own, 2)
    kv_one = along_rows(kv_own, 1)
    sent = kernel(
        pack_queries, "pack_queries", [VMEM] * 4, [((PIECE, WIDE), BF16)] * ROW, size=5 << 20
    )(queries, outputs, out_grads, log_norms)
    pieces = [along_row(sent[shift], shift) for shift in range(ROW)]

    dq_shape = ((ROW, DH, WIDE), F32)
    kv_shape = (ROW, BLOCK, 2 * DH)
    scratch = [pltpu.VMEM(kv_shape, F32)]
    dkv_two, dq = kernel(
        row_two,
        "row_two",
        [SMEM] + [VMEM] * 5,
        [(kv_shape, BF16), dq_shape],
        scratch,
        flops=6 * 1 << 30,
    )(doc_start, *pieces, kv_two)
    back_two = along_rows(dkv_two, -2)
    dkv_one, dq = kernel(
        row_one,
        "row_one",
        [SMEM] + [VMEM] * 6,
        [(kv_shape, BF16), dq_shape],
        scratch,
        flops=16 * 1 << 30,
    )(doc_start, *pieces, kv_one, dq)
    back_one = along_rows(dkv_one, -1)
    dkv_own, *dq_sent = kernel(
        row_own,
        "row_own",
        [SMEM] + [VMEM] * 6,
        [(kv_shape, F32)] + [((BLOCK, WIDE), BF16)] * ROW,
        [pltpu.VMEM(*dq_shape)],
        flops=10 * 1 << 30,
    )(doc_start, *pieces, kv_own, dq)
    dq_pieces = [along_row(dq_sent[slot], -slot) for slot in range(ROW)]
    dkv_sent = kernel(
        add_up, "add_up", [VMEM] * 3, [((BLOCK, 2 * DH), BF16)] * ROW, size=1 << 20
    )(dkv_own, back_one, back_two)
    dkv_pieces = [along_row(dkv_sent[slot], -slot) for slot in range(ROW)]
    (query_out,) = kernel(
        join_queries, "join_queries", [VMEM] * ROW, [((BLOCK, H * DH), BF16)], size=2 << 20
    )(*dq_pieces)
    key_out, value_out = kernel(
        join_kv, "join_kv", [VMEM] * ROW, [((BLOCK, KVH * DH), BF16)] * 2, size=1 << 19
    )(*dkv_pieces)
    return (query_out, key_out, value_out)


def solution(mesh):
    placed = P(("seq", "head"), None)
    return jax.shard_map(
        per_device,
        mesh=mesh,
        in_specs=(placed,) * 6 + (P("seq"),),
        out_specs=(placed,) * 3,
        check_vma=False,
    )
```

time: 343 us -> 116 us (0.34)
  waiting for transfers between devices: 137 us -> 48.5 us
  local copies, waits for them, and re-layouts: 54.8 us -> 5.83 us
  matrix products: 40.4 us -> 0 us
  starting transfers between devices: 82 us -> 41.8 us
  other arithmetic: 22.5 us -> 0.04 us
  Pallas kernels: 0 us -> 17.6 us
    all_to_all x9 -> x0, waiting for transfers between devices: 122 us -> none  [the longest x1 26.3 us: per_device(): lax.all_to_all(queries, 'head', split_axis=1, concat_axis=0, tiled=True)]
    all_to_all x9 -> x0, starting transfers between devices: 72.6 us -> none  [the longest x1 14.8 us: per_device(): lax.all_to_all(own_key.reshape(group_rows, kv_local * DH), 'head', split_...]
    dot_general x20 -> x0, matrix products: 40.4 us -> none  [the longest x4 11.2 us: core_grads(): jnp.einsum('rhgd,khd->hgrk', query_part, key_part, preferred_element_type...]
    ppermute x4 -> x16, waiting for transfers between devices: 15.1 us -> 48.5 us  [the longest x12 31.7 us: along_row(): return lax.ppermute(value, AXES, pairs)]
    ppermute x4 -> x16, starting transfers between devices: 9.44 us -> 41.8 us  [the longest x4 22.8 us: along_rows(): lax.ppermute(value, AXES, [(b, b + by) for b in range(total) if 0 <= b +...]
    pallas_call x0 -> x8, Pallas kernels: none -> 17.6 us  [the longest x1 6.18 us: per_device(): kernel(row_one, 'row_one', [SMEM] + [VMEM] * 6, [(kv_shape, BF16), dq_sha...]
    dynamic_slice x20 -> x0, local copies, waits for them, and re-layouts: 10.7 us -> none  [the longest x16 8.13 us: window(): return lax.dynamic_slice_in_dim(array, start, length, 0)]
    dynamic_update_slice x16 -> x0, local copies, waits for them, and re-layouts: 9.38 us -> none  [the longest x8 4.71 us: turn(): lax.dynamic_update_slice_in_dim(value_acc, window(value_acc, span) + valu...]
  transfers between devices with their start and end apart: 13 -> 16, of which waited for: 12 -> 10; matrix products, arithmetic and copies ran while one was open for 11% -> 0% of each run, Pallas kernels for 0% -> 8%
where the time goes in v1:
time: 116 us; the launch traced here: 115 us
  waiting for transfers between devices  48.5 us (42%)
  starting transfers between devices  41.8 us (36%)
  Pallas kernels  17.6 us (15%)
  local copies, waits for them, and re-layouts  5.83 us (5%)
    ppermute x12, waiting for transfers between devices, along_row(): return lax.ppermute(value, AXES, pairs)  31.7 us
    ppermute x4, starting transfers between devices, along_rows(): lax.ppermute(value, AXES, [(b, b + by) for b in range(total) if 0 <= b +...  22.8 us
    ppermute x12, starting transfers between devices, along_row(): return lax.ppermute(value, AXES, pairs)  19 us
    ppermute x4, waiting for transfers between devices, along_rows(): lax.ppermute(value, AXES, [(b, b + by) for b in range(total) if 0 <= b +...  16.8 us
    pallas_call x1, Pallas kernels, per_device(): kernel(row_one, 'row_one', [SMEM] + [VMEM] * 6, [(kv_shape, BF16), dq_sha...  6.18 us
    unnamed x15, local copies, waits for them, and re-layouts  5.83 us
    pallas_call x1, Pallas kernels, per_device(): kernel(row_own, 'row_own', [SMEM] + [VMEM] * 6, [(kv_shape, F32)] + [((BL...  5.14 us
    pallas_call x1, Pallas kernels, per_device(): kernel(row_two, 'row_two', [SMEM] + [VMEM] * 5, [(kv_shape, BF16), dq_sha...  3.07 us
  transfers between devices with their start and end apart: 16, of which 10 were waited for; matrix products, arithmetic and copies ran while one was open for 0% of the time, Pallas kernels for 8%

profile of v1, /device:TPU:34, one launch (start us, length us, event | category | flops | bytes accessed | tf_op | source)
XLA Modules:
  0.0 114.5 jit_solution(7398581781647566629)
XLA Ops:
  0.6 0.0 copy-start.5
  0.6 0.8 copy.10.norms
  1.5 1.2 %copy-done = bf16[128,4096]{1,0:T(8,128)(2,1)S(1)} copy-done((bf16[128,4096]{1,0:T(8,128)(2,1)S(1)}, bf16[128,4096]{1,0:T(8,128)(2,1)}, u32[]{:S(2)}) %copy-start) | copy-done | bytes 1048600
  2.7 1.2 %copy-done.1 = bf16[128,4096]{1,0:T(8,128)(2,1)S(1)} copy-done((bf16[128,4096]{1,0:T(8,128)(2,1)S(1)}, bf16[128,4096]{1,0:T(8,128)(2,1)}, u32[]{:S(2)}) %copy-start.1) | copy-done | bytes 1048600
  3.9 1.2 %copy-done.2 = bf16[128,4096]{1,0:T(8,128)(2,1)S(1)} copy-done((bf16[128,4096]{1,0:T(8,128)(2,1)S(1)}, bf16[128,4096]{1,0:T(8,128)(2,1)}, u32[]{:S(2)}) %copy-start.2) | copy-done | bytes 1048600
  5.1 1.3 %pack_queries.1 = (bf16[272,1024]{1,0:T(8,128)(2,1)S(1)}, bf16[272,1024]{1,0:T(8,128)(2,1)S(1)}, bf16[272,1024]{1,0:T(8,128)(2,1)S(1)}, bf16[272,1024]{1,0:T(8,128)(2,1)S(1)}) custom-call(bf16[128,4096]{1,0:T(8,128)(2,1)S(1)} %copy-done, bf16[128,4096]{1,0:T(8,128)(2,1)S(1)} %copy-done.1, bf16[128,4096]{1,0:T(8,128)(2,1)S(1)} %copy-done.2, ...), custom_call_target="tpu_custom_call" | custom-call | bytes 5242880 | tf_op jit(solution)/shard_map/pack_queries/pallas_call | solution.py:209
  6.5 1.7 %collective-permute-start = (bf16[272,1024]{1,0:T(8,128)(2,1)S(1)}, bf16[272,1024]{1,0:T(8,128)(2,1)S(1)}, u32[]{:S(2)}, u32[]{:S(2)}) collective-permute-start(bf16[272,1024]{1,0:T(8,128)(2,1)S(1)} %get-tuple-element.27), channel_id=1, source_target_pairs={{0,1},{1,2},{2,3},{3,0},{4,5},{5,6},{6,7},{7,4},{8,9},{9,10},{10,1... | collective-permute-start | bytes 1671176 | tf_op jit(solution)/shard_map/ppermute | solution.py:195
  8.1 2.9 %collective-permute-start.1 = (bf16[272,1024]{1,0:T(8,128)(2,1)S(1)}, bf16[272,1024]{1,0:T(8,128)(2,1)S(1)}, u32[]{:S(2)}, u32[]{:S(2)}) collective-permute-start(bf16[272,1024]{1,0:T(8,128)(2,1)S(1)} %get-tuple-element.28), channel_id=1, source_target_pairs={{0,2},{1,3},{2,0},{3,1},{4,6},{5,7},{6,4},{7,5},{8,10},{9,11},{10,... | collective-permute-start | bytes 1671176 | tf_op jit(solution)/shard_map/ppermute | solution.py:195
  11.0 1.3 %collective-permute-start.2 = (bf16[272,1024]{1,0:T(8,128)(2,1)S(1)}, bf16[272,1024]{1,0:T(8,128)(2,1)S(1)}, u32[]{:S(2)}, u32[]{:S(2)}) collective-permute-start(bf16[272,1024]{1,0:T(8,128)(2,1)S(1)} %get-tuple-element.29), channel_id=1, source_target_pairs={{0,3},{1,0},{2,1},{3,2},{4,7},{5,4},{6,5},{7,6},{8,11},{9,8},{10,9... | collective-permute-start | bytes 1671176 | tf_op jit(solution)/shard_map/ppermute | solution.py:195
  12.4 0.0 copy-done.3
  12.4 0.0 copy-done.4
  12.4 0.8 collective-permute-start.3
  13.2 0.8 collective-permute-start.4
  14.0 20.6 %collective-permute-done.3 = bf16[128,256]{1,0:T(8,128)(2,1)S(1)} collective-permute-done((bf16[128,256]{1,0:T(8,128)(2,1)S(1)}, bf16[128,256]{1,0:T(8,128)(2,1)S(1)}, u32[]{:S(2)}, u32[]{:S(2)}) %collective-permute-start.3) | collective-permute-done | bytes 65568 | tf_op jit(solution)/shard_map/ppermute | solution.py:195
  34.5 3.5 %collective-permute-start.5 = (bf16[128,256]{1,0:T(8,128)(2,1)S(1)}, bf16[128,256]{1,0:T(8,128)(2,1)S(1)}, u32[]{:S(2)}, u32[]{:S(2)}) collective-permute-start(bf16[128,256]{1,0:T(8,128)(2,1)S(1)} %get-tuple-element.33), channel_id=1, source_target_pairs={{0,3},{1,0},{2,1},{3,2},{4,7},{5,4},{6,5},{7,6},{8,11},{9,8},{10,9... | collective-permute-start | bytes 196616 | tf_op jit(solution)/shard_map/ppermute | solution.py:195
  38.0 0.1 collective-permute-done.4
  38.1 1.8 %collective-permute-done.5 = bf16[128,256]{1,0:T(8,128)(2,1)S(1)} collective-permute-done((bf16[128,256]{1,0:T(8,128)(2,1)S(1)}, bf16[128,256]{1,0:T(8,128)(2,1)S(1)}, u32[]{:S(2)}, u32[]{:S(2)}) %collective-permute-start.5) | collective-permute-done | bytes 65568 | tf_op jit(solution)/shard_map/ppermute | solution.py:195
  39.9 8.2 %collective-permute-start.7 = (bf16[4,128,256]{2,1,0:T(8,128)(2,1)S(1)}, bf16[4,128,256]{2,1,0:T(8,128)(2,1)S(1)}, u32[]{:S(2)}, u32[]{:S(2)}) collective-permute-start(bf16[4,128,256]{2,1,0:T(8,128)(2,1)S(1)} %pad_maximum_fusion.kv), channel_id=1, source_target_pairs={{0,8},{1,9},{2,10},{3,11},{4,12},{5,13},{6,14},{7,15},{8,16},{9,17... | collective-permute-start | bytes 786440 | tf_op jit(solution)/shard_map/ppermute | solution.py:199
  48.1 3.4 %collective-permute-start.6 = (bf16[4,128,256]{2,1,0:T(8,128)(2,1)S(1)}, bf16[4,128,256]{2,1,0:T(8,128)(2,1)S(1)}, u32[]{:S(2)}, u32[]{:S(2)}) collective-permute-start(bf16[4,128,256]{2,1,0:T(8,128)(2,1)S(1)} %pad_maximum_fusion.kv), channel_id=1, source_target_pairs={{0,4},{1,5},{2,6},{3,7},{4,8},{5,9},{6,10},{7,11},{8,12},{9,13},{1... | collective-permute-start | bytes 786440 | tf_op jit(solution)/shard_map/ppermute | solution.py:199
  51.5 9.3 %collective-permute-done.7.kv = bf16[4,128,256]{2,1,0:T(8,128)(2,1)S(1)} collective-permute-done((bf16[4,128,256]{2,1,0:T(8,128)(2,1)S(1)}, bf16[4,128,256]{2,1,0:T(8,128)(2,1)S(1)}, u32[]{:S(2)}, u32[]{:S(2)}) %collective-permute-start.7) | collective-permute-done | bytes 262176 | tf_op jit(solution)/shard_map/ppermute | solution.py:199
  60.9 0.0 collective-permute-done.piece1
  60.9 0.0 collective-permute-done.1.piece2
  60.9 0.0 collective-permute-done.2.piece3
  60.9 0.0 copy-done.5
  60.9 3.1 %row_two.1 = (bf16[4,128,256]{2,1,0:T(8,128)(2,1)S(1)}, f32[4,128,1024]{2,1,0:T(8,128)S(1)}) custom-call(s32[16]{0:T(128)S(1)} %copy-done.5, bf16[272,1024]{1,0:T(8,128)(2,1)S(1)} %get-tuple-element.26.piece0, bf16[272,1024]{1,0:T(8,128)(2,1)S(1)} %collective-permute-done.piece1, bf16[272,1024]{1,0:T(8,128)(2,1)S(1)} %collective-permute-done.1.piece2, ...), custom_call_target="tpu_custom_call" | custom-call | flops 6442450944 | tf_op jit(solution)/shard_map/row_two/pallas_call | solution.py:217
  64.0 1.3 %copy-done.6 = f32[4,128,1024]{2,1,0:T(8,128)} copy-done((f32[4,128,1024]{2,1,0:T(8,128)}, f32[4,128,1024]{2,1,0:T(8,128)S(1)}, u32[]{:S(2)}) %copy-start.6) | copy-done | bytes 2097176
  65.3 6.4 %collective-permute-done.6.kv = bf16[4,128,256]{2,1,0:T(8,128)(2,1)S(1)} collective-permute-done((bf16[4,128,256]{2,1,0:T(8,128)(2,1)S(1)}, bf16[4,128,256]{2,1,0:T(8,128)(2,1)S(1)}, u32[]{:S(2)}, u32[]{:S(2)}) %collective-permute-start.6) | collective-permute-done | bytes 262176 | tf_op jit(solution)/shard_map/ppermute | solution.py:199
  71.6 6.2 %row_one.1 = (bf16[4,128,256]{2,1,0:T(8,128)(2,1)S(1)}, f32[4,128,1024]{2,1,0:T(8,128)S(1)}) custom-call(s32[16]{0:T(128)S(1)} %copy-done.5, bf16[272,1024]{1,0:T(8,128)(2,1)S(1)} %get-tuple-element.26.piece0, bf16[272,1024]{1,0:T(8,128)(2,1)S(1)} %collective-permute-done.piece1, bf16[272,1024]{1,0:T(8,128)(2,1)S(1)} %collective-permute-done.1.piece2, ...), custom_call_target="tpu_custom_call" | custom-call | flops 17179869184 | tf_op jit(solution)/shard_map/row_one/pallas_call | solution.py:226
  77.8 2.2 %collective-permute-start.11 = (bf16[4,128,256]{2,1,0:T(8,128)(2,1)S(1)}, bf16[4,128,256]{2,1,0:T(8,128)(2,1)S(1)}, u32[]{:S(2)}, u32[]{:S(2)}) collective-permute-start(bf16[4,128,256]{2,1,0:T(8,128)(2,1)S(1)} %get-tuple-element.41), channel_id=1, source_target_pairs={{4,0},{5,1},{6,2},{7,3},{8,4},{9,5},{10,6},{11,7},{12,8},{13,9},{1... | collective-permute-start | bytes 786440 | tf_op jit(solution)/shard_map/ppermute | solution.py:199
  80.0 9.1 %collective-permute-start.12 = (bf16[4,128,256]{2,1,0:T(8,128)(2,1)S(1)}, bf16[4,128,256]{2,1,0:T(8,128)(2,1)S(1)}, u32[]{:S(2)}, u32[]{:S(2)}) collective-permute-start(bf16[4,128,256]{2,1,0:T(8,128)(2,1)S(1)} %get-tuple-element.42), channel_id=1, source_target_pairs={{8,0},{9,1},{10,2},{11,3},{12,4},{13,5},{14,6},{15,7},{16,8},{17,9... | collective-permute-start | bytes 786440 | tf_op jit(solution)/shard_map/ppermute | solution.py:199
  89.1 5.1 %row_own.1 = (f32[4,128,256]{2,1,0:T(8,128)S(1)}, bf16[128,1024]{1,0:T(8,128)(2,1)S(1)}, bf16[128,1024]{1,0:T(8,128)(2,1)S(1)}, bf16[128,1024]{1,0:T(8,128)(2,1)S(1)}, bf16[128,1024]{1,0:T(8,128)(2,1)S(1)}) custom-call(s32[16]{0:T(128)S(1)} %copy-done.5, bf16[272,1024]{1,0:T(8,128)(2,1)S(1)} %get-tuple-element.26.piece0, ...), custom_call_target="tpu_custom_call" | custom-call | flops 10737418240 | tf_op jit(solution)/shard_map/row_own/pallas_call | solution.py:235
  94.2 3.3 %collective-permute-start.8 = (bf16[128,1024]{1,0:T(8,128)(2,1)S(1)}, bf16[128,1024]{1,0:T(8,128)(2,1)S(1)}, u32[]{:S(2)}, u32[]{:S(2)}) collective-permute-start(bf16[128,1024]{1,0:T(8,128)(2,1)S(1)} %get-tuple-element.37), channel_id=1, source_target_pairs={{0,3},{1,0},{2,1},{3,2},{4,7},{5,4},{6,5},{7,6},{8,11},{9,8},{10,9... | collective-permute-start | bytes 786440 | tf_op jit(solution)/shard_map/ppermute | solution.py:195
  97.5 0.0 collective-permute-start.9
  97.5 1.0 collective-permute-start.10
  98.5 0.0 collective-permute-done.11.one
  98.5 1.1 collective-permute-done.12.two
  99.6 0.1 add_up.1
  99.7 3.8 %collective-permute-start.13 = (bf16[128,256]{1,0:T(8,128)(2,1)S(1)}, bf16[128,256]{1,0:T(8,128)(2,1)S(1)}, u32[]{:S(2)}, u32[]{:S(2)}) collective-permute-start(bf16[128,256]{1,0:T(8,128)(2,1)S(1)} %get-tuple-element.44), channel_id=1, source_target_pairs={{0,3},{1,0},{2,1},{3,2},{4,7},{5,4},{6,5},{7,6},{8,11},{9,8},{10,9... | collective-permute-start | bytes 196616 | tf_op jit(solution)/shard_map/ppermute | solution.py:195
  103.5 0.0 collective-permute-start.14
  103.5 4.4 %collective-permute-done.8.piece1 = bf16[128,1024]{1,0:T(8,128)(2,1)S(1)} collective-permute-done((bf16[128,1024]{1,0:T(8,128)(2,1)S(1)}, bf16[128,1024]{1,0:T(8,128)(2,1)S(1)}, u32[]{:S(2)}, u32[]{:S(2)}) %collective-permute-start.8) | collective-permute-done | bytes 262176 | tf_op jit(solution)/shard_map/ppermute | solution.py:195
  107.9 0.0 collective-permute-start.15
  107.9 0.1 collective-permute-done.9.piece2
  108.0 2.6 %collective-permute-done.10.piece3 = bf16[128,1024]{1,0:T(8,128)(2,1)S(1)} collective-permute-done((bf16[128,1024]{1,0:T(8,128)(2,1)S(1)}, bf16[128,1024]{1,0:T(8,128)(2,1)S(1)}, u32[]{:S(2)}, u32[]{:S(2)}) %collective-permute-start.10) | collective-permute-done | bytes 262176 | tf_op jit(solution)/shard_map/ppermute | solution.py:195
  110.5 1.1 join_queries.1
  111.6 0.0 collective-permute-done.13.piece1
  111.6 0.0 collective-permute-done.14.piece2
  111.6 2.1 %collective-permute-done.15.piece3 = bf16[128,256]{1,0:T(8,128)(2,1)S(1)} collective-permute-done((bf16[128,256]{1,0:T(8,128)(2,1)S(1)}, bf16[128,256]{1,0:T(8,128)(2,1)S(1)}, u32[]{:S(2)}, u32[]{:S(2)}) %collective-permute-start.15) | collective-permute-done | bytes 65568 | tf_op jit(solution)/shard_map/ppermute | solution.py:195
  113.8 0.7 join_kv.1
  (8 shorter events, 0.1 us)
Async XLA Ops:
  0.6 60.2 %copy-start.5 = (s32[16]{0:T(128)S(1)}, s32[16]{0:T(128)}, u32[]{:S(2)}) copy-start(s32[16]{0:T(128)} %doc_start.5) | copy-start | bytes 196
  1.5 1.2 %copy-start = (bf16[128,4096]{1,0:T(8,128)(2,1)S(1)}, bf16[128,4096]{1,0:T(8,128)(2,1)}, u32[]{:S(2)}) copy-start(bf16[128,4096]{1,0:T(8,128)(2,1)} %queries.1) | copy-start | bytes 3145732
  2.7 1.2 %copy-start.1 = (bf16[128,4096]{1,0:T(8,128)(2,1)S(1)}, bf16[128,4096]{1,0:T(8,128)(2,1)}, u32[]{:S(2)}) copy-start(bf16[128,4096]{1,0:T(8,128)(2,1)} %outputs.1) | copy-start | bytes 3145732
  3.9 1.2 %copy-start.2 = (bf16[128,4096]{1,0:T(8,128)(2,1)S(1)}, bf16[128,4096]{1,0:T(8,128)(2,1)}, u32[]{:S(2)}) copy-start(bf16[128,4096]{1,0:T(8,128)(2,1)} %grads.1) | copy-start | bytes 3145732
  5.1 7.2 %copy-start.3 = (bf16[128,512]{1,0:T(8,128)(2,1)S(1)}, bf16[128,512]{1,0:T(8,128)(2,1)}, u32[]{:S(2)}) copy-start(bf16[128,512]{1,0:T(8,128)(2,1)} %keys.1) | copy-start | bytes 393220
  5.1 7.2 %copy-start.4 = (bf16[128,512]{1,0:T(8,128)(2,1)S(1)}, bf16[128,512]{1,0:T(8,128)(2,1)}, u32[]{:S(2)}) copy-start(bf16[128,512]{1,0:T(8,128)(2,1)} %values.1) | copy-start | bytes 393220
  6.5 54.4 %collective-permute-start = (bf16[272,1024]{1,0:T(8,128)(2,1)S(1)}, bf16[272,1024]{1,0:T(8,128)(2,1)S(1)}, u32[]{:S(2)}, u32[]{:S(2)}) collective-permute-start(bf16[272,1024]{1,0:T(8,128)(2,1)S(1)} %get-tuple-element.27), channel_id=1, source_target_pairs={{0,1},{1,2},{2,3},{3,0},{4,5},{5,6},{6,7},{7,4},{8,9},{9,10},{10,1... | collective-permute-start | bytes 1671176 | tf_op jit(solution)/shard_map/ppermute | solution.py:195
  8.1 52.8 %collective-permute-start.1 = (bf16[272,1024]{1,0:T(8,128)(2,1)S(1)}, bf16[272,1024]{1,0:T(8,128)(2,1)S(1)}, u32[]{:S(2)}, u32[]{:S(2)}) collective-permute-start(bf16[272,1024]{1,0:T(8,128)(2,1)S(1)} %get-tuple-element.28), channel_id=1, source_target_pairs={{0,2},{1,3},{2,0},{3,1},{4,6},{5,7},{6,4},{7,5},{8,10},{9,11},{10,... | collective-permute-start | bytes 1671176 | tf_op jit(solution)/shard_map/ppermute | solution.py:195
  11.0 49.9 %collective-permute-start.2 = (bf16[272,1024]{1,0:T(8,128)(2,1)S(1)}, bf16[272,1024]{1,0:T(8,128)(2,1)S(1)}, u32[]{:S(2)}, u32[]{:S(2)}) collective-permute-start(bf16[272,1024]{1,0:T(8,128)(2,1)S(1)} %get-tuple-element.29), channel_id=1, source_target_pairs={{0,3},{1,0},{2,1},{3,2},{4,7},{5,4},{6,5},{7,6},{8,11},{9,8},{10,9... | collective-permute-start | bytes 1671176 | tf_op jit(solution)/shard_map/ppermute | solution.py:195
  12.4 22.1 %collective-permute-start.3 = (bf16[128,256]{1,0:T(8,128)(2,1)S(1)}, bf16[128,256]{1,0:T(8,128)(2,1)S(1)}, u32[]{:S(2)}, u32[]{:S(2)}) collective-permute-start(bf16[128,256]{1,0:T(8,128)(2,1)S(1)} %get-tuple-element.31), channel_id=1, source_target_pairs={{0,1},{1,2},{2,3},{3,0},{4,5},{5,6},{6,7},{7,4},{8,9},{9,10},{10,1... | collective-permute-start | bytes 196616 | tf_op jit(solution)/shard_map/ppermute | solution.py:195
  13.2 25.0 %collective-permute-start.4 = (bf16[128,256]{1,0:T(8,128)(2,1)S(1)}, bf16[128,256]{1,0:T(8,128)(2,1)S(1)}, u32[]{:S(2)}, u32[]{:S(2)}) collective-permute-start(bf16[128,256]{1,0:T(8,128)(2,1)S(1)} %get-tuple-element.32), channel_id=1, source_target_pairs={{0,2},{1,3},{2,0},{3,1},{4,6},{5,7},{6,4},{7,5},{8,10},{9,11},{10,... | collective-permute-start | bytes 196616 | tf_op jit(solution)/shard_map/ppermute | solution.py:195
  34.5 5.4 %collective-permute-start.5 = (bf16[128,256]{1,0:T(8,128)(2,1)S(1)}, bf16[128,256]{1,0:T(8,128)(2,1)S(1)}, u32[]{:S(2)}, u32[]{:S(2)}) collective-permute-start(bf16[128,256]{1,0:T(8,128)(2,1)S(1)} %get-tuple-element.33), channel_id=1, source_target_pairs={{0,3},{1,0},{2,1},{3,2},{4,7},{5,4},{6,5},{7,6},{8,11},{9,8},{10,9... | collective-permute-start | bytes 196616 | tf_op jit(solution)/shard_map/ppermute | solution.py:195
  39.9 20.9 %collective-permute-start.7 = (bf16[4,128,256]{2,1,0:T(8,128)(2,1)S(1)}, bf16[4,128,256]{2,1,0:T(8,128)(2,1)S(1)}, u32[]{:S(2)}, u32[]{:S(2)}) collective-permute-start(bf16[4,128,256]{2,1,0:T(8,128)(2,1)S(1)} %pad_maximum_fusion.kv), channel_id=1, source_target_pairs={{0,8},{1,9},{2,10},{3,11},{4,12},{5,13},{6,14},{7,15},{8,16},{9,17... | collective-permute-start | bytes 786440 | tf_op jit(solution)/shard_map/ppermute | solution.py:199
  48.1 23.5 %collective-permute-start.6 = (bf16[4,128,256]{2,1,0:T(8,128)(2,1)S(1)}, bf16[4,128,256]{2,1,0:T(8,128)(2,1)S(1)}, u32[]{:S(2)}, u32[]{:S(2)}) collective-permute-start(bf16[4,128,256]{2,1,0:T(8,128)(2,1)S(1)} %pad_maximum_fusion.kv), channel_id=1, source_target_pairs={{0,4},{1,5},{2,6},{3,7},{4,8},{5,9},{6,10},{7,11},{8,12},{9,13},{1... | collective-permute-start | bytes 786440 | tf_op jit(solution)/shard_map/ppermute | solution.py:199
  64.0 1.3 %copy-start.6 = (f32[4,128,1024]{2,1,0:T(8,128)}, f32[4,128,1024]{2,1,0:T(8,128)S(1)}, u32[]{:S(2)}) copy-start(f32[4,128,1024]{2,1,0:T(8,128)S(1)} %get-tuple-element.34.dq_in) | copy-start | bytes 6291460
  77.8 20.6 %collective-permute-start.11 = (bf16[4,128,256]{2,1,0:T(8,128)(2,1)S(1)}, bf16[4,128,256]{2,1,0:T(8,128)(2,1)S(1)}, u32[]{:S(2)}, u32[]{:S(2)}) collective-permute-start(bf16[4,128,256]{2,1,0:T(8,128)(2,1)S(1)} %get-tuple-element.41), channel_id=1, source_target_pairs={{4,0},{5,1},{6,2},{7,3},{8,4},{9,5},{10,6},{11,7},{12,8},{13,9},{1... | collective-permute-start | bytes 786440 | tf_op jit(solution)/shard_map/ppermute | solution.py:199
  80.0 19.6 %collective-permute-start.12 = (bf16[4,128,256]{2,1,0:T(8,128)(2,1)S(1)}, bf16[4,128,256]{2,1,0:T(8,128)(2,1)S(1)}, u32[]{:S(2)}, u32[]{:S(2)}) collective-permute-start(bf16[4,128,256]{2,1,0:T(8,128)(2,1)S(1)} %get-tuple-element.42), channel_id=1, source_target_pairs={{8,0},{9,1},{10,2},{11,3},{12,4},{13,5},{14,6},{15,7},{16,8},{17,9... | collective-permute-start | bytes 786440 | tf_op jit(solution)/shard_map/ppermute | solution.py:199
  94.2 13.6 %collective-permute-start.8 = (bf16[128,1024]{1,0:T(8,128)(2,1)S(1)}, bf16[128,1024]{1,0:T(8,128)(2,1)S(1)}, u32[]{:S(2)}, u32[]{:S(2)}) collective-permute-start(bf16[128,1024]{1,0:T(8,128)(2,1)S(1)} %get-tuple-element.37), channel_id=1, source_target_pairs={{0,3},{1,0},{2,1},{3,2},{4,7},{5,4},{6,5},{7,6},{8,11},{9,8},{10,9... | collective-permute-start | bytes 786440 | tf_op jit(solution)/shard_map/ppermute | solution.py:195
  97.5 10.4 %collective-permute-start.9 = (bf16[128,1024]{1,0:T(8,128)(2,1)S(1)}, bf16[128,1024]{1,0:T(8,128)(2,1)S(1)}, u32[]{:S(2)}, u32[]{:S(2)}) collective-permute-start(bf16[128,1024]{1,0:T(8,128)(2,1)S(1)} %get-tuple-element.38), channel_id=1, source_target_pairs={{0,2},{1,3},{2,0},{3,1},{4,6},{5,7},{6,4},{7,5},{8,10},{9,11},{10,... | collective-permute-start | bytes 786440 | tf_op jit(solution)/shard_map/ppermute | solution.py:195
  97.5 13.0 %collective-permute-start.10 = (bf16[128,1024]{1,0:T(8,128)(2,1)S(1)}, bf16[128,1024]{1,0:T(8,128)(2,1)S(1)}, u32[]{:S(2)}, u32[]{:S(2)}) collective-permute-start(bf16[128,1024]{1,0:T(8,128)(2,1)S(1)} %get-tuple-element.39), channel_id=1, source_target_pairs={{0,1},{1,2},{2,3},{3,0},{4,5},{5,6},{6,7},{7,4},{8,9},{9,10},{10,1... | collective-permute-start | bytes 786440 | tf_op jit(solution)/shard_map/ppermute | solution.py:195
  99.7 11.9 %collective-permute-start.13 = (bf16[128,256]{1,0:T(8,128)(2,1)S(1)}, bf16[128,256]{1,0:T(8,128)(2,1)S(1)}, u32[]{:S(2)}, u32[]{:S(2)}) collective-permute-start(bf16[128,256]{1,0:T(8,128)(2,1)S(1)} %get-tuple-element.44), channel_id=1, source_target_pairs={{0,3},{1,0},{2,1},{3,2},{4,7},{5,4},{6,5},{7,6},{8,11},{9,8},{10,9... | collective-permute-start | bytes 196616 | tf_op jit(solution)/shard_map/ppermute | solution.py:195
  103.5 8.1 %collective-permute-start.14 = (bf16[128,256]{1,0:T(8,128)(2,1)S(1)}, bf16[128,256]{1,0:T(8,128)(2,1)S(1)}, u32[]{:S(2)}, u32[]{:S(2)}) collective-permute-start(bf16[128,256]{1,0:T(8,128)(2,1)S(1)} %get-tuple-element.45), channel_id=1, source_target_pairs={{0,2},{1,3},{2,0},{3,1},{4,6},{5,7},{6,4},{7,5},{8,10},{9,11},{10,... | collective-permute-start | bytes 196616 | tf_op jit(solution)/shard_map/ppermute | solution.py:195
  107.9 5.9 %collective-permute-start.15 = (bf16[128,256]{1,0:T(8,128)(2,1)S(1)}, bf16[128,256]{1,0:T(8,128)(2,1)S(1)}, u32[]{:S(2)}, u32[]{:S(2)}) collective-permute-start(bf16[128,256]{1,0:T(8,128)(2,1)S(1)} %get-tuple-element.46), channel_id=1, source_target_pairs={{0,1},{1,2},{2,3},{3,0},{4,5},{5,6},{6,7},{7,4},{8,9},{9,10},{10,1... | collective-permute-start | bytes 196616 | tf_op jit(solution)/shard_map/ppermute | solution.py:195

commit v2 on v1

--- a/solution.py
+++ b/solution.py
@@ -21,7 +21,7 @@
 
 VMEM = pl.BlockSpec(memory_space=pltpu.VMEM)
 SMEM = pl.BlockSpec(memory_space=pltpu.SMEM)
-PARAMS = pltpu.CompilerParams(vmem_limit_bytes=48 << 20)
+PARAMS = pltpu.CompilerParams(vmem_limit_bytes=24 << 20)
 
 
 def nt(left, right):
@@ -86,7 +86,6 @@
     place = lax.rem(head, ROW)
     own_row = head // ROW
     first_key = lax.axis_index("seq") * (ROW * ROW) + (own_row - back) * ROW
-    dkv[...] = jnp.zeros_like(dkv)
     for slot in range(ROW):
         query_place = lax.rem(place + ROW - slot, ROW)
         start = doc_start[own_row * ROW + query_place]
@@ -125,6 +124,7 @@
 
 def row_two(doc_start, piece0, piece1, piece2, piece3, kv, dkv_out, dq, dkv):
     dq[...] = jnp.zeros_like(dq)
+    dkv[...] = jnp.zeros_like(dkv)
     sweep(2, doc_start, (piece0, piece1, piece2, piece3), kv, dq, dkv)
     dkv_out[:, :, :DH] = (dkv[:, :, :DH] * SCALE).astype(BF16)
     dkv_out[:, :, DH:] = dkv[:, :, DH:].astype(BF16)
@@ -132,27 +132,28 @@
 
 def row_one(doc_start, piece0, piece1, piece2, piece3, kv, dq_in, dkv_out, dq, dkv):
     dq[...] = dq_in[...]
+    dkv[...] = jnp.zeros_like(dkv)
     sweep(1, doc_start, (piece0, piece1, piece2, piece3), kv, dq, dkv)
     dkv_out[:, :, :DH] = (dkv[:, :, :DH] * SCALE).astype(BF16)
     dkv_out[:, :, DH:] = dkv[:, :, DH:].astype(BF16)
 
 
-def row_own(doc_start, piece0, piece1, piece2, piece3, kv, dq_in, dkv, *rest):
+def row_own(doc_start, piece0, piece1, piece2, piece3, kv, dq_in, back_two, dkv, *rest):
     outs, dq = rest[:ROW], rest[ROW]
     dq[...] = dq_in[...]
+    dkv[...] = jnp.zeros_like(dkv)
     sweep(0, doc_start, (piece0, piece1, piece2, piece3), kv, dq, dkv)
-    dkv[:, :, :DH] = dkv[:, :, :DH] * SCALE
+    dkv[:, :, :DH] = dkv[:, :, :DH] * SCALE + back_two[:, :, :DH].astype(F32)
+    dkv[:, :, DH:] = dkv[:, :, DH:] + back_two[:, :, DH:].astype(F32)
     for slot in range(ROW):
         for head in range(GQ):
             cut = slice(head * DH, (head + 1) * DH)
             outs[slot][:, cut] = (dq[slot, :, cut].T * SCALE).astype(BF16)
 
 
-def add_up(own, one, two, *pieces):
+def add_up(own, one, *pieces):
     for slot in range(ROW):
-        pieces[slot][...] = (
-            own[slot] + one[slot].astype(F32) + two[slot].astype(F32)
-        ).astype(BF16)
+        pieces[slot][...] = (own[slot] + one[slot].astype(F32)).astype(BF16)
 
 
 def join_queries(piece0, piece1, piece2, piece3, out):
@@ -201,14 +202,15 @@
         )
 
     kv_sent = kernel(
-        pack_kv, "pack_kv", [VMEM] * 2, [((BLOCK, 2 * DH), BF16)] * ROW, size=1 << 19
+        pack_kv, "pack_kv", [VMEM] * 2, [((BLOCK, 2 * DH), BF16)] * ROW
     )(keys, values)
     kv_own = jnp.stack([along_row(kv_sent[shift], shift) for shift in range(ROW)])
+    sent = kernel(
+        pack_queries, "pack_queries", [VMEM] * 4, [((PIECE, WIDE), BF16)] * ROW
+    )(queries, outputs, out_grads, log_norms)
+    kv_own, *sent = lax.optimization_barrier((kv_own, *sent))
     kv_two = along_rows(kv_own, 2)
     kv_one = along_rows(kv_own, 1)
-    sent = kernel(
-        pack_queries, "pack_queries", [VMEM] * 4, [((PIECE, WIDE), BF16)] * ROW, size=5 << 20
-    )(queries, outputs, out_grads, log_norms)
     pieces = [along_row(sent[shift], shift) for shift in range(ROW)]
 
     dq_shape = ((ROW, DH, WIDE), F32)
@@ -220,7 +222,6 @@
         [SMEM] + [VMEM] * 5,
         [(kv_shape, BF16), dq_shape],
         scratch,
-        flops=6 * 1 << 30,
     )(doc_start, *pieces, kv_two)
     back_two = along_rows(dkv_two, -2)
     dkv_one, dq = kernel(
@@ -229,27 +230,25 @@
         [SMEM] + [VMEM] * 6,
         [(kv_shape, BF16), dq_shape],
         scratch,
-        flops=16 * 1 << 30,
     )(doc_start, *pieces, kv_one, dq)
     back_one = along_rows(dkv_one, -1)
     dkv_own, *dq_sent = kernel(
         row_own,
         "row_own",
-        [SMEM] + [VMEM] * 6,
+        [SMEM] + [VMEM] * 7,
         [(kv_shape, F32)] + [((BLOCK, WIDE), BF16)] * ROW,
         [pltpu.VMEM(*dq_shape)],
-        flops=10 * 1 << 30,
-    )(doc_start, *pieces, kv_own, dq)
+    )(doc_start, *pieces, kv_own, dq, back_two)
     dq_pieces = [along_row(dq_sent[slot], -slot) for slot in range(ROW)]
     dkv_sent = kernel(
-        add_up, "add_up", [VMEM] * 3, [((BLOCK, 2 * DH), BF16)] * ROW, size=1 << 20
-    )(dkv_own, back_one, back_two)
+        add_up, "add_up", [VMEM] * 2, [((BLOCK, 2 * DH), BF16)] * ROW
+    )(dkv_own, back_one)
     dkv_pieces = [along_row(dkv_sent[slot], -slot) for slot in range(ROW)]
     (query_out,) = kernel(
-        join_queries, "join_queries", [VMEM] * ROW, [((BLOCK, H * DH), BF16)], size=2 << 20
+        join_queries, "join_queries", [VMEM] * ROW, [((BLOCK, H * DH), BF16)]
     )(*dq_pieces)
     key_out, value_out = kernel(
-        join_kv, "join_kv", [VMEM] * ROW, [((BLOCK, KVH * DH), BF16)] * 2, size=1 << 19
+        join_kv, "join_kv", [VMEM] * ROW, [((BLOCK, KVH * DH), BF16)] * 2
     )(*dkv_pieces)
     return (query_out, key_out, value_out)
 

time: 116 us -> 96.7 us (0.83)
  waiting for transfers between devices: 48.5 us -> 34.8 us
  starting transfers between devices: 41.8 us -> 37.4 us
  Pallas kernels: 17.6 us -> 15.6 us
    ppermute x12, waiting for transfers between devices: 31.7 us -> 17.7 us  [along_row(): return lax.ppermute(value, AXES, pairs)]
    ppermute x4, starting transfers between devices: 22.8 us -> 20.2 us  [along_rows(): lax.ppermute(value, AXES, [(b, b + by) for b in range(total) if 0 <= b +...]
    pallas_call x1, Pallas kernels: 3.07 us -> 0.98 us  [per_device(): kernel(row_two, 'row_two', [SMEM] + [VMEM] * 5, [(kv_shape, BF16), dq_sha...]
    ppermute x12, starting transfers between devices: 19 us -> 17.1 us  [along_row(): return lax.ppermute(value, AXES, pairs)]
    unnamed x15 -> x13, local copies, waits for them, and re-layouts: 5.83 us -> 6.29 us
  transfers between devices with their start and end apart: 16 -> 16, of which waited for: 10 -> 8; matrix products, arithmetic and copies ran while one was open for 0% -> 1% of each run, Pallas kernels for 8% -> 15%
where the time goes in v2:
time: 96.7 us; the launch traced here: 94.8 us
  starting transfers between devices  37.4 us (39%)
  waiting for transfers between devices  34.8 us (36%)
  Pallas kernels  15.6 us (16%)
  local copies, waits for them, and re-layouts  6.29 us (7%)
    ppermute x4, starting transfers between devices, along_rows(): lax.ppermute(value, AXES, [(b, b + by) for b in range(total) if 0 <= b +...  20.2 us
    ppermute x12, waiting for transfers between devices, along_row(): return lax.ppermute(value, AXES, pairs)  17.7 us
    ppermute x12, starting transfers between devices, along_row(): return lax.ppermute(value, AXES, pairs)  17.1 us
    ppermute x4, waiting for transfers between devices, along_rows(): lax.ppermute(value, AXES, [(b, b + by) for b in range(total) if 0 <= b +...  17.1 us
    unnamed x13, local copies, waits for them, and re-layouts  6.29 us
    pallas_call x1, Pallas kernels, per_device(): kernel(row_own, 'row_own', [SMEM] + [VMEM] * 7, [(kv_shape, F32)] + [((BL...  5.76 us
    pallas_call x1, Pallas kernels, per_device(): kernel(row_one, 'row_one', [SMEM] + [VMEM] * 6, [(kv_shape, BF16), dq_sha...  5.64 us
  transfers between devices with their start and end apart: 16, of which 8 were waited for; matrix products, arithmetic and copies ran while one was open for 1% of the time, Pallas kernels for 15%

profile of v2, /device:TPU:34, one launch (start us, length us, event | category | flops | bytes accessed | tf_op | source)
XLA Modules:
  0.0 94.8 jit_solution(7822938500391201567)
XLA Ops:
  0.6 0.0 copy-start.3
  0.6 0.9 copy-done.3
  1.5 0.0 copy-start.4
  1.5 0.9 copy-done.4
  2.4 0.0 copy-start.5
  2.5 1.7 %collective-permute-start = (bf16[128,256]{1,0:T(8,128)(2,1)S(1)}, bf16[128,256]{1,0:T(8,128)(2,1)S(1)}, u32[]{:S(2)}, u32[]{:S(2)}) collective-permute-start(bf16[128,256]{1,0:T(8,128)(2,1)S(1)} %get-tuple-element.32), channel_id=1, source_target_pairs={{0,1},{1,2},{2,3},{3,0},{4,5},{5,6},{6,7},{7,4},{8,9},{9,10},{10,1... | collective-permute-start | bytes 196616 | tf_op jit(solution)/shard_map/ppermute | solution.py:196
  4.2 2.9 %collective-permute-start.1 = (bf16[128,256]{1,0:T(8,128)(2,1)S(1)}, bf16[128,256]{1,0:T(8,128)(2,1)S(1)}, u32[]{:S(2)}, u32[]{:S(2)}) collective-permute-start(bf16[128,256]{1,0:T(8,128)(2,1)S(1)} %get-tuple-element.33), channel_id=1, source_target_pairs={{0,2},{1,3},{2,0},{3,1},{4,6},{5,7},{6,4},{7,5},{8,10},{9,11},{10,... | collective-permute-start | bytes 196616 | tf_op jit(solution)/shard_map/ppermute | solution.py:196
  7.1 1.3 %collective-permute-start.2 = (bf16[128,256]{1,0:T(8,128)(2,1)S(1)}, bf16[128,256]{1,0:T(8,128)(2,1)S(1)}, u32[]{:S(2)}, u32[]{:S(2)}) collective-permute-start(bf16[128,256]{1,0:T(8,128)(2,1)S(1)} %get-tuple-element.34), channel_id=1, source_target_pairs={{0,3},{1,0},{2,1},{3,2},{4,7},{5,4},{6,5},{7,6},{8,11},{9,8},{10,9... | collective-permute-start | bytes 196616 | tf_op jit(solution)/shard_map/ppermute | solution.py:196
  8.4 0.8 copy.10.norms
  9.2 1.2 %copy-done = bf16[128,4096]{1,0:T(8,128)(2,1)S(1)} copy-done((bf16[128,4096]{1,0:T(8,128)(2,1)S(1)}, bf16[128,4096]{1,0:T(8,128)(2,1)}, u32[]{:S(2)}) %copy-start) | copy-done | bytes 1048600
  10.4 1.2 %copy-done.1 = bf16[128,4096]{1,0:T(8,128)(2,1)S(1)} copy-done((bf16[128,4096]{1,0:T(8,128)(2,1)S(1)}, bf16[128,4096]{1,0:T(8,128)(2,1)}, u32[]{:S(2)}) %copy-start.1) | copy-done | bytes 1048600
  11.7 1.2 %copy-done.2 = bf16[128,4096]{1,0:T(8,128)(2,1)S(1)} copy-done((bf16[128,4096]{1,0:T(8,128)(2,1)S(1)}, bf16[128,4096]{1,0:T(8,128)(2,1)}, u32[]{:S(2)}) %copy-start.2) | copy-done | bytes 1048600
  12.9 1.3 %pack_queries.1 = (bf16[272,1024]{1,0:T(8,128)(2,1)S(1)}, bf16[272,1024]{1,0:T(8,128)(2,1)S(1)}, bf16[272,1024]{1,0:T(8,128)(2,1)S(1)}, bf16[272,1024]{1,0:T(8,128)(2,1)S(1)}) custom-call(bf16[128,4096]{1,0:T(8,128)(2,1)S(1)} %copy-done, bf16[128,4096]{1,0:T(8,128)(2,1)S(1)} %copy-done.1, bf16[128,4096]{1,0:T(8,128)(2,1)S(1)} %copy-done.2, ...), custom_call_target="tpu_custom_call" | custom-call | tf_op jit(solution)/shard_map/pack_queries/pallas_call | solution.py:208
  14.2 0.0 collective-permute-done
  14.2 0.0 collective-permute-done.1
  14.2 0.0 collective-permute-done.2
  14.3 0.8 collective-permute-start.3
  15.0 0.8 collective-permute-start.4
  15.8 2.0 %collective-permute-start.5 = (bf16[272,1024]{1,0:T(8,128)(2,1)S(1)}, bf16[272,1024]{1,0:T(8,128)(2,1)S(1)}, u32[]{:S(2)}, u32[]{:S(2)}) collective-permute-start(bf16[272,1024]{1,0:T(8,128)(2,1)S(1)} %get-tuple-element.42), channel_id=1, source_target_pairs={{0,3},{1,0},{2,1},{3,2},{4,7},{5,4},{6,5},{7,6},{8,11},{9,8},{10,9... | collective-permute-start | bytes 1671176 | tf_op jit(solution)/shard_map/ppermute | solution.py:196
  17.8 8.2 %collective-permute-start.7 = (bf16[4,128,256]{2,1,0:T(8,128)(2,1)S(1)}, bf16[4,128,256]{2,1,0:T(8,128)(2,1)S(1)}, u32[]{:S(2)}, u32[]{:S(2)}) collective-permute-start(bf16[4,128,256]{2,1,0:T(8,128)(2,1)S(1)} %pad_maximum_fusion.kv), channel_id=1, source_target_pairs={{0,8},{1,9},{2,10},{3,11},{4,12},{5,13},{6,14},{7,15},{8,16},{9,17... | collective-permute-start | bytes 786440 | tf_op jit(solution)/shard_map/ppermute | solution.py:200
  26.0 3.4 %collective-permute-start.6 = (bf16[4,128,256]{2,1,0:T(8,128)(2,1)S(1)}, bf16[4,128,256]{2,1,0:T(8,128)(2,1)S(1)}, u32[]{:S(2)}, u32[]{:S(2)}) collective-permute-start(bf16[4,128,256]{2,1,0:T(8,128)(2,1)S(1)} %pad_maximum_fusion.kv), channel_id=1, source_target_pairs={{0,4},{1,5},{2,6},{3,7},{4,8},{5,9},{6,10},{7,11},{8,12},{9,13},{1... | collective-permute-start | bytes 786440 | tf_op jit(solution)/shard_map/ppermute | solution.py:200
  29.4 9.3 %collective-permute-done.7.kv = bf16[4,128,256]{2,1,0:T(8,128)(2,1)S(1)} collective-permute-done((bf16[4,128,256]{2,1,0:T(8,128)(2,1)S(1)}, bf16[4,128,256]{2,1,0:T(8,128)(2,1)S(1)}, u32[]{:S(2)}, u32[]{:S(2)}) %collective-permute-start.7) | collective-permute-done | bytes 262176 | tf_op jit(solution)/shard_map/ppermute | solution.py:200
  38.7 2.3 %collective-permute-done.3.piece1 = bf16[272,1024]{1,0:T(8,128)(2,1)S(1)} collective-permute-done((bf16[272,1024]{1,0:T(8,128)(2,1)S(1)}, bf16[272,1024]{1,0:T(8,128)(2,1)S(1)}, u32[]{:S(2)}, u32[]{:S(2)}) %collective-permute-start.3) | collective-permute-done | bytes 557088 | tf_op jit(solution)/shard_map/ppermute | solution.py:196
  41.0 0.0 collective-permute-done.4.piece2
  41.0 0.6 collective-permute-done.5.piece3
  41.7 0.0 copy-done.5
  41.7 1.0 %row_two.1 = (bf16[4,128,256]{2,1,0:T(8,128)(2,1)S(1)}, f32[4,128,1024]{2,1,0:T(8,128)S(1)}) custom-call(s32[16]{0:T(128)S(1)} %copy-done.5, bf16[272,1024]{1,0:T(8,128)(2,1)S(1)} %get-tuple-element.39.piece0, bf16[272,1024]{1,0:T(8,128)(2,1)S(1)} %collective-permute-done.3.piece1, bf16[272,1024]{1,0:T(8,128)(2,1)S(1)} %collective-permute-done.4.piece2, ...), custom_call_target="tpu_custom_call" | custom-call | tf_op jit(solution)/shard_map/row_two/pallas_call | solution.py:219
  42.6 6.6 %collective-permute-start.8 = (bf16[4,128,256]{2,1,0:T(8,128)(2,1)S(1)}, bf16[4,128,256]{2,1,0:T(8,128)(2,1)S(1)}, u32[]{:S(2)}, u32[]{:S(2)}) collective-permute-start(bf16[4,128,256]{2,1,0:T(8,128)(2,1)S(1)} %get-tuple-element.46), channel_id=1, source_target_pairs={{8,0},{9,1},{10,2},{11,3},{12,4},{13,5},{14,6},{15,7},{16,8},{17,9... | collective-permute-start | bytes 786440 | tf_op jit(solution)/shard_map/ppermute | solution.py:200
  49.2 0.3 collective-permute-done.6.kv
  49.5 5.6 %row_one.1 = (bf16[4,128,256]{2,1,0:T(8,128)(2,1)S(1)}, f32[4,128,1024]{2,1,0:T(8,128)S(1)}) custom-call(s32[16]{0:T(128)S(1)} %copy-done.5, bf16[272,1024]{1,0:T(8,128)(2,1)S(1)} %get-tuple-element.39.piece0, bf16[272,1024]{1,0:T(8,128)(2,1)S(1)} %collective-permute-done.3.piece1, bf16[272,1024]{1,0:T(8,128)(2,1)S(1)} %collective-permute-done.4.piece2, ...), custom_call_target="tpu_custom_call" | custom-call | tf_op jit(solution)/shard_map/row_one/pallas_call | solution.py:227
  55.2 2.1 %collective-permute-start.12 = (bf16[4,128,256]{2,1,0:T(8,128)(2,1)S(1)}, bf16[4,128,256]{2,1,0:T(8,128)(2,1)S(1)}, u32[]{:S(2)}, u32[]{:S(2)}) collective-permute-start(bf16[4,128,256]{2,1,0:T(8,128)(2,1)S(1)} %get-tuple-element.52), channel_id=1, source_target_pairs={{4,0},{5,1},{6,2},{7,3},{8,4},{9,5},{10,6},{11,7},{12,8},{13,9},{1... | collective-permute-start | bytes 786440 | tf_op jit(solution)/shard_map/ppermute | solution.py:200
  57.3 7.5 %collective-permute-done.8.back_two = bf16[4,128,256]{2,1,0:T(8,128)(2,1)S(1)} collective-permute-done((bf16[4,128,256]{2,1,0:T(8,128)(2,1)S(1)}, bf16[4,128,256]{2,1,0:T(8,128)(2,1)S(1)}, u32[]{:S(2)}, u32[]{:S(2)}) %collective-permute-start.8) | collective-permute-done | bytes 262176 | tf_op jit(solution)/shard_map/ppermute | solution.py:200
  64.8 5.8 %row_own.1 = (f32[4,128,256]{2,1,0:T(8,128)S(1)}, bf16[128,1024]{1,0:T(8,128)(2,1)S(1)}, bf16[128,1024]{1,0:T(8,128)(2,1)S(1)}, bf16[128,1024]{1,0:T(8,128)(2,1)S(1)}, bf16[128,1024]{1,0:T(8,128)(2,1)S(1)}) custom-call(s32[16]{0:T(128)S(1)} %copy-done.5, bf16[272,1024]{1,0:T(8,128)(2,1)S(1)} %get-tuple-element.39.piece0, ...), custom_call_target="tpu_custom_call" | custom-call | tf_op jit(solution)/shard_map/row_own/pallas_call | solution.py:235
  70.5 2.1 %collective-permute-start.9 = (bf16[128,1024]{1,0:T(8,128)(2,1)S(1)}, bf16[128,1024]{1,0:T(8,128)(2,1)S(1)}, u32[]{:S(2)}, u32[]{:S(2)}) collective-permute-start(bf16[128,1024]{1,0:T(8,128)(2,1)S(1)} %get-tuple-element.48), channel_id=1, source_target_pairs={{0,3},{1,0},{2,1},{3,2},{4,7},{5,4},{6,5},{7,6},{8,11},{9,8},{10,9... | collective-permute-start | bytes 786440 | tf_op jit(solution)/shard_map/ppermute | solution.py:196
  72.6 0.0 collective-permute-start.10
  72.6 1.0 %collective-permute-start.11 = (bf16[128,1024]{1,0:T(8,128)(2,1)S(1)}, bf16[128,1024]{1,0:T(8,128)(2,1)S(1)}, u32[]{:S(2)}, u32[]{:S(2)}) collective-permute-start(bf16[128,1024]{1,0:T(8,128)(2,1)S(1)} %get-tuple-element.50), channel_id=1, source_target_pairs={{0,1},{1,2},{2,3},{3,0},{4,5},{5,6},{6,7},{7,4},{8,9},{9,10},{10,1... | collective-permute-start | bytes 786440 | tf_op jit(solution)/shard_map/ppermute | solution.py:196
  73.6 0.0 collective-permute-done.12.one
  73.6 2.4 %collective-permute-start.13 = (bf16[128,256]{1,0:T(8,128)(2,1)S(1)}, bf16[128,256]{1,0:T(8,128)(2,1)S(1)}, u32[]{:S(2)}, u32[]{:S(2)}) collective-permute-start(bf16[128,256]{1,0:T(8,128)(2,1)S(1)} %get-tuple-element.54), channel_id=1, source_target_pairs={{0,3},{1,0},{2,1},{3,2},{4,7},{5,4},{6,5},{7,6},{8,11},{9,8},{10,9... | collective-permute-start | bytes 196616 | tf_op jit(solution)/shard_map/ppermute | solution.py:196
  76.0 2.3 %collective-permute-start.14 = (bf16[128,256]{1,0:T(8,128)(2,1)S(1)}, bf16[128,256]{1,0:T(8,128)(2,1)S(1)}, u32[]{:S(2)}, u32[]{:S(2)}) collective-permute-start(bf16[128,256]{1,0:T(8,128)(2,1)S(1)} %get-tuple-element.55), channel_id=1, source_target_pairs={{0,2},{1,3},{2,0},{3,1},{4,6},{5,7},{6,4},{7,5},{8,10},{9,11},{10,... | collective-permute-start | bytes 196616 | tf_op jit(solution)/shard_map/ppermute | solution.py:196
  78.3 8.8 %collective-permute-done.13.piece1 = bf16[128,256]{1,0:T(8,128)(2,1)S(1)} collective-permute-done((bf16[128,256]{1,0:T(8,128)(2,1)S(1)}, bf16[128,256]{1,0:T(8,128)(2,1)S(1)}, u32[]{:S(2)}, u32[]{:S(2)}) %collective-permute-start.13) | collective-permute-done | bytes 65568 | tf_op jit(solution)/shard_map/ppermute | solution.py:196
  87.1 0.0 collective-permute-start.15
  87.1 2.3 %collective-permute-done.14.piece2 = bf16[128,256]{1,0:T(8,128)(2,1)S(1)} collective-permute-done((bf16[128,256]{1,0:T(8,128)(2,1)S(1)}, bf16[128,256]{1,0:T(8,128)(2,1)S(1)}, u32[]{:S(2)}, u32[]{:S(2)}) %collective-permute-start.14) | collective-permute-done | bytes 65568 | tf_op jit(solution)/shard_map/ppermute | solution.py:196
  89.4 3.6 %collective-permute-done.15.piece3 = bf16[128,256]{1,0:T(8,128)(2,1)S(1)} collective-permute-done((bf16[128,256]{1,0:T(8,128)(2,1)S(1)}, bf16[128,256]{1,0:T(8,128)(2,1)S(1)}, u32[]{:S(2)}, u32[]{:S(2)}) %collective-permute-start.15) | collective-permute-done | bytes 65568 | tf_op jit(solution)/shard_map/ppermute | solution.py:196
  93.0 0.7 join_kv.1
  93.8 0.0 collective-permute-done.9.piece1
  93.8 0.0 collective-permute-done.10.piece2
  93.8 0.0 collective-permute-done.11.piece3
  93.8 1.1 %join_queries.1 = bf16[128,4096]{1,0:T(8,128)(2,1)} custom-call(bf16[128,1024]{1,0:T(8,128)(2,1)S(1)} %get-tuple-element.47.piece0, bf16[128,1024]{1,0:T(8,128)(2,1)S(1)} %collective-permute-done.9.piece1, bf16[128,1024]{1,0:T(8,128)(2,1)S(1)} %collective-permute-done.10.piece2, bf16[128,1024]{1,0:T(8,128)(2,1)S(1)} %collective-permute-done.11.piece3), custom_call_target="tpu_custom_call" | custom-call | tf_op jit(solution)/shard_map/join_queries/pallas_call | solution.py:247
  (6 shorter events, 0.1 us)
Async XLA Ops:
  0.6 0.9 copy-start.3
  1.5 0.9 copy-start.4
  2.4 39.2 %copy-start.5 = (s32[16]{0:T(128)S(1)}, s32[16]{0:T(128)}, u32[]{:S(2)}) copy-start(s32[16]{0:T(128)} %doc_start.5) | copy-start | bytes 196
  2.5 11.7 %collective-permute-start = (bf16[128,256]{1,0:T(8,128)(2,1)S(1)}, bf16[128,256]{1,0:T(8,128)(2,1)S(1)}, u32[]{:S(2)}, u32[]{:S(2)}) collective-permute-start(bf16[128,256]{1,0:T(8,128)(2,1)S(1)} %get-tuple-element.32), channel_id=1, source_target_pairs={{0,1},{1,2},{2,3},{3,0},{4,5},{5,6},{6,7},{7,4},{8,9},{9,10},{10,1... | collective-permute-start | bytes 196616 | tf_op jit(solution)/shard_map/ppermute | solution.py:196
  4.2 10.1 %collective-permute-start.1 = (bf16[128,256]{1,0:T(8,128)(2,1)S(1)}, bf16[128,256]{1,0:T(8,128)(2,1)S(1)}, u32[]{:S(2)}, u32[]{:S(2)}) collective-permute-start(bf16[128,256]{1,0:T(8,128)(2,1)S(1)} %get-tuple-element.33), channel_id=1, source_target_pairs={{0,2},{1,3},{2,0},{3,1},{4,6},{5,7},{6,4},{7,5},{8,10},{9,11},{10,... | collective-permute-start | bytes 196616 | tf_op jit(solution)/shard_map/ppermute | solution.py:196
  7.1 7.2 %collective-permute-start.2 = (bf16[128,256]{1,0:T(8,128)(2,1)S(1)}, bf16[128,256]{1,0:T(8,128)(2,1)S(1)}, u32[]{:S(2)}, u32[]{:S(2)}) collective-permute-start(bf16[128,256]{1,0:T(8,128)(2,1)S(1)} %get-tuple-element.34), channel_id=1, source_target_pairs={{0,3},{1,0},{2,1},{3,2},{4,7},{5,4},{6,5},{7,6},{8,11},{9,8},{10,9... | collective-permute-start | bytes 196616 | tf_op jit(solution)/shard_map/ppermute | solution.py:196
  9.2 1.2 %copy-start = (bf16[128,4096]{1,0:T(8,128)(2,1)S(1)}, bf16[128,4096]{1,0:T(8,128)(2,1)}, u32[]{:S(2)}) copy-start(bf16[128,4096]{1,0:T(8,128)(2,1)} %queries.1) | copy-start | bytes 3145732
  10.4 1.2 %copy-start.1 = (bf16[128,4096]{1,0:T(8,128)(2,1)S(1)}, bf16[128,4096]{1,0:T(8,128)(2,1)}, u32[]{:S(2)}) copy-start(bf16[128,4096]{1,0:T(8,128)(2,1)} %outputs.1) | copy-start | bytes 3145732
  11.7 1.2 %copy-start.2 = (bf16[128,4096]{1,0:T(8,128)(2,1)S(1)}, bf16[128,4096]{1,0:T(8,128)(2,1)}, u32[]{:S(2)}) copy-start(bf16[128,4096]{1,0:T(8,128)(2,1)} %grads.1) | copy-start | bytes 3145732
  14.3 26.8 %collective-permute-start.3 = (bf16[272,1024]{1,0:T(8,128)(2,1)S(1)}, bf16[272,1024]{1,0:T(8,128)(2,1)S(1)}, u32[]{:S(2)}, u32[]{:S(2)}) collective-permute-start(bf16[272,1024]{1,0:T(8,128)(2,1)S(1)} %get-tuple-element.40), channel_id=1, source_target_pairs={{0,1},{1,2},{2,3},{3,0},{4,5},{5,6},{6,7},{7,4},{8,9},{9,10},{10,1... | collective-permute-start | bytes 1671176 | tf_op jit(solution)/shard_map/ppermute | solution.py:196
  15.0 26.0 %collective-permute-start.4 = (bf16[272,1024]{1,0:T(8,128)(2,1)S(1)}, bf16[272,1024]{1,0:T(8,128)(2,1)S(1)}, u32[]{:S(2)}, u32[]{:S(2)}) collective-permute-start(bf16[272,1024]{1,0:T(8,128)(2,1)S(1)} %get-tuple-element.41), channel_id=1, source_target_pairs={{0,2},{1,3},{2,0},{3,1},{4,6},{5,7},{6,4},{7,5},{8,10},{9,11},{10,... | collective-permute-start | bytes 1671176 | tf_op jit(solution)/shard_map/ppermute | solution.py:196
  15.8 25.8 %collective-permute-start.5 = (bf16[272,1024]{1,0:T(8,128)(2,1)S(1)}, bf16[272,1024]{1,0:T(8,128)(2,1)S(1)}, u32[]{:S(2)}, u32[]{:S(2)}) collective-permute-start(bf16[272,1024]{1,0:T(8,128)(2,1)S(1)} %get-tuple-element.42), channel_id=1, source_target_pairs={{0,3},{1,0},{2,1},{3,2},{4,7},{5,4},{6,5},{7,6},{8,11},{9,8},{10,9... | collective-permute-start | bytes 1671176 | tf_op jit(solution)/shard_map/ppermute | solution.py:196
  17.8 20.9 %collective-permute-start.7 = (bf16[4,128,256]{2,1,0:T(8,128)(2,1)S(1)}, bf16[4,128,256]{2,1,0:T(8,128)(2,1)S(1)}, u32[]{:S(2)}, u32[]{:S(2)}) collective-permute-start(bf16[4,128,256]{2,1,0:T(8,128)(2,1)S(1)} %pad_maximum_fusion.kv), channel_id=1, source_target_pairs={{0,8},{1,9},{2,10},{3,11},{4,12},{5,13},{6,14},{7,15},{8,16},{9,17... | collective-permute-start | bytes 786440 | tf_op jit(solution)/shard_map/ppermute | solution.py:200
  26.0 23.5 %collective-permute-start.6 = (bf16[4,128,256]{2,1,0:T(8,128)(2,1)S(1)}, bf16[4,128,256]{2,1,0:T(8,128)(2,1)S(1)}, u32[]{:S(2)}, u32[]{:S(2)}) collective-permute-start(bf16[4,128,256]{2,1,0:T(8,128)(2,1)S(1)} %pad_maximum_fusion.kv), channel_id=1, source_target_pairs={{0,4},{1,5},{2,6},{3,7},{4,8},{5,9},{6,10},{7,11},{8,12},{9,13},{1... | collective-permute-start | bytes 786440 | tf_op jit(solution)/shard_map/ppermute | solution.py:200
  42.6 22.1 %collective-permute-start.8 = (bf16[4,128,256]{2,1,0:T(8,128)(2,1)S(1)}, bf16[4,128,256]{2,1,0:T(8,128)(2,1)S(1)}, u32[]{:S(2)}, u32[]{:S(2)}) collective-permute-start(bf16[4,128,256]{2,1,0:T(8,128)(2,1)S(1)} %get-tuple-element.46), channel_id=1, source_target_pairs={{8,0},{9,1},{10,2},{11,3},{12,4},{13,5},{14,6},{15,7},{16,8},{17,9... | collective-permute-start | bytes 786440 | tf_op jit(solution)/shard_map/ppermute | solution.py:200
  55.2 18.4 %collective-permute-start.12 = (bf16[4,128,256]{2,1,0:T(8,128)(2,1)S(1)}, bf16[4,128,256]{2,1,0:T(8,128)(2,1)S(1)}, u32[]{:S(2)}, u32[]{:S(2)}) collective-permute-start(bf16[4,128,256]{2,1,0:T(8,128)(2,1)S(1)} %get-tuple-element.52), channel_id=1, source_target_pairs={{4,0},{5,1},{6,2},{7,3},{8,4},{9,5},{10,6},{11,7},{12,8},{13,9},{1... | collective-permute-start | bytes 786440 | tf_op jit(solution)/shard_map/ppermute | solution.py:200
  70.5 23.2 %collective-permute-start.9 = (bf16[128,1024]{1,0:T(8,128)(2,1)S(1)}, bf16[128,1024]{1,0:T(8,128)(2,1)S(1)}, u32[]{:S(2)}, u32[]{:S(2)}) collective-permute-start(bf16[128,1024]{1,0:T(8,128)(2,1)S(1)} %get-tuple-element.48), channel_id=1, source_target_pairs={{0,3},{1,0},{2,1},{3,2},{4,7},{5,4},{6,5},{7,6},{8,11},{9,8},{10,9... | collective-permute-start | bytes 786440 | tf_op jit(solution)/shard_map/ppermute | solution.py:196
  72.6 21.1 %collective-permute-start.10 = (bf16[128,1024]{1,0:T(8,128)(2,1)S(1)}, bf16[128,1024]{1,0:T(8,128)(2,1)S(1)}, u32[]{:S(2)}, u32[]{:S(2)}) collective-permute-start(bf16[128,1024]{1,0:T(8,128)(2,1)S(1)} %get-tuple-element.49), channel_id=1, source_target_pairs={{0,2},{1,3},{2,0},{3,1},{4,6},{5,7},{6,4},{7,5},{8,10},{9,11},{10,... | collective-permute-start | bytes 786440 | tf_op jit(solution)/shard_map/ppermute | solution.py:196
  72.6 21.1 %collective-permute-start.11 = (bf16[128,1024]{1,0:T(8,128)(2,1)S(1)}, bf16[128,1024]{1,0:T(8,128)(2,1)S(1)}, u32[]{:S(2)}, u32[]{:S(2)}) collective-permute-start(bf16[128,1024]{1,0:T(8,128)(2,1)S(1)} %get-tuple-element.50), channel_id=1, source_target_pairs={{0,1},{1,2},{2,3},{3,0},{4,5},{5,6},{6,7},{7,4},{8,9},{9,10},{10,1... | collective-permute-start | bytes 786440 | tf_op jit(solution)/shard_map/ppermute | solution.py:196
  73.6 13.4 %collective-permute-start.13 = (bf16[128,256]{1,0:T(8,128)(2,1)S(1)}, bf16[128,256]{1,0:T(8,128)(2,1)S(1)}, u32[]{:S(2)}, u32[]{:S(2)}) collective-permute-start(bf16[128,256]{1,0:T(8,128)(2,1)S(1)} %get-tuple-element.54), channel_id=1, source_target_pairs={{0,3},{1,0},{2,1},{3,2},{4,7},{5,4},{6,5},{7,6},{8,11},{9,8},{10,9... | collective-permute-start | bytes 196616 | tf_op jit(solution)/shard_map/ppermute | solution.py:196
  76.0 13.4 %collective-permute-start.14 = (bf16[128,256]{1,0:T(8,128)(2,1)S(1)}, bf16[128,256]{1,0:T(8,128)(2,1)S(1)}, u32[]{:S(2)}, u32[]{:S(2)}) collective-permute-start(bf16[128,256]{1,0:T(8,128)(2,1)S(1)} %get-tuple-element.55), channel_id=1, source_target_pairs={{0,2},{1,3},{2,0},{3,1},{4,6},{5,7},{6,4},{7,5},{8,10},{9,11},{10,... | collective-permute-start | bytes 196616 | tf_op jit(solution)/shard_map/ppermute | solution.py:196
  87.1 5.9 %collective-permute-start.15 = (bf16[128,256]{1,0:T(8,128)(2,1)S(1)}, bf16[128,256]{1,0:T(8,128)(2,1)S(1)}, u32[]{:S(2)}, u32[]{:S(2)}) collective-permute-start(bf16[128,256]{1,0:T(8,128)(2,1)S(1)} %get-tuple-element.56), channel_id=1, source_target_pairs={{0,1},{1,2},{2,3},{3,0},{4,5},{5,6},{6,7},{7,4},{8,9},{9,10},{10,1... | collective-permute-start | bytes 196616 | tf_op jit(solution)/shard_map/ppermute | solution.py:196

commit v3 on v1

v3 whole, which is shorter than its diff:
```python
import jax
import jax.numpy as jnp
from jax import lax
from jax.experimental import pallas as pl
from jax.experimental.pallas import tpu as pltpu
from jax.sharding import PartitionSpec as P

H = 32
KVH = 4
DH = 128
BLOCK = 128
GQ = 8
ROW = 4
WIDE = GQ * DH
SCALE = DH ** (-0.5)
AXES = ("seq", "head")
STAT = 2 * BLOCK
PIECE = STAT + 16
F32 = jnp.float32
BF16 = jnp.bfloat16

VMEM = pl.BlockSpec(memory_space=pltpu.VMEM)
HBM = pl.BlockSpec(memory_space=pltpu.HBM)
SMEM = pl.BlockSpec(memory_space=pltpu.SMEM)


def nt(left, right):
    return lax.dot_general(left, right, (((1,), (1,)), ((), ())), preferred_element_type=F32)


def nn(left, right):
    return jnp.dot(left, right, preferred_element_type=F32)


def pack_kv(keys, values, piece0, piece1, piece2, piece3, sems):
    place = lax.rem(lax.axis_index("head"), ROW)
    copies = []
    for shift, piece in enumerate((piece0, piece1, piece2, piece3)):
        columns = pl.ds(pl.multiple_of(lax.rem(place + shift, ROW) * DH, DH), DH)
        for part, source in enumerate((keys, values)):
            copies.append(
                pltpu.make_async_copy(
                    source.at[:, columns],
                    piece.at[:, pl.ds(part * DH, DH)],
                    sems.at[shift, part],
                )
            )
    for copy in copies:
        copy.start()
    for copy in copies:
        copy.wait()


def pack_queries(
    queries, outputs, grads, norms, piece0, piece1, piece2, piece3, held, sems
):
    place = lax.rem(lax.axis_index("head"), ROW)
    pieces = (piece0, piece1, piece2, piece3)
    copies = []
    for shift, piece in enumerate(pieces):
        group = lax.rem(place + shift, ROW)
        span = pl.ds(pl.multiple_of(group * WIDE, WIDE), WIDE)
        copies.append(
            [
                pltpu.make_async_copy(source.at[:, span], target, sems.at[shift, part])
                for part, (source, target) in enumerate(
                    (
                        (grads, piece.at[pl.ds(BLOCK, BLOCK), :]),
                        (outputs, held.at[shift]),
                        (queries, piece.at[pl.ds(0, BLOCK), :]),
                    )
                )
            ]
        )
    for copy in copies:
        for part in copy:
            part.start()
    turned = norms[...].astype(F32)
    ones = jnp.ones((16, DH), BF16)
    row_id = lax.broadcasted_iota(jnp.int32, (16, BLOCK), 0)
    head_id = lax.broadcasted_iota(jnp.int32, (H, BLOCK), 0)
    for shift, piece in enumerate(pieces):
        group = lax.rem(place + shift, ROW)
        copies[shift][0].wait()
        copies[shift][1].wait()
        for head in range(GQ):
            cut = slice(head * DH, (head + 1) * DH)
            product = piece[BLOCK:STAT, cut].astype(F32) * held[shift, :, cut].astype(F32)
            high = product.astype(BF16)
            low = (product - high.astype(F32)).astype(BF16)
            dots = nt(ones, high) + nt(ones, low)
            first = dots.astype(BF16).astype(F32)
            second = (dots - first).astype(BF16).astype(F32)
            third = dots - first - second
            norm = jnp.sum(
                jnp.where(head_id == group * GQ + head, turned, 0.0), axis=0, keepdims=True
            )
            stats = jnp.where(
                row_id == 0,
                norm,
                jnp.where(row_id == 1, first, jnp.where(row_id == 2, second, third)),
            )
            piece[STAT:, cut] = stats.astype(BF16)
    for copy in copies:
        copy[2].wait()


def stacked(piece, start):
    return jnp.concatenate(
        [piece[start : start + BLOCK, head * DH : (head + 1) * DH] for head in range(GQ)], axis=0
    )


def sweep(back, doc_start, pieces, kv, dq, dkv):
    head = lax.axis_index("head")
    place = lax.rem(head, ROW)
    own_row = head // ROW
    first_key = lax.axis_index("seq") * (ROW * ROW) + (own_row - back) * ROW
    for slot, piece in pieces.items():
        query_place = lax.rem(place + ROW - slot, ROW)
        start = doc_start[own_row * ROW + query_place]

        def turn(key_slot, carry, slot=slot, piece=piece, start=start, query_place=query_place):
            key_place = lax.rem(place + ROW - key_slot, ROW)
            seen = first_key + key_place >= start
            if back == 0:
                seen = seen & (key_place <= query_place)

            @pl.when(seen)
            def _():
                key = kv[key_slot, :, :DH]
                value = kv[key_slot, :, DH:]
                query = stacked(piece, 0)
                grad = stacked(piece, BLOCK)
                stats = piece[STAT:, :].astype(F32)
                norm = stats[0:1]
                dots = stats[1:2] + stats[2:3] + stats[3:4]
                weights = jnp.exp(nt(key, query) * SCALE - norm)
                if back == 0:
                    key_pos = lax.broadcasted_iota(jnp.int32, (BLOCK, WIDE), 0)
                    query_pos = lax.broadcasted_iota(jnp.int32, (BLOCK, WIDE), 1) % BLOCK
                    ahead = (query_place - key_place) * BLOCK
                    weights = jnp.where(key_pos <= query_pos + ahead, weights, 0.0)
                grad_scores = (weights * (nt(value, grad) - dots)).astype(BF16)
                dkv[key_slot, :, DH:] += nn(weights.astype(BF16), grad)
                dkv[key_slot, :, :DH] += nn(grad_scores, query)
                dq[slot] += nn(key.T, grad_scores)

            return carry

        lax.fori_loop(0, ROW, turn, 0)


def begin_own(doc_start, piece0, piece1, piece3, kv, dkv, dq):
    dkv[...] = jnp.zeros_like(dkv)
    for slot in (0, 1, 3):
        dq[slot] = jnp.zeros((DH, WIDE), F32)
    sweep(0, doc_start, {0: piece0, 1: piece1, 3: piece3}, kv, dq, dkv)


def begin_one(doc_start, piece0, piece1, piece3, kv, dq_in, dkv, dq):
    dkv[...] = jnp.zeros_like(dkv)
    for slot in (0, 1, 3):
        dq[slot] = dq_in[slot]
    sweep(1, doc_start, {0: piece0, 1: piece1, 3: piece3}, kv, dq, dkv)


def round_kv(dkv, out):
    out[:, :, :DH] = (dkv[:, :, :DH] * SCALE).astype(BF16)
    out[:, :, DH:] = dkv[:, :, DH:].astype(BF16)


def finish_earlier(
    doc_start, piece0, piece1, piece2, piece3, kv_two, kv_one, dkv_in, dq_in,
    two_out, one_out, dq, dkv,
):
    for slot in (0, 1, 3):
        dq[slot] = dq_in[slot]
    dq[2] = jnp.zeros((DH, WIDE), F32)
    dkv[...] = jnp.zeros_like(dkv)
    sweep(2, doc_start, {0: piece0, 1: piece1, 2: piece2, 3: piece3}, kv_two, dq, dkv)
    round_kv(dkv, two_out)
    dkv[...] = dkv_in[...]
    sweep(1, doc_start, {2: piece2}, kv_one, dq, dkv)
    round_kv(dkv, one_out)


def finish_own(doc_start, piece2, kv, dkv_in, dq_in, dkv, out0, out1, out2, out3, late):
    dkv[...] = dkv_in[...]
    late[0] = dq_in[2]
    sweep(0, doc_start, {2: piece2}, kv, Shifted(late), dkv)
    dkv[:, :, :DH] = dkv[:, :, :DH] * SCALE
    for slot, out in enumerate((out0, out1, out2, out3)):
        for head in range(GQ):
            cut = slice(head * DH, (head + 1) * DH)
            total = late[0, :, cut] if slot == 2 else dq_in[slot, :, cut]
            out[:, cut] = (total.T * SCALE).astype(BF16)


class Shifted:
    def __init__(self, ref):
        self.ref = ref

    def __getitem__(self, slot):
        return self.ref[slot - 2]

    def __setitem__(self, slot, value):
        self.ref[slot - 2] = value


def add_up(own, one, two, *pieces):
    for slot in range(ROW):
        pieces[slot][...] = (
            own[slot] + one[slot].astype(F32) + two[slot].astype(F32)
        ).astype(BF16)


def join_queries(piece0, piece1, piece2, piece3, out, sems):
    place = lax.rem(lax.axis_index("head"), ROW)
    copies = []
    for shift, piece in enumerate((piece0, piece1, piece2, piece3)):
        span = pl.ds(pl.multiple_of(lax.rem(place + shift, ROW) * WIDE, WIDE), WIDE)
        copies.append(pltpu.make_async_copy(piece, out.at[:, span], sems.at[shift]))
    for copy in copies:
        copy.start()
    for copy in copies:
        copy.wait()


def join_kv(piece0, piece1, piece2, piece3, key_out, value_out, sems):
    place = lax.rem(lax.axis_index("head"), ROW)
    copies = []
    for shift, piece in enumerate((piece0, piece1, piece2, piece3)):
        columns = pl.ds(pl.multiple_of(lax.rem(place + shift, ROW) * DH, DH), DH)
        for part, out in enumerate((key_out, value_out)):
            copies.append(
                pltpu.make_async_copy(
                    piece.at[:, pl.ds(part * DH, DH)], out.at[:, columns], sems.at[shift, part]
                )
            )
    for copy in copies:
        copy.start()
    for copy in copies:
        copy.wait()


def kernel(body, name, in_specs, shapes, scratch=(), out_spec=VMEM, grant=24):
    return pl.pallas_call(
        body,
        in_specs=in_specs,
        out_specs=[out_spec] * len(shapes),
        out_shape=[jax.ShapeDtypeStruct(*shape) for shape in shapes],
        scratch_shapes=scratch,
        compiler_params=pltpu.CompilerParams(vmem_limit_bytes=grant << 20),
        name=name,
    )


def per_device(queries, outputs, out_grads, log_norms, keys, values, doc_start):
    seqs = lax.axis_size("seq")
    heads = lax.axis_size("head")
    total = seqs * heads
    sems = pltpu.SemaphoreType.DMA

    def along_row(value, shift):
        if shift % ROW == 0:
            return value
        pairs = [(b, b - b % ROW + (b + shift) % ROW) for b in range(total)]
        return lax.ppermute(value, AXES, pairs)

    def along_rows(value, rows):
        by = rows * ROW
        return lax.ppermute(
            value, AXES, [(b, b + by) for b in range(total) if 0 <= b + by < total]
        )

    kv_sent = kernel(
        pack_kv,
        "pack_kv",
        [HBM] * 2,
        [((BLOCK, 2 * DH), BF16)] * ROW,
        [sems((ROW, 2))],
        grant=56,
    )(keys, values)
    kv_pieces = [along_row(kv_sent[shift], shift) for shift in range(ROW)]
    sent = kernel(
        pack_queries,
        "pack_queries",
        [HBM] * 3 + [VMEM],
        [((PIECE, WIDE), BF16)] * ROW,
        [pltpu.VMEM((ROW, BLOCK, WIDE), BF16), sems((ROW, 3))],
        grant=56,
    )(queries, outputs, out_grads, log_norms.T)
    kv_pieces, sent = lax.optimization_barrier((kv_pieces, sent))
    piece0 = sent[0]
    piece1 = along_row(sent[1], 1)
    piece3 = along_row(sent[3], 3)
    kv_own = jnp.stack(kv_pieces)
    kv_two = along_rows(kv_own, 2)
    kv_one = along_rows(kv_own, 1)
    piece2 = along_row(sent[2], 2)

    dq_shape = ((ROW, DH, WIDE), F32)
    kv_shape = (ROW, BLOCK, 2 * DH)
    dkv_own, dq = kernel(
        begin_own, "begin_own", [SMEM] + [VMEM] * 4, [(kv_shape, F32), dq_shape]
    )(doc_start, piece0, piece1, piece3, kv_own)
    dkv_one, dq = kernel(
        begin_one, "begin_one", [SMEM] + [VMEM] * 5, [(kv_shape, F32), dq_shape]
    )(doc_start, piece0, piece1, piece3, kv_one, dq)
    dkv_two, dkv_one, dq = kernel(
        finish_earlier,
        "finish_earlier",
        [SMEM] + [VMEM] * 8,
        [(kv_shape, BF16), (kv_shape, BF16), dq_shape],
        [pltpu.VMEM(kv_shape, F32)],
    )(doc_start, piece0, piece1, piece2, piece3, kv_two, kv_one, dkv_one, dq)
    back_two = along_rows(dkv_two, -2)
    back_one = along_rows(dkv_one, -1)
    dkv_own, *dq_sent = kernel(
        finish_own,
        "finish_own",
        [SMEM] + [VMEM] * 4,
        [(kv_shape, F32)] + [((BLOCK, WIDE), BF16)] * ROW,
        [pltpu.VMEM((1, DH, WIDE), F32)],
    )(doc_start, piece2, kv_own, dkv_own, dq)
    dq_pieces = [along_row(dq_sent[slot], -slot) for slot in range(ROW)]
    dkv_sent = kernel(add_up, "add_up", [VMEM] * 3, [((BLOCK, 2 * DH), BF16)] * ROW)(
        dkv_own, back_one, back_two
    )
    dkv_pieces = [along_row(dkv_sent[slot], -slot) for slot in range(ROW)]
    (query_out,) = kernel(
        join_queries,
        "join_queries",
        [VMEM] * ROW,
        [((BLOCK, H * DH), BF16)],
        [sems((ROW,))],
        HBM,
    )(*dq_pieces)
    key_out, value_out = kernel(
        join_kv,
        "join_kv",
        [VMEM] * ROW,
        [((BLOCK, KVH * DH), BF16)] * 2,
        [sems((ROW, 2))],
        HBM,
    )(*dkv_pieces)
    return (query_out, key_out, value_out)


def solution(mesh):
    placed = P(("seq", "head"), None)
    return jax.shard_map(
        per_device,
        mesh=mesh,
        in_specs=(placed,) * 6 + (P("seq"),),
        out_specs=(placed,) * 3,
        check_vma=False,
    )
```

time: 116 us -> 89.8 us (0.77)
  waiting for transfers between devices: 48.5 us -> 29.7 us
  starting transfers between devices: 41.8 us -> 32.7 us
  Pallas kernels: 17.6 us -> 24.6 us
  local copies, waits for them, and re-layouts: 5.83 us -> 1.06 us
    ppermute x12, waiting for transfers between devices: 31.7 us -> 16.2 us  [along_row(): return lax.ppermute(value, AXES, pairs)]
    ppermute x4, starting transfers between devices: 22.8 us -> 15.6 us  [along_rows(): lax.ppermute(value, AXES, [(b, b + by) for b in range(total) if 0 <= b +...]
    pallas_call x6 -> x7, Pallas kernels: 15.8 us -> 22.8 us  [the longest x1 5.51 us: per_device(): kernel(begin_one, 'begin_one', [SMEM] + [VMEM] * 5, [(kv_shape, F32), dq_...]
    unnamed x15 -> x6, local copies, waits for them, and re-layouts: 5.83 us -> 1.06 us
    ppermute x4, waiting for transfers between devices: 16.8 us -> 13.4 us  [along_rows(): lax.ppermute(value, AXES, [(b, b + by) for b in range(total) if 0 <= b +...]
    ppermute x12, starting transfers between devices: 19 us -> 17.1 us  [along_row(): return lax.ppermute(value, AXES, pairs)]
  transfers between devices with their start and end apart: 16 -> 16, of which waited for: 10 -> 6; matrix products, arithmetic and copies ran while one was open for 0% -> 0% of each run, Pallas kernels for 8% -> 22%
where the time goes in v3:
time: 89.8 us; the launch traced here: 89.1 us
  starting transfers between devices  32.7 us (36%)
  waiting for transfers between devices  29.7 us (33%)
  Pallas kernels  24.6 us (27%)
  local copies, waits for them, and re-layouts  1.06 us (1%)
  between operations  0.96 us (1%)
    ppermute x12, starting transfers between devices, along_row(): return lax.ppermute(value, AXES, pairs)  17.1 us
    ppermute x12, waiting for transfers between devices, along_row(): return lax.ppermute(value, AXES, pairs)  16.2 us
    ppermute x4, starting transfers between devices, along_rows(): lax.ppermute(value, AXES, [(b, b + by) for b in range(total) if 0 <= b +...  15.6 us
    ppermute x4, waiting for transfers between devices, along_rows(): lax.ppermute(value, AXES, [(b, b + by) for b in range(total) if 0 <= b +...  13.4 us
    pallas_call x1, Pallas kernels, per_device(): kernel(begin_one, 'begin_one', [SMEM] + [VMEM] * 5, [(kv_shape, F32), dq_...  5.51 us
    pallas_call x1, Pallas kernels, per_device(): kernel(begin_own, 'begin_own', [SMEM] + [VMEM] * 4, [(kv_shape, F32), dq_...  5.03 us
    pallas_call x1, Pallas kernels, per_device(): kernel(pack_queries, 'pack_queries', [HBM] * 3 + [VMEM], [((PIECE, WIDE),...  4.82 us
    pallas_call x1, Pallas kernels, per_device(): kernel(finish_own, 'finish_own', [SMEM] + [VMEM] * 4, [(kv_shape, F32)] +...  3.07 us
  transfers between devices with their start and end apart: 16, of which 6 were waited for; matrix products, arithmetic and copies ran while one was open for 0% of the time, Pallas kernels for 22%

profile of v3, /device:TPU:34, one launch (start us, length us, event | category | flops | bytes accessed | tf_op | source)
XLA Modules:
  0.0 89.1 jit_solution(10634524615015553788)
XLA Ops:
  0.6 0.0 copy-start.1
  0.6 1.7 %pack_kv.1 = (bf16[128,256]{1,0:T(8,128)(2,1)}, bf16[128,256]{1,0:T(8,128)(2,1)}, bf16[128,256]{1,0:T(8,128)(2,1)}, bf16[128,256]{1,0:T(8,128)(2,1)}) custom-call(bf16[128,512]{1,0:T(8,128)(2,1)} %keys.1, bf16[128,512]{1,0:T(8,128)(2,1)} %values.1), custom_call_target="tpu_custom_call" | custom-call | tf_op jit(solution)/shard_map/pack_kv/pallas_call | solution.py:277
  2.3 0.0 copy-start.2
  2.3 1.7 %collective-permute-start = (bf16[128,256]{1,0:T(8,128)(2,1)}, bf16[128,256]{1,0:T(8,128)(2,1)S(1)}, u32[]{:S(2)}, u32[]{:S(2)}) collective-permute-start(bf16[128,256]{1,0:T(8,128)(2,1)} %get-tuple-element.38), channel_id=1, source_target_pairs={{0,1},{1,2},{2,3},{3,0},{4,5},{5,6},{6,7},{7,4},{8,9},{9,10},{10,1... | collective-permute-start | bytes 196616 | tf_op jit(solution)/shard_map/ppermute | solution.py:269
  4.0 2.9 %collective-permute-start.1 = (bf16[128,256]{1,0:T(8,128)(2,1)}, bf16[128,256]{1,0:T(8,128)(2,1)S(1)}, u32[]{:S(2)}, u32[]{:S(2)}) collective-permute-start(bf16[128,256]{1,0:T(8,128)(2,1)} %get-tuple-element.39), channel_id=1, source_target_pairs={{0,2},{1,3},{2,0},{3,1},{4,6},{5,7},{6,4},{7,5},{8,10},{9,11},{10,... | collective-permute-start | bytes 196616 | tf_op jit(solution)/shard_map/ppermute | solution.py:269
  6.9 1.3 %collective-permute-start.2 = (bf16[128,256]{1,0:T(8,128)(2,1)}, bf16[128,256]{1,0:T(8,128)(2,1)S(1)}, u32[]{:S(2)}, u32[]{:S(2)}) collective-permute-start(bf16[128,256]{1,0:T(8,128)(2,1)} %get-tuple-element.40), channel_id=1, source_target_pairs={{0,3},{1,0},{2,1},{3,2},{4,7},{5,4},{6,5},{7,6},{8,11},{9,8},{10,9... | collective-permute-start | bytes 196616 | tf_op jit(solution)/shard_map/ppermute | solution.py:269
  8.2 4.8 %pack_queries.1 = (bf16[272,1024]{1,0:T(8,128)(2,1)}, bf16[272,1024]{1,0:T(8,128)(2,1)}, bf16[272,1024]{1,0:T(8,128)(2,1)}, bf16[272,1024]{1,0:T(8,128)(2,1)}) custom-call(bf16[128,4096]{1,0:T(8,128)(2,1)} %queries.1, bf16[128,4096]{1,0:T(8,128)(2,1)} %outputs.1, bf16[128,4096]{1,0:T(8,128)(2,1)} %grads.1, bf16[32,128]{1,0:T(8,128)(2,1)} %bitcast.9), custom_call_target="tpu_custom_call" | custom-call | tf_op jit(solution)/shard_map/pack_queries/pallas_call | solution.py:286
  13.1 0.0 collective-permute-done
  13.1 0.0 collective-permute-done.1
  13.1 0.0 collective-permute-done.2
  13.1 0.8 collective-permute-start.4
  13.8 2.6 %collective-permute-start.5 = (bf16[272,1024]{1,0:T(8,128)(2,1)}, bf16[272,1024]{1,0:T(8,128)(2,1)S(1)}, u32[]{:S(2)}, u32[]{:S(2)}) collective-permute-start(bf16[272,1024]{1,0:T(8,128)(2,1)} %get-tuple-element.52), channel_id=1, source_target_pairs={{0,3},{1,0},{2,1},{3,2},{4,7},{5,4},{6,5},{7,6},{8,11},{9,8},{10,9... | collective-permute-start | bytes 1671176 | tf_op jit(solution)/shard_map/ppermute | solution.py:269
  16.4 0.0 collective-permute-start.3
  16.4 0.0 copy-done.2
  16.4 5.2 %collective-permute-start.7 = (bf16[4,128,256]{2,1,0:T(8,128)(2,1)S(1)}, bf16[4,128,256]{2,1,0:T(8,128)(2,1)S(1)}, u32[]{:S(2)}, u32[]{:S(2)}) collective-permute-start(bf16[4,128,256]{2,1,0:T(8,128)(2,1)S(1)} %pad_maximum_fusion.kv), channel_id=1, source_target_pairs={{0,4},{1,5},{2,6},{3,7},{4,8},{5,9},{6,10},{7,11},{8,12},{9,13},{1... | collective-permute-start | bytes 786440 | tf_op jit(solution)/shard_map/ppermute | solution.py:273
  21.6 6.4 %collective-permute-start.6 = (bf16[4,128,256]{2,1,0:T(8,128)(2,1)S(1)}, bf16[4,128,256]{2,1,0:T(8,128)(2,1)S(1)}, u32[]{:S(2)}, u32[]{:S(2)}) collective-permute-start(bf16[4,128,256]{2,1,0:T(8,128)(2,1)S(1)} %pad_maximum_fusion.kv), channel_id=1, source_target_pairs={{0,8},{1,9},{2,10},{3,11},{4,12},{5,13},{6,14},{7,15},{8,16},{9,17... | collective-permute-start | bytes 786440 | tf_op jit(solution)/shard_map/ppermute | solution.py:273
  28.0 12.0 %collective-permute-done.4.piece1 = bf16[272,1024]{1,0:T(8,128)(2,1)S(1)} collective-permute-done((bf16[272,1024]{1,0:T(8,128)(2,1)}, bf16[272,1024]{1,0:T(8,128)(2,1)S(1)}, u32[]{:S(2)}, u32[]{:S(2)}) %collective-permute-start.4) | collective-permute-done | bytes 557088 | tf_op jit(solution)/shard_map/ppermute | solution.py:269
  40.0 0.0 collective-permute-done.5.piece3
  40.0 0.0 copy-done.1
  40.1 0.0 copy-start
  40.1 1.1 %copy-done = bf16[272,1024]{1,0:T(8,128)(2,1)S(1)} copy-done((bf16[272,1024]{1,0:T(8,128)(2,1)S(1)}, bf16[272,1024]{1,0:T(8,128)(2,1)}, u32[]{:S(2)}) %copy-start) | copy-done | bytes 557080
  41.1 5.0 %begin_own.1 = (f32[4,128,256]{2,1,0:T(8,128)S(1)}, f32[4,128,1024]{2,1,0:T(8,128)S(1)}) custom-call(s32[16]{0:T(128)S(1)} %copy-done.1, bf16[272,1024]{1,0:T(8,128)(2,1)S(1)} %copy-done, bf16[272,1024]{1,0:T(8,128)(2,1)S(1)} %collective-permute-done.4.piece1, bf16[272,1024]{1,0:T(8,128)(2,1)S(1)} %collective-permute-done.5.piece3, ...), custom_call_target="tpu_custom_call" | custom-call | tf_op jit(solution)/shard_map/begin_own/pallas_call | solution.py:305
  46.1 0.0 collective-permute-done.7.kv.kv_one
  46.2 5.5 %begin_one.1 = (f32[4,128,256]{2,1,0:T(8,128)S(1)}, f32[4,128,1024]{2,1,0:T(8,128)S(1)}) custom-call(s32[16]{0:T(128)S(1)} %copy-done.1, bf16[272,1024]{1,0:T(8,128)(2,1)S(1)} %copy-done, bf16[272,1024]{1,0:T(8,128)(2,1)S(1)} %collective-permute-done.4.piece1, bf16[272,1024]{1,0:T(8,128)(2,1)S(1)} %collective-permute-done.5.piece3, ...), custom_call_target="tpu_custom_call" | custom-call | tf_op jit(solution)/shard_map/begin_one/pallas_call | solution.py:308
  51.7 0.0 collective-permute-done.6.kv_two
  51.7 0.0 collective-permute-done.3.piece2
  51.7 2.7 %finish_earlier.1 = (bf16[4,128,256]{2,1,0:T(8,128)(2,1)S(1)}, bf16[4,128,256]{2,1,0:T(8,128)(2,1)S(1)}, f32[4,128,1024]{2,1,0:T(8,128)S(1)}) custom-call(s32[16]{0:T(128)S(1)} %copy-done.1, bf16[272,1024]{1,0:T(8,128)(2,1)S(1)} %copy-done, bf16[272,1024]{1,0:T(8,128)(2,1)S(1)} %collective-permute-done.4.piece1, ...), custom_call_target="tpu_custom_call" | custom-call | tf_op jit(solution)/shard_map/finish_earlier/pallas_call | solution.py:311
  54.4 1.9 %collective-permute-start.11 = (bf16[4,128,256]{2,1,0:T(8,128)(2,1)S(1)}, bf16[4,128,256]{2,1,0:T(8,128)(2,1)S(1)}, u32[]{:S(2)}, u32[]{:S(2)}) collective-permute-start(bf16[4,128,256]{2,1,0:T(8,128)(2,1)S(1)} %get-tuple-element.63), channel_id=1, source_target_pairs={{4,0},{5,1},{6,2},{7,3},{8,4},{9,5},{10,6},{11,7},{12,8},{13,9},{1... | collective-permute-start | bytes 786440 | tf_op jit(solution)/shard_map/ppermute | solution.py:273
  56.3 2.1 %collective-permute-start.12 = (bf16[4,128,256]{2,1,0:T(8,128)(2,1)S(1)}, bf16[4,128,256]{2,1,0:T(8,128)(2,1)S(1)}, u32[]{:S(2)}, u32[]{:S(2)}) collective-permute-start(bf16[4,128,256]{2,1,0:T(8,128)(2,1)S(1)} %get-tuple-element.64), channel_id=1, source_target_pairs={{8,0},{9,1},{10,2},{11,3},{12,4},{13,5},{14,6},{15,7},{16,8},{17,9... | collective-permute-start | bytes 786440 | tf_op jit(solution)/shard_map/ppermute | solution.py:273
  58.4 3.1 %finish_own.1 = (f32[4,128,256]{2,1,0:T(8,128)S(1)}, bf16[128,1024]{1,0:T(8,128)(2,1)S(1)}, bf16[128,1024]{1,0:T(8,128)(2,1)S(1)}, bf16[128,1024]{1,0:T(8,128)(2,1)S(1)}, bf16[128,1024]{1,0:T(8,128)(2,1)S(1)}) custom-call(s32[16]{0:T(128)S(1)} %copy-done.1, bf16[272,1024]{1,0:T(8,128)(2,1)S(1)} %collective-permute-done.3.piece2, ...), custom_call_target="tpu_custom_call" | custom-call | tf_op jit(solution)/shard_map/finish_own/pallas_call | solution.py:320
  61.5 3.0 %collective-permute-start.8 = (bf16[128,1024]{1,0:T(8,128)(2,1)S(1)}, bf16[128,1024]{1,0:T(8,128)(2,1)S(1)}, u32[]{:S(2)}, u32[]{:S(2)}) collective-permute-start(bf16[128,1024]{1,0:T(8,128)(2,1)S(1)} %get-tuple-element.59), channel_id=1, source_target_pairs={{0,3},{1,0},{2,1},{3,2},{4,7},{5,4},{6,5},{7,6},{8,11},{9,8},{10,9... | collective-permute-start | bytes 786440 | tf_op jit(solution)/shard_map/ppermute | solution.py:269
  64.5 0.0 collective-permute-start.9
  64.5 1.0 %collective-permute-start.10 = (bf16[128,1024]{1,0:T(8,128)(2,1)S(1)}, bf16[128,1024]{1,0:T(8,128)(2,1)S(1)}, u32[]{:S(2)}, u32[]{:S(2)}) collective-permute-start(bf16[128,1024]{1,0:T(8,128)(2,1)S(1)} %get-tuple-element.61), channel_id=1, source_target_pairs={{0,1},{1,2},{2,3},{3,0},{4,5},{5,6},{6,7},{7,4},{8,9},{9,10},{10,1... | collective-permute-start | bytes 786440 | tf_op jit(solution)/shard_map/ppermute | solution.py:269
  65.5 2.3 %collective-permute-done.11.one = bf16[4,128,256]{2,1,0:T(8,128)(2,1)S(1)} collective-permute-done((bf16[4,128,256]{2,1,0:T(8,128)(2,1)S(1)}, bf16[4,128,256]{2,1,0:T(8,128)(2,1)S(1)}, u32[]{:S(2)}, u32[]{:S(2)}) %collective-permute-start.11) | collective-permute-done | bytes 262176 | tf_op jit(solution)/shard_map/ppermute | solution.py:273
  67.8 11.2 %collective-permute-done.12.two = bf16[4,128,256]{2,1,0:T(8,128)(2,1)S(1)} collective-permute-done((bf16[4,128,256]{2,1,0:T(8,128)(2,1)S(1)}, bf16[4,128,256]{2,1,0:T(8,128)(2,1)S(1)}, u32[]{:S(2)}, u32[]{:S(2)}) %collective-permute-start.12) | collective-permute-done | bytes 262176 | tf_op jit(solution)/shard_map/ppermute | solution.py:273
  78.9 0.1 add_up.1
  79.0 3.0 %collective-permute-start.13 = (bf16[128,256]{1,0:T(8,128)(2,1)S(1)}, bf16[128,256]{1,0:T(8,128)(2,1)S(1)}, u32[]{:S(2)}, u32[]{:S(2)}) collective-permute-start(bf16[128,256]{1,0:T(8,128)(2,1)S(1)} %get-tuple-element.66), channel_id=1, source_target_pairs={{0,3},{1,0},{2,1},{3,2},{4,7},{5,4},{6,5},{7,6},{8,11},{9,8},{10,9... | collective-permute-start | bytes 196616 | tf_op jit(solution)/shard_map/ppermute | solution.py:269
  82.0 0.0 collective-permute-start.14
  82.0 0.0 collective-permute-done.8.piece1
  82.0 1.0 %collective-permute-start.15 = (bf16[128,256]{1,0:T(8,128)(2,1)S(1)}, bf16[128,256]{1,0:T(8,128)(2,1)S(1)}, u32[]{:S(2)}, u32[]{:S(2)}) collective-permute-start(bf16[128,256]{1,0:T(8,128)(2,1)S(1)} %get-tuple-element.68), channel_id=1, source_target_pairs={{0,1},{1,2},{2,3},{3,0},{4,5},{5,6},{6,7},{7,4},{8,9},{9,10},{10,1... | collective-permute-start | bytes 196616 | tf_op jit(solution)/shard_map/ppermute | solution.py:269
  82.9 0.0 collective-permute-done.9.piece2
  82.9 0.0 collective-permute-done.10.piece3
  82.9 1.0 %join_queries.1 = bf16[128,4096]{1,0:T(8,128)(2,1)} custom-call(bf16[128,1024]{1,0:T(8,128)(2,1)S(1)} %get-tuple-element.58.piece0, bf16[128,1024]{1,0:T(8,128)(2,1)S(1)} %collective-permute-done.8.piece1, bf16[128,1024]{1,0:T(8,128)(2,1)S(1)} %collective-permute-done.9.piece2, bf16[128,1024]{1,0:T(8,128)(2,1)S(1)} %collective-permute-done.10.piece3), custom_call_target="tpu_custom_call" | custom-call | tf_op jit(solution)/shard_map/join_queries/pallas_call | solution.py:332
  84.0 0.5 collective-permute-done.13.piece1
  84.5 3.4 %collective-permute-done.14.piece2 = bf16[128,256]{1,0:T(8,128)(2,1)S(1)} collective-permute-done((bf16[128,256]{1,0:T(8,128)(2,1)S(1)}, bf16[128,256]{1,0:T(8,128)(2,1)S(1)}, u32[]{:S(2)}, u32[]{:S(2)}) %collective-permute-start.14) | collective-permute-done | bytes 65568 | tf_op jit(solution)/shard_map/ppermute | solution.py:269
  87.9 0.3 collective-permute-done.15.piece3
  88.2 0.8 join_kv.1
  (1 shorter events, 0.0 us)
Async XLA Ops:
  0.6 39.4 %copy-start.1 = (s32[16]{0:T(128)S(1)}, s32[16]{0:T(128)}, u32[]{:S(2)}) copy-start(s32[16]{0:T(128)} %doc_start.7) | copy-start | bytes 196
  2.3 14.1 %copy-start.2 = (bf16[128,256]{1,0:T(8,128)(2,1)S(1)}, bf16[128,256]{1,0:T(8,128)(2,1)}, u32[]{:S(2)}) copy-start(bf16[128,256]{1,0:T(8,128)(2,1)} %get-tuple-element.46) | copy-start | bytes 196612
  2.3 10.7 %collective-permute-start = (bf16[128,256]{1,0:T(8,128)(2,1)}, bf16[128,256]{1,0:T(8,128)(2,1)S(1)}, u32[]{:S(2)}, u32[]{:S(2)}) collective-permute-start(bf16[128,256]{1,0:T(8,128)(2,1)} %get-tuple-element.38), channel_id=1, source_target_pairs={{0,1},{1,2},{2,3},{3,0},{4,5},{5,6},{6,7},{7,4},{8,9},{9,10},{10,1... | collective-permute-start | bytes 196616 | tf_op jit(solution)/shard_map/ppermute | solution.py:269
  4.0 9.1 %collective-permute-start.1 = (bf16[128,256]{1,0:T(8,128)(2,1)}, bf16[128,256]{1,0:T(8,128)(2,1)S(1)}, u32[]{:S(2)}, u32[]{:S(2)}) collective-permute-start(bf16[128,256]{1,0:T(8,128)(2,1)} %get-tuple-element.39), channel_id=1, source_target_pairs={{0,2},{1,3},{2,0},{3,1},{4,6},{5,7},{6,4},{7,5},{8,10},{9,11},{10,... | collective-permute-start | bytes 196616 | tf_op jit(solution)/shard_map/ppermute | solution.py:269
  6.9 6.2 %collective-permute-start.2 = (bf16[128,256]{1,0:T(8,128)(2,1)}, bf16[128,256]{1,0:T(8,128)(2,1)S(1)}, u32[]{:S(2)}, u32[]{:S(2)}) collective-permute-start(bf16[128,256]{1,0:T(8,128)(2,1)} %get-tuple-element.40), channel_id=1, source_target_pairs={{0,3},{1,0},{2,1},{3,2},{4,7},{5,4},{6,5},{7,6},{8,11},{9,8},{10,9... | collective-permute-start | bytes 196616 | tf_op jit(solution)/shard_map/ppermute | solution.py:269
  13.1 27.0 %collective-permute-start.4 = (bf16[272,1024]{1,0:T(8,128)(2,1)}, bf16[272,1024]{1,0:T(8,128)(2,1)S(1)}, u32[]{:S(2)}, u32[]{:S(2)}) collective-permute-start(bf16[272,1024]{1,0:T(8,128)(2,1)} %get-tuple-element.51), channel_id=1, source_target_pairs={{0,1},{1,2},{2,3},{3,0},{4,5},{5,6},{6,7},{7,4},{8,9},{9,10},{10,1... | collective-permute-start | bytes 1671176 | tf_op jit(solution)/shard_map/ppermute | solution.py:269
  13.8 26.2 %collective-permute-start.5 = (bf16[272,1024]{1,0:T(8,128)(2,1)}, bf16[272,1024]{1,0:T(8,128)(2,1)S(1)}, u32[]{:S(2)}, u32[]{:S(2)}) collective-permute-start(bf16[272,1024]{1,0:T(8,128)(2,1)} %get-tuple-element.52), channel_id=1, source_target_pairs={{0,3},{1,0},{2,1},{3,2},{4,7},{5,4},{6,5},{7,6},{8,11},{9,8},{10,9... | collective-permute-start | bytes 1671176 | tf_op jit(solution)/shard_map/ppermute | solution.py:269
  16.4 35.3 %collective-permute-start.3 = (bf16[272,1024]{1,0:T(8,128)(2,1)}, bf16[272,1024]{1,0:T(8,128)(2,1)S(1)}, u32[]{:S(2)}, u32[]{:S(2)}) collective-permute-start(bf16[272,1024]{1,0:T(8,128)(2,1)} %get-tuple-element.45), channel_id=1, source_target_pairs={{0,2},{1,3},{2,0},{3,1},{4,6},{5,7},{6,4},{7,5},{8,10},{9,11},{10,... | collective-permute-start | bytes 1671176 | tf_op jit(solution)/shard_map/ppermute | solution.py:269
  16.4 29.7 %collective-permute-start.7 = (bf16[4,128,256]{2,1,0:T(8,128)(2,1)S(1)}, bf16[4,128,256]{2,1,0:T(8,128)(2,1)S(1)}, u32[]{:S(2)}, u32[]{:S(2)}) collective-permute-start(bf16[4,128,256]{2,1,0:T(8,128)(2,1)S(1)} %pad_maximum_fusion.kv), channel_id=1, source_target_pairs={{0,4},{1,5},{2,6},{3,7},{4,8},{5,9},{6,10},{7,11},{8,12},{9,13},{1... | collective-permute-start | bytes 786440 | tf_op jit(solution)/shard_map/ppermute | solution.py:273
  21.6 30.0 %collective-permute-start.6 = (bf16[4,128,256]{2,1,0:T(8,128)(2,1)S(1)}, bf16[4,128,256]{2,1,0:T(8,128)(2,1)S(1)}, u32[]{:S(2)}, u32[]{:S(2)}) collective-permute-start(bf16[4,128,256]{2,1,0:T(8,128)(2,1)S(1)} %pad_maximum_fusion.kv), channel_id=1, source_target_pairs={{0,8},{1,9},{2,10},{3,11},{4,12},{5,13},{6,14},{7,15},{8,16},{9,17... | collective-permute-start | bytes 786440 | tf_op jit(solution)/shard_map/ppermute | solution.py:273
  40.1 1.1 %copy-start = (bf16[272,1024]{1,0:T(8,128)(2,1)S(1)}, bf16[272,1024]{1,0:T(8,128)(2,1)}, u32[]{:S(2)}) copy-start(bf16[272,1024]{1,0:T(8,128)(2,1)} %get-tuple-element.50.piece0) | copy-start | bytes 1671172
  54.4 13.4 %collective-permute-start.11 = (bf16[4,128,256]{2,1,0:T(8,128)(2,1)S(1)}, bf16[4,128,256]{2,1,0:T(8,128)(2,1)S(1)}, u32[]{:S(2)}, u32[]{:S(2)}) collective-permute-start(bf16[4,128,256]{2,1,0:T(8,128)(2,1)S(1)} %get-tuple-element.63), channel_id=1, source_target_pairs={{4,0},{5,1},{6,2},{7,3},{8,4},{9,5},{10,6},{11,7},{12,8},{13,9},{1... | collective-permute-start | bytes 786440 | tf_op jit(solution)/shard_map/ppermute | solution.py:273
  56.3 22.6 %collective-permute-start.12 = (bf16[4,128,256]{2,1,0:T(8,128)(2,1)S(1)}, bf16[4,128,256]{2,1,0:T(8,128)(2,1)S(1)}, u32[]{:S(2)}, u32[]{:S(2)}) collective-permute-start(bf16[4,128,256]{2,1,0:T(8,128)(2,1)S(1)} %get-tuple-element.64), channel_id=1, source_target_pairs={{8,0},{9,1},{10,2},{11,3},{12,4},{13,5},{14,6},{15,7},{16,8},{17,9... | collective-permute-start | bytes 786440 | tf_op jit(solution)/shard_map/ppermute | solution.py:273
  61.5 20.5 %collective-permute-start.8 = (bf16[128,1024]{1,0:T(8,128)(2,1)S(1)}, bf16[128,1024]{1,0:T(8,128)(2,1)S(1)}, u32[]{:S(2)}, u32[]{:S(2)}) collective-permute-start(bf16[128,1024]{1,0:T(8,128)(2,1)S(1)} %get-tuple-element.59), channel_id=1, source_target_pairs={{0,3},{1,0},{2,1},{3,2},{4,7},{5,4},{6,5},{7,6},{8,11},{9,8},{10,9... | collective-permute-start | bytes 786440 | tf_op jit(solution)/shard_map/ppermute | solution.py:269
  64.5 18.4 %collective-permute-start.9 = (bf16[128,1024]{1,0:T(8,128)(2,1)S(1)}, bf16[128,1024]{1,0:T(8,128)(2,1)S(1)}, u32[]{:S(2)}, u32[]{:S(2)}) collective-permute-start(bf16[128,1024]{1,0:T(8,128)(2,1)S(1)} %get-tuple-element.60), channel_id=1, source_target_pairs={{0,2},{1,3},{2,0},{3,1},{4,6},{5,7},{6,4},{7,5},{8,10},{9,11},{10,... | collective-permute-start | bytes 786440 | tf_op jit(solution)/shard_map/ppermute | solution.py:269
  64.5 18.4 %collective-permute-start.10 = (bf16[128,1024]{1,0:T(8,128)(2,1)S(1)}, bf16[128,1024]{1,0:T(8,128)(2,1)S(1)}, u32[]{:S(2)}, u32[]{:S(2)}) collective-permute-start(bf16[128,1024]{1,0:T(8,128)(2,1)S(1)} %get-tuple-element.61), channel_id=1, source_target_pairs={{0,1},{1,2},{2,3},{3,0},{4,5},{5,6},{6,7},{7,4},{8,9},{9,10},{10,1... | collective-permute-start | bytes 786440 | tf_op jit(solution)/shard_map/ppermute | solution.py:269
  79.0 5.5 %collective-permute-start.13 = (bf16[128,256]{1,0:T(8,128)(2,1)S(1)}, bf16[128,256]{1,0:T(8,128)(2,1)S(1)}, u32[]{:S(2)}, u32[]{:S(2)}) collective-permute-start(bf16[128,256]{1,0:T(8,128)(2,1)S(1)} %get-tuple-element.66), channel_id=1, source_target_pairs={{0,3},{1,0},{2,1},{3,2},{4,7},{5,4},{6,5},{7,6},{8,11},{9,8},{10,9... | collective-permute-start | bytes 196616 | tf_op jit(solution)/shard_map/ppermute | solution.py:269
  82.0 5.9 %collective-permute-start.14 = (bf16[128,256]{1,0:T(8,128)(2,1)S(1)}, bf16[128,256]{1,0:T(8,128)(2,1)S(1)}, u32[]{:S(2)}, u32[]{:S(2)}) collective-permute-start(bf16[128,256]{1,0:T(8,128)(2,1)S(1)} %get-tuple-element.67), channel_id=1, source_target_pairs={{0,2},{1,3},{2,0},{3,1},{4,6},{5,7},{6,4},{7,5},{8,10},{9,11},{10,... | collective-permute-start | bytes 196616 | tf_op jit(solution)/shard_map/ppermute | solution.py:269
  82.0 6.2 %collective-permute-start.15 = (bf16[128,256]{1,0:T(8,128)(2,1)S(1)}, bf16[128,256]{1,0:T(8,128)(2,1)S(1)}, u32[]{:S(2)}, u32[]{:S(2)}) collective-permute-start(bf16[128,256]{1,0:T(8,128)(2,1)S(1)} %get-tuple-element.68), channel_id=1, source_target_pairs={{0,1},{1,2},{2,3},{3,0},{4,5},{5,6},{6,7},{7,4},{8,9},{9,10},{10,1... | collective-permute-start | bytes 196616 | tf_op jit(solution)/shard_map/ppermute | solution.py:269

commit v4 on v3

--- a/solution.py
+++ b/solution.py
@@ -32,34 +32,24 @@
     return jnp.dot(left, right, preferred_element_type=F32)
 
 
-def pack_kv(keys, values, piece0, piece1, piece2, piece3, sems):
-    place = lax.rem(lax.axis_index("head"), ROW)
+def pack(
+    queries, outputs, grads, norms, keys, values,
+    kv0, kv1, kv2, kv3, piece0, piece1, piece2, piece3, held, sems,
+):
+    place = lax.rem(lax.axis_index("head"), ROW)
+    pieces = (piece0, piece1, piece2, piece3)
+    early = []
     copies = []
-    for shift, piece in enumerate((piece0, piece1, piece2, piece3)):
-        columns = pl.ds(pl.multiple_of(lax.rem(place + shift, ROW) * DH, DH), DH)
-        for part, source in enumerate((keys, values)):
-            copies.append(
-                pltpu.make_async_copy(
-                    source.at[:, columns],
-                    piece.at[:, pl.ds(part * DH, DH)],
-                    sems.at[shift, part],
-                )
-            )
-    for copy in copies:
-        copy.start()
-    for copy in copies:
-        copy.wait()
-
-
-def pack_queries(
-    queries, outputs, grads, norms, piece0, piece1, piece2, piece3, held, sems
-):
-    place = lax.rem(lax.axis_index("head"), ROW)
-    pieces = (piece0, piece1, piece2, piece3)
-    copies = []
-    for shift, piece in enumerate(pieces):
+    for shift, (piece, kv) in enumerate(zip(pieces, (kv0, kv1, kv2, kv3))):
         group = lax.rem(place + shift, ROW)
         span = pl.ds(pl.multiple_of(group * WIDE, WIDE), WIDE)
+        columns = pl.ds(pl.multiple_of(group * DH, DH), DH)
+        for part, (source, target) in enumerate(
+            ((keys, kv.at[:, pl.ds(0, DH)]), (values, kv.at[:, pl.ds(DH, DH)]))
+        ):
+            early.append(
+                pltpu.make_async_copy(source.at[:, columns], target, sems.at[shift, 3 + part])
+            )
         copies.append(
             [
                 pltpu.make_async_copy(source.at[:, span], target, sems.at[shift, part])
@@ -72,9 +62,11 @@
                 )
             ]
         )
-    for copy in copies:
-        for part in copy:
-            part.start()
+    for part in range(3):
+        for copy in copies:
+            copy[part].start()
+    for copy in early:
+        copy.start()
     turned = norms[...].astype(F32)
     ones = jnp.ones((16, DH), BF16)
     row_id = lax.broadcasted_iota(jnp.int32, (16, BLOCK), 0)
@@ -103,6 +95,20 @@
             piece[STAT:, cut] = stats.astype(BF16)
     for copy in copies:
         copy[2].wait()
+    for copy in early:
+        copy.wait()
+
+
+def in_order(piece0, piece1, piece2, piece3, all_out, late_out):
+    place = lax.rem(lax.axis_index("head"), ROW)
+    for block in range(ROW):
+        shift = lax.rem(place + ROW - block, ROW)
+        value = piece0[...]
+        for number, piece in enumerate((piece1, piece2, piece3)):
+            value = jnp.where(shift == number + 1, piece[...], value)
+        all_out[block] = value
+        if block > 0:
+            late_out[block - 1] = value
 
 
 def stacked(piece, start):
@@ -121,7 +127,7 @@
         start = doc_start[own_row * ROW + query_place]
 
         def turn(key_slot, carry, slot=slot, piece=piece, start=start, query_place=query_place):
-            key_place = lax.rem(place + ROW - key_slot, ROW)
+            key_place = key_slot + (1 if back == 2 else 0)
             seen = first_key + key_place >= start
             if back == 0:
                 seen = seen & (key_place <= query_place)
@@ -148,7 +154,7 @@
 
             return carry
 
-        lax.fori_loop(0, ROW, turn, 0)
+        lax.fori_loop(0, ROW - 1 if back == 2 else ROW, turn, 0)
 
 
 def begin_own(doc_start, piece0, piece1, piece3, kv, dkv, dq):
@@ -172,14 +178,14 @@
 
 def finish_earlier(
     doc_start, piece0, piece1, piece2, piece3, kv_two, kv_one, dkv_in, dq_in,
-    two_out, one_out, dq, dkv,
+    two_out, one_out, dq, dkv_two, dkv,
 ):
     for slot in (0, 1, 3):
         dq[slot] = dq_in[slot]
     dq[2] = jnp.zeros((DH, WIDE), F32)
-    dkv[...] = jnp.zeros_like(dkv)
-    sweep(2, doc_start, {0: piece0, 1: piece1, 2: piece2, 3: piece3}, kv_two, dq, dkv)
-    round_kv(dkv, two_out)
+    dkv_two[...] = jnp.zeros_like(dkv_two)
+    sweep(2, doc_start, {0: piece0, 1: piece1, 2: piece2, 3: piece3}, kv_two, dq, dkv_two)
+    round_kv(dkv_two, two_out)
     dkv[...] = dkv_in[...]
     sweep(1, doc_start, {2: piece2}, kv_one, dq, dkv)
     round_kv(dkv, one_out)
@@ -209,10 +215,11 @@
 
 
 def add_up(own, one, two, *pieces):
+    place = lax.rem(lax.axis_index("head"), ROW)
     for slot in range(ROW):
-        pieces[slot][...] = (
-            own[slot] + one[slot].astype(F32) + two[slot].astype(F32)
-        ).astype(BF16)
+        block = lax.rem(place + ROW - slot, ROW)
+        earlier = jnp.where(block > 0, two[jnp.maximum(block - 1, 0)].astype(F32), 0.0)
+        pieces[slot][...] = (own[block] + one[block].astype(F32) + earlier).astype(BF16)
 
 
 def join_queries(piece0, piece1, piece2, piece3, out, sems):
@@ -244,7 +251,7 @@
         copy.wait()
 
 
-def kernel(body, name, in_specs, shapes, scratch=(), out_spec=VMEM, grant=24):
+def kernel(body, name, in_specs, shapes, scratch=(), out_spec=VMEM, grant=24, cost=200_000_000_000):
     return pl.pallas_call(
         body,
         in_specs=in_specs,
@@ -252,6 +259,7 @@
         out_shape=[jax.ShapeDtypeStruct(*shape) for shape in shapes],
         scratch_shapes=scratch,
         compiler_params=pltpu.CompilerParams(vmem_limit_bytes=grant << 20),
+        cost_estimate=pl.CostEstimate(flops=cost, bytes_accessed=cost, transcendentals=0),
         name=name,
     )
 
@@ -274,34 +282,30 @@
             value, AXES, [(b, b + by) for b in range(total) if 0 <= b + by < total]
         )
 
-    kv_sent = kernel(
-        pack_kv,
-        "pack_kv",
-        [HBM] * 2,
-        [((BLOCK, 2 * DH), BF16)] * ROW,
-        [sems((ROW, 2))],
-        grant=56,
-    )(keys, values)
-    kv_pieces = [along_row(kv_sent[shift], shift) for shift in range(ROW)]
-    sent = kernel(
-        pack_queries,
-        "pack_queries",
-        [HBM] * 3 + [VMEM],
-        [((PIECE, WIDE), BF16)] * ROW,
-        [pltpu.VMEM((ROW, BLOCK, WIDE), BF16), sems((ROW, 3))],
-        grant=56,
-    )(queries, outputs, out_grads, log_norms.T)
-    kv_pieces, sent = lax.optimization_barrier((kv_pieces, sent))
+    kv_shape = (ROW, BLOCK, 2 * DH)
+    late_shape = (ROW - 1, BLOCK, 2 * DH)
+    packed = kernel(
+        pack,
+        "pack",
+        [HBM] * 3 + [VMEM] + [HBM] * 2,
+        [((BLOCK, 2 * DH), BF16)] * ROW + [((PIECE, WIDE), BF16)] * ROW,
+        [pltpu.VMEM((ROW, BLOCK, WIDE), BF16), sems((ROW, 5))],
+        grant=52,
+    )(queries, outputs, out_grads, log_norms.T, keys, values)
+    kv_pieces = [along_row(packed[shift], shift) for shift in range(ROW)]
+    kv_pieces, sent = lax.optimization_barrier((kv_pieces, packed[ROW:]))
     piece0 = sent[0]
     piece1 = along_row(sent[1], 1)
     piece3 = along_row(sent[3], 3)
-    kv_own = jnp.stack(kv_pieces)
-    kv_two = along_rows(kv_own, 2)
+    kv_own, kv_late = kernel(
+        in_order, "in_order", [VMEM] * ROW, [(kv_shape, BF16), (late_shape, BF16)]
+    )(*kv_pieces)
     kv_one = along_rows(kv_own, 1)
-    piece2 = along_row(sent[2], 2)
+    kv_two = along_rows(kv_late, 2)
+    piece1, piece3, far = lax.optimization_barrier((piece1, piece3, sent[2]))
+    piece2 = along_row(far, 2)
 
     dq_shape = ((ROW, DH, WIDE), F32)
-    kv_shape = (ROW, BLOCK, 2 * DH)
     dkv_own, dq = kernel(
         begin_own, "begin_own", [SMEM] + [VMEM] * 4, [(kv_shape, F32), dq_shape]
     )(doc_start, piece0, piece1, piece3, kv_own)
@@ -312,8 +316,8 @@
         finish_earlier,
         "finish_earlier",
         [SMEM] + [VMEM] * 8,
-        [(kv_shape, BF16), (kv_shape, BF16), dq_shape],
-        [pltpu.VMEM(kv_shape, F32)],
+        [(late_shape, BF16), (kv_shape, BF16), dq_shape],
+        [pltpu.VMEM(late_shape, F32), pltpu.VMEM(kv_shape, F32)],
     )(doc_start, piece0, piece1, piece2, piece3, kv_two, kv_one, dkv_one, dq)
     back_two = along_rows(dkv_two, -2)
     back_one = along_rows(dkv_one, -1)
@@ -325,10 +329,6 @@
         [pltpu.VMEM((1, DH, WIDE), F32)],
     )(doc_start, piece2, kv_own, dkv_own, dq)
     dq_pieces = [along_row(dq_sent[slot], -slot) for slot in range(ROW)]
-    dkv_sent = kernel(add_up, "add_up", [VMEM] * 3, [((BLOCK, 2 * DH), BF16)] * ROW)(
-        dkv_own, back_one, back_two
-    )
-    dkv_pieces = [along_row(dkv_sent[slot], -slot) for slot in range(ROW)]
     (query_out,) = kernel(
         join_queries,
         "join_queries",
@@ -337,6 +337,10 @@
         [sems((ROW,))],
         HBM,
     )(*dq_pieces)
+    dkv_sent = kernel(add_up, "add_up", [VMEM] * 3, [((BLOCK, 2 * DH), BF16)] * ROW)(
+        dkv_own, back_one, back_two
+    )
+    dkv_pieces = [along_row(dkv_sent[slot], -slot) for slot in range(ROW)]
     key_out, value_out = kernel(
         join_kv,
         "join_kv",

time: 89.8 us -> 95.6 us (1.065)
  the two profiles are of different devices: /device:TPU:34 before, /device:TPU:67 now
where the time goes in v4:
time: 95.6 us; the launch traced here: 95.9 us
  starting transfers between devices  37.6 us (39%)
  waiting for transfers between devices  31.1 us (33%)
  Pallas kernels  23.8 us (25%)
  local copies, waits for them, and re-layouts  2.5 us (3%)
    ppermute x4, starting transfers between devices, along_rows(): lax.ppermute(value, AXES, [(b, b + by) for b in range(total) if 0 <= b +...  25 us
    ppermute x4, waiting for transfers between devices, along_rows(): lax.ppermute(value, AXES, [(b, b + by) for b in range(total) if 0 <= b +...  24.6 us
    ppermute x12, starting transfers between devices, along_row(): return lax.ppermute(value, AXES, pairs)  12.7 us
    ppermute x12, waiting for transfers between devices, along_row(): return lax.ppermute(value, AXES, pairs)  6.46 us
    pallas_call x1, Pallas kernels, per_device(): kernel(begin_own, 'begin_own', [SMEM] + [VMEM] * 4, [(kv_shape, F32), dq_...  4.59 us
    pallas_call x1, Pallas kernels, per_device(): kernel(pack, 'pack', [HBM] * 3 + [VMEM] + [HBM] * 2, [((BLOCK, 2 * DH), B...  4.28 us
    pallas_call x1, Pallas kernels, per_device(): kernel(finish_own, 'finish_own', [SMEM] + [VMEM] * 4, [(kv_shape, F32)] +...  3.77 us
    pallas_call x1, Pallas kernels, per_device(): kernel(finish_earlier, 'finish_earlier', [SMEM] + [VMEM] * 8, [(late_shap...  2.72 us
  transfers between devices with their start and end apart: 16, of which 7 were waited for; matrix products, arithmetic and copies ran while one was open for 0% of the time, Pallas kernels for 16%

profile of v4, /device:TPU:67, one launch (start us, length us, event | category | flops | bytes accessed | tf_op | source)
XLA Modules:
  0.0 95.9 jit_solution(6889589835507732335)
XLA Ops:
  0.6 0.0 copy-start
  0.6 0.9 copy-done
  1.5 0.0 copy-start.1
  1.5 0.9 copy-done.1
  2.4 0.0 copy-start.2
  2.4 0.7 copy-done.2
  3.1 4.3 %pack.1 = (bf16[128,256]{1,0:T(8,128)(2,1)S(1)}, bf16[128,256]{1,0:T(8,128)(2,1)S(1)}, bf16[128,256]{1,0:T(8,128)(2,1)S(1)}, bf16[128,256]{1,0:T(8,128)(2,1)S(1)...) custom-call(bf16[128,4096]{1,0:T(8,128)(2,1)} %queries.1, ...), custom_call_target="tpu_custom_call" | custom-call | flops 199999995904 | bytes 199999995904 | tf_op jit(solution)/shard_map/pack/pallas_call | solution.py:287
  7.4 1.4 %collective-permute-start = (bf16[128,256]{1,0:T(8,128)(2,1)S(1)}, bf16[128,256]{1,0:T(8,128)(2,1)S(1)}, u32[]{:S(2)}, u32[]{:S(2)}) collective-permute-start(bf16[128,256]{1,0:T(8,128)(2,1)S(1)} %get-tuple-element.43), channel_id=1, source_target_pairs={{0,1},{1,2},{2,3},{3,0},{4,5},{5,6},{6,7},{7,4},{8,9},{9,10},{10,1... | collective-permute-start | bytes 196616 | tf_op jit(solution)/shard_map/ppermute | solution.py:277
  8.8 2.6 %collective-permute-start.1 = (bf16[128,256]{1,0:T(8,128)(2,1)S(1)}, bf16[128,256]{1,0:T(8,128)(2,1)S(1)}, u32[]{:S(2)}, u32[]{:S(2)}) collective-permute-start(bf16[128,256]{1,0:T(8,128)(2,1)S(1)} %get-tuple-element.44), channel_id=1, source_target_pairs={{0,2},{1,3},{2,0},{3,1},{4,6},{5,7},{6,4},{7,5},{8,10},{9,11},{10,... | collective-permute-start | bytes 196616 | tf_op jit(solution)/shard_map/ppermute | solution.py:277
  11.4 1.1 %collective-permute-start.2 = (bf16[128,256]{1,0:T(8,128)(2,1)S(1)}, bf16[128,256]{1,0:T(8,128)(2,1)S(1)}, u32[]{:S(2)}, u32[]{:S(2)}) collective-permute-start(bf16[128,256]{1,0:T(8,128)(2,1)S(1)} %get-tuple-element.45), channel_id=1, source_target_pairs={{0,3},{1,0},{2,1},{3,2},{4,7},{5,4},{6,5},{7,6},{8,11},{9,8},{10,9... | collective-permute-start | bytes 196616 | tf_op jit(solution)/shard_map/ppermute | solution.py:277
  12.5 0.0 collective-permute-done.piece1
  12.5 1.5 %collective-permute-done.1.piece2 = bf16[128,256]{1,0:T(8,128)(2,1)S(1)} collective-permute-done((bf16[128,256]{1,0:T(8,128)(2,1)S(1)}, bf16[128,256]{1,0:T(8,128)(2,1)S(1)}, u32[]{:S(2)}, u32[]{:S(2)}) %collective-permute-start.1) | collective-permute-done | bytes 65568 | tf_op jit(solution)/shard_map/ppermute | solution.py:277
  14.0 0.8 collective-permute-done.2.piece3
  14.8 0.0 collective-permute-start.3
  14.8 2.7 %collective-permute-start.4 = (bf16[272,1024]{1,0:T(8,128)(2,1)}, bf16[272,1024]{1,0:T(8,128)(2,1)}, u32[]{:S(2)}, u32[]{:S(2)}) collective-permute-start(bf16[272,1024]{1,0:T(8,128)(2,1)} %get-tuple-element.51), channel_id=1, source_target_pairs={{0,3},{1,0},{2,1},{3,2},{4,7},{5,4},{6,5},{7,6},{8,11},{9,8},{10,9... | collective-permute-start | bytes 1671176 | tf_op jit(solution)/shard_map/ppermute | solution.py:277
  17.5 0.8 in_order.1
  18.4 7.0 %collective-permute-start.6 = (bf16[3,128,256]{2,1,0:T(8,128)(2,1)}, bf16[3,128,256]{2,1,0:T(8,128)(2,1)}, u32[]{:S(2)}, u32[]{:S(2)}) collective-permute-start(bf16[3,128,256]{2,1,0:T(8,128)(2,1)} %get-tuple-element.63), channel_id=1, source_target_pairs={{0,8},{1,9},{2,10},{3,11},{4,12},{5,13},{6,14},{7,15},{8,16},{9,17... | collective-permute-start | bytes 589832 | tf_op jit(solution)/shard_map/ppermute | solution.py:281
  25.4 2.9 %collective-permute-start.7 = (bf16[4,128,256]{2,1,0:T(8,128)(2,1)}, bf16[4,128,256]{2,1,0:T(8,128)(2,1)}, u32[]{:S(2)}, u32[]{:S(2)}) collective-permute-start(bf16[4,128,256]{2,1,0:T(8,128)(2,1)} %get-tuple-element.58.kv), channel_id=1, source_target_pairs={{0,4},{1,5},{2,6},{3,7},{4,8},{5,9},{6,10},{7,11},{8,12},{9,13},{1... | collective-permute-start | bytes 786440 | tf_op jit(solution)/shard_map/ppermute | solution.py:281
  28.3 0.1 collective-permute-done.3.piece1
  28.4 0.0 collective-permute-done.4.piece3
  28.4 1.6 %collective-permute-start.5 = (bf16[272,1024]{1,0:T(8,128)(2,1)}, bf16[272,1024]{1,0:T(8,128)(2,1)}, u32[]{:S(2)}, u32[]{:S(2)}) collective-permute-start(bf16[272,1024]{1,0:T(8,128)(2,1)} %get-tuple-element.53), channel_id=1, source_target_pairs={{0,2},{1,3},{2,0},{3,1},{4,6},{5,7},{6,4},{7,5},{8,10},{9,11},{10,... | collective-permute-start | bytes 1671176 | tf_op jit(solution)/shard_map/ppermute | solution.py:277
  30.0 0.0 copy-done.3
  30.0 4.6 %begin_own.1 = (f32[4,128,256]{2,1,0:T(8,128)S(1)}, f32[4,128,1024]{2,1,0:T(8,128)S(1)}) custom-call(s32[16]{0:T(128)S(1)} %copy-done.3, bf16[272,1024]{1,0:T(8,128)(2,1)S(1)} %get-tuple-element.59.piece0, bf16[272,1024]{1,0:T(8,128)(2,1)} %collective-permute-done.3.piece1, bf16[272,1024]{1,0:T(8,128)(2,1)} %collective-permute-done.4.piece3, ...), custom_call_target="tpu_custom_call" | custom-call | flops 199999995904 | bytes 199999995904 | tf_op jit(solution)/shard_map/begin_own/pallas_call | solution.py:309
  34.6 7.7 %collective-permute-done.7.kv.kv_one = bf16[4,128,256]{2,1,0:T(8,128)(2,1)} collective-permute-done((bf16[4,128,256]{2,1,0:T(8,128)(2,1)}, bf16[4,128,256]{2,1,0:T(8,128)(2,1)}, u32[]{:S(2)}, u32[]{:S(2)}) %collective-permute-start.7) | collective-permute-done | bytes 262176 | tf_op jit(solution)/shard_map/ppermute | solution.py:281
  42.3 2.1 %begin_one.1 = (f32[4,128,256]{2,1,0:T(8,128)S(1)}, f32[4,128,1024]{2,1,0:T(8,128)S(1)}) custom-call(s32[16]{0:T(128)S(1)} %copy-done.3, bf16[272,1024]{1,0:T(8,128)(2,1)S(1)} %get-tuple-element.59.piece0, bf16[272,1024]{1,0:T(8,128)(2,1)} %collective-permute-done.3.piece1, bf16[272,1024]{1,0:T(8,128)(2,1)} %collective-permute-done.4.piece3, ...), custom_call_target="tpu_custom_call" | custom-call | flops 199999995904 | bytes 199999995904 | tf_op jit(solution)/shard_map/begin_one/pallas_call | solution.py:312
  44.3 0.0 collective-permute-done.6.kv_two
  44.4 0.0 collective-permute-done.5.piece2
  44.4 2.7 %finish_earlier.1 = (bf16[3,128,256]{2,1,0:T(8,128)(2,1)}, bf16[4,128,256]{2,1,0:T(8,128)(2,1)}, f32[4,128,1024]{2,1,0:T(8,128)S(1)}) custom-call(s32[16]{0:T(128)S(1)} %copy-done.3, bf16[272,1024]{1,0:T(8,128)(2,1)S(1)} %get-tuple-element.59.piece0, bf16[272,1024]{1,0:T(8,128)(2,1)} %collective-permute-done.3.piece1, ...), custom_call_target="tpu_custom_call" | custom-call | flops 199999995904 | bytes 199999995904 | tf_op jit(solution)/shard_map/finish_earlier/pallas_call | solution.py:315
  47.1 13.1 %collective-permute-start.12 = (bf16[3,128,256]{2,1,0:T(8,128)(2,1)}, bf16[3,128,256]{2,1,0:T(8,128)(2,1)}, u32[]{:S(2)}, u32[]{:S(2)}) collective-permute-start(bf16[3,128,256]{2,1,0:T(8,128)(2,1)} %get-tuple-element.74), channel_id=1, source_target_pairs={{8,0},{9,1},{10,2},{11,3},{12,4},{13,5},{14,6},{15,7},{16,8},{17,9... | collective-permute-start | bytes 589832 | tf_op jit(solution)/shard_map/ppermute | solution.py:281
  60.2 1.9 %collective-permute-start.11 = (bf16[4,128,256]{2,1,0:T(8,128)(2,1)}, bf16[4,128,256]{2,1,0:T(8,128)(2,1)}, u32[]{:S(2)}, u32[]{:S(2)}) collective-permute-start(bf16[4,128,256]{2,1,0:T(8,128)(2,1)} %get-tuple-element.73), channel_id=1, source_target_pairs={{4,0},{5,1},{6,2},{7,3},{8,4},{9,5},{10,6},{11,7},{12,8},{13,9},{1... | collective-permute-start | bytes 786440 | tf_op jit(solution)/shard_map/ppermute | solution.py:281
  62.1 3.8 %finish_own.1 = (f32[4,128,256]{2,1,0:T(8,128)S(1)}, bf16[128,1024]{1,0:T(8,128)(2,1)S(1)}, bf16[128,1024]{1,0:T(8,128)(2,1)}, bf16[128,1024]{1,0:T(8,128)(2,1)}, bf16[128,1024]{1,0:T(8,128)(2,1)}) custom-call(s32[16]{0:T(128)S(1)} %copy-done.3, bf16[272,1024]{1,0:T(8,128)(2,1)} %collective-permute-done.5.piece2, bf16[4,128,256]{2,1,0:T(8,128)(2,1)} %get-tuple-element.58.kv, ...), custom_call_target="tpu_custom_call" | custom-call | flops 199999995904 | bytes 199999995904 | tf_op jit(solution)/shard_map/finish_own/pallas_call | solution.py:324
  65.9 0.2 collective-permute-start.8
  66.1 1.7 %collective-permute-start.9 = (bf16[128,1024]{1,0:T(8,128)(2,1)}, bf16[128,1024]{1,0:T(8,128)(2,1)}, u32[]{:S(2)}, u32[]{:S(2)}) collective-permute-start(bf16[128,1024]{1,0:T(8,128)(2,1)} %get-tuple-element.70), channel_id=1, source_target_pairs={{0,2},{1,3},{2,0},{3,1},{4,6},{5,7},{6,4},{7,5},{8,10},{9,11},{10,... | collective-permute-start | bytes 786440 | tf_op jit(solution)/shard_map/ppermute | solution.py:277
  67.8 0.0 collective-permute-start.10
  67.8 0.0 collective-permute-done.12.two
  67.8 17.0 %collective-permute-done.11.one = bf16[4,128,256]{2,1,0:T(8,128)(2,1)} collective-permute-done((bf16[4,128,256]{2,1,0:T(8,128)(2,1)}, bf16[4,128,256]{2,1,0:T(8,128)(2,1)}, u32[]{:S(2)}, u32[]{:S(2)}) %collective-permute-start.11) | collective-permute-done | bytes 262176 | tf_op jit(solution)/shard_map/ppermute | solution.py:281
  84.8 1.7 %add_up.1 = (bf16[128,256]{1,0:T(8,128)(2,1)S(1)}, bf16[128,256]{1,0:T(8,128)(2,1)}, bf16[128,256]{1,0:T(8,128)(2,1)}, bf16[128,256]{1,0:T(8,128)(2,1)}) custom-call(f32[4,128,256]{2,1,0:T(8,128)S(1)} %get-tuple-element.72.own, bf16[4,128,256]{2,1,0:T(8,128)(2,1)} %collective-permute-done.11.one, bf16[3,128,256]{2,1,0:T(8,128)(2,1)} %collective-permute-done.12.two), custom_call_target="tpu_custom_call" | custom-call | flops 199999995904 | bytes 199999995904 | tf_op jit(solution)/shard_map/add_up/pallas_call | solution.py:340
  86.5 0.7 collective-permute-start.13
  87.2 0.0 collective-permute-start.14
  87.2 0.0 collective-permute-done.8.piece1
  87.2 0.7 collective-permute-start.15
  88.0 0.0 collective-permute-done.9.piece2
  88.0 0.0 collective-permute-done.10.piece3
  88.0 2.1 %join_queries.1 = bf16[128,4096]{1,0:T(8,128)(2,1)} custom-call(bf16[128,1024]{1,0:T(8,128)(2,1)S(1)} %get-tuple-element.68.piece0, bf16[128,1024]{1,0:T(8,128)(2,1)} %collective-permute-done.8.piece1, bf16[128,1024]{1,0:T(8,128)(2,1)} %collective-permute-done.9.piece2, bf16[128,1024]{1,0:T(8,128)(2,1)} %collective-permute-done.10.piece3), custom_call_target="tpu_custom_call" | custom-call | flops 199999995904 | bytes 199999995904 | tf_op jit(solution)/shard_map/join_queries/pallas_call | solution.py:332
  90.1 0.0 collective-permute-done.13.piece1
  90.1 2.1 %collective-permute-done.14.piece2 = bf16[128,256]{1,0:T(8,128)(2,1)} collective-permute-done((bf16[128,256]{1,0:T(8,128)(2,1)}, bf16[128,256]{1,0:T(8,128)(2,1)}, u32[]{:S(2)}, u32[]{:S(2)}) %collective-permute-start.14) | collective-permute-done | bytes 65568 | tf_op jit(solution)/shard_map/ppermute | solution.py:277
  92.2 1.9 %collective-permute-done.15.piece3 = bf16[128,256]{1,0:T(8,128)(2,1)} collective-permute-done((bf16[128,256]{1,0:T(8,128)(2,1)}, bf16[128,256]{1,0:T(8,128)(2,1)}, u32[]{:S(2)}, u32[]{:S(2)}) %collective-permute-start.15) | collective-permute-done | bytes 65568 | tf_op jit(solution)/shard_map/ppermute | solution.py:277
  94.1 1.7 %join_kv.1 = (bf16[128,512]{1,0:T(8,128)(2,1)}, bf16[128,512]{1,0:T(8,128)(2,1)}) custom-call(bf16[128,256]{1,0:T(8,128)(2,1)S(1)} %get-tuple-element.75.piece0, bf16[128,256]{1,0:T(8,128)(2,1)} %collective-permute-done.13.piece1, bf16[128,256]{1,0:T(8,128)(2,1)} %collective-permute-done.14.piece2, bf16[128,256]{1,0:T(8,128)(2,1)} %collective-permute-done.15.piece3), custom_call_target="tpu_custom_call" | custom-call | flops 199999995904 | bytes 199999995904 | tf_op jit(solution)/shard_map/join_kv/pallas_call | solution.py:344
  (1 shorter events, 0.0 us)
Async XLA Ops:
  0.6 0.9 copy-start
  1.5 0.9 copy-start.1
  2.4 0.7 copy-start.2
  7.4 5.1 %collective-permute-start = (bf16[128,256]{1,0:T(8,128)(2,1)S(1)}, bf16[128,256]{1,0:T(8,128)(2,1)S(1)}, u32[]{:S(2)}, u32[]{:S(2)}) collective-permute-start(bf16[128,256]{1,0:T(8,128)(2,1)S(1)} %get-tuple-element.43), channel_id=1, source_target_pairs={{0,1},{1,2},{2,3},{3,0},{4,5},{5,6},{6,7},{7,4},{8,9},{9,10},{10,1... | collective-permute-start | bytes 196616 | tf_op jit(solution)/shard_map/ppermute | solution.py:277
  8.8 5.2 %collective-permute-start.1 = (bf16[128,256]{1,0:T(8,128)(2,1)S(1)}, bf16[128,256]{1,0:T(8,128)(2,1)S(1)}, u32[]{:S(2)}, u32[]{:S(2)}) collective-permute-start(bf16[128,256]{1,0:T(8,128)(2,1)S(1)} %get-tuple-element.44), channel_id=1, source_target_pairs={{0,2},{1,3},{2,0},{3,1},{4,6},{5,7},{6,4},{7,5},{8,10},{9,11},{10,... | collective-permute-start | bytes 196616 | tf_op jit(solution)/shard_map/ppermute | solution.py:277
  11.4 3.4 %collective-permute-start.2 = (bf16[128,256]{1,0:T(8,128)(2,1)S(1)}, bf16[128,256]{1,0:T(8,128)(2,1)S(1)}, u32[]{:S(2)}, u32[]{:S(2)}) collective-permute-start(bf16[128,256]{1,0:T(8,128)(2,1)S(1)} %get-tuple-element.45), channel_id=1, source_target_pairs={{0,3},{1,0},{2,1},{3,2},{4,7},{5,4},{6,5},{7,6},{8,11},{9,8},{10,9... | collective-permute-start | bytes 196616 | tf_op jit(solution)/shard_map/ppermute | solution.py:277
  14.8 13.6 %collective-permute-start.3 = (bf16[272,1024]{1,0:T(8,128)(2,1)}, bf16[272,1024]{1,0:T(8,128)(2,1)}, u32[]{:S(2)}, u32[]{:S(2)}) collective-permute-start(bf16[272,1024]{1,0:T(8,128)(2,1)} %get-tuple-element.50), channel_id=1, source_target_pairs={{0,1},{1,2},{2,3},{3,0},{4,5},{5,6},{6,7},{7,4},{8,9},{9,10},{10,1... | collective-permute-start | bytes 1671176 | tf_op jit(solution)/shard_map/ppermute | solution.py:277
  14.8 13.6 %collective-permute-start.4 = (bf16[272,1024]{1,0:T(8,128)(2,1)}, bf16[272,1024]{1,0:T(8,128)(2,1)}, u32[]{:S(2)}, u32[]{:S(2)}) collective-permute-start(bf16[272,1024]{1,0:T(8,128)(2,1)} %get-tuple-element.51), channel_id=1, source_target_pairs={{0,3},{1,0},{2,1},{3,2},{4,7},{5,4},{6,5},{7,6},{8,11},{9,8},{10,9... | collective-permute-start | bytes 1671176 | tf_op jit(solution)/shard_map/ppermute | solution.py:277
  17.5 12.5 %copy-start.3 = (s32[16]{0:T(128)S(1)}, s32[16]{0:T(128)}, u32[]{:S(2)}) copy-start(s32[16]{0:T(128)} %doc_start.7) | copy-start | bytes 196
  18.4 26.0 %collective-permute-start.6 = (bf16[3,128,256]{2,1,0:T(8,128)(2,1)}, bf16[3,128,256]{2,1,0:T(8,128)(2,1)}, u32[]{:S(2)}, u32[]{:S(2)}) collective-permute-start(bf16[3,128,256]{2,1,0:T(8,128)(2,1)} %get-tuple-element.63), channel_id=1, source_target_pairs={{0,8},{1,9},{2,10},{3,11},{4,12},{5,13},{6,14},{7,15},{8,16},{9,17... | collective-permute-start | bytes 589832 | tf_op jit(solution)/shard_map/ppermute | solution.py:281
  25.4 16.9 %collective-permute-start.7 = (bf16[4,128,256]{2,1,0:T(8,128)(2,1)}, bf16[4,128,256]{2,1,0:T(8,128)(2,1)}, u32[]{:S(2)}, u32[]{:S(2)}) collective-permute-start(bf16[4,128,256]{2,1,0:T(8,128)(2,1)} %get-tuple-element.58.kv), channel_id=1, source_target_pairs={{0,4},{1,5},{2,6},{3,7},{4,8},{5,9},{6,10},{7,11},{8,12},{9,13},{1... | collective-permute-start | bytes 786440 | tf_op jit(solution)/shard_map/ppermute | solution.py:281
  28.4 16.0 %collective-permute-start.5 = (bf16[272,1024]{1,0:T(8,128)(2,1)}, bf16[272,1024]{1,0:T(8,128)(2,1)}, u32[]{:S(2)}, u32[]{:S(2)}) collective-permute-start(bf16[272,1024]{1,0:T(8,128)(2,1)} %get-tuple-element.53), channel_id=1, source_target_pairs={{0,2},{1,3},{2,0},{3,1},{4,6},{5,7},{6,4},{7,5},{8,10},{9,11},{10,... | collective-permute-start | bytes 1671176 | tf_op jit(solution)/shard_map/ppermute | solution.py:277
  47.1 20.7 %collective-permute-start.12 = (bf16[3,128,256]{2,1,0:T(8,128)(2,1)}, bf16[3,128,256]{2,1,0:T(8,128)(2,1)}, u32[]{:S(2)}, u32[]{:S(2)}) collective-permute-start(bf16[3,128,256]{2,1,0:T(8,128)(2,1)} %get-tuple-element.74), channel_id=1, source_target_pairs={{8,0},{9,1},{10,2},{11,3},{12,4},{13,5},{14,6},{15,7},{16,8},{17,9... | collective-permute-start | bytes 589832 | tf_op jit(solution)/shard_map/ppermute | solution.py:281
  60.2 24.6 %collective-permute-start.11 = (bf16[4,128,256]{2,1,0:T(8,128)(2,1)}, bf16[4,128,256]{2,1,0:T(8,128)(2,1)}, u32[]{:S(2)}, u32[]{:S(2)}) collective-permute-start(bf16[4,128,256]{2,1,0:T(8,128)(2,1)} %get-tuple-element.73), channel_id=1, source_target_pairs={{4,0},{5,1},{6,2},{7,3},{8,4},{9,5},{10,6},{11,7},{12,8},{13,9},{1... | collective-permute-start | bytes 786440 | tf_op jit(solution)/shard_map/ppermute | solution.py:281
  65.9 21.3 %collective-permute-start.8 = (bf16[128,1024]{1,0:T(8,128)(2,1)}, bf16[128,1024]{1,0:T(8,128)(2,1)}, u32[]{:S(2)}, u32[]{:S(2)}) collective-permute-start(bf16[128,1024]{1,0:T(8,128)(2,1)} %get-tuple-element.69), channel_id=1, source_target_pairs={{0,3},{1,0},{2,1},{3,2},{4,7},{5,4},{6,5},{7,6},{8,11},{9,8},{10,9... | collective-permute-start | bytes 786440 | tf_op jit(solution)/shard_map/ppermute | solution.py:277
  66.1 21.8 %collective-permute-start.9 = (bf16[128,1024]{1,0:T(8,128)(2,1)}, bf16[128,1024]{1,0:T(8,128)(2,1)}, u32[]{:S(2)}, u32[]{:S(2)}) collective-permute-start(bf16[128,1024]{1,0:T(8,128)(2,1)} %get-tuple-element.70), channel_id=1, source_target_pairs={{0,2},{1,3},{2,0},{3,1},{4,6},{5,7},{6,4},{7,5},{8,10},{9,11},{10,... | collective-permute-start | bytes 786440 | tf_op jit(solution)/shard_map/ppermute | solution.py:277
  67.8 20.2 %collective-permute-start.10 = (bf16[128,1024]{1,0:T(8,128)(2,1)}, bf16[128,1024]{1,0:T(8,128)(2,1)}, u32[]{:S(2)}, u32[]{:S(2)}) collective-permute-start(bf16[128,1024]{1,0:T(8,128)(2,1)} %get-tuple-element.71), channel_id=1, source_target_pairs={{0,1},{1,2},{2,3},{3,0},{4,5},{5,6},{6,7},{7,4},{8,9},{9,10},{10,1... | collective-permute-start | bytes 786440 | tf_op jit(solution)/shard_map/ppermute | solution.py:277
  86.5 3.6 %collective-permute-start.13 = (bf16[128,256]{1,0:T(8,128)(2,1)}, bf16[128,256]{1,0:T(8,128)(2,1)}, u32[]{:S(2)}, u32[]{:S(2)}) collective-permute-start(bf16[128,256]{1,0:T(8,128)(2,1)} %get-tuple-element.76), channel_id=1, source_target_pairs={{0,3},{1,0},{2,1},{3,2},{4,7},{5,4},{6,5},{7,6},{8,11},{9,8},{10,9... | collective-permute-start | bytes 196616 | tf_op jit(solution)/shard_map/ppermute | solution.py:277
  87.2 5.0 %collective-permute-start.14 = (bf16[128,256]{1,0:T(8,128)(2,1)}, bf16[128,256]{1,0:T(8,128)(2,1)}, u32[]{:S(2)}, u32[]{:S(2)}) collective-permute-start(bf16[128,256]{1,0:T(8,128)(2,1)} %get-tuple-element.77), channel_id=1, source_target_pairs={{0,2},{1,3},{2,0},{3,1},{4,6},{5,7},{6,4},{7,5},{8,10},{9,11},{10,... | collective-permute-start | bytes 196616 | tf_op jit(solution)/shard_map/ppermute | solution.py:277
  87.2 6.9 %collective-permute-start.15 = (bf16[128,256]{1,0:T(8,128)(2,1)}, bf16[128,256]{1,0:T(8,128)(2,1)}, u32[]{:S(2)}, u32[]{:S(2)}) collective-permute-start(bf16[128,256]{1,0:T(8,128)(2,1)} %get-tuple-element.78), channel_id=1, source_target_pairs={{0,1},{1,2},{2,3},{3,0},{4,5},{5,6},{6,7},{7,4},{8,9},{9,10},{10,1... | collective-permute-start | bytes 196616 | tf_op jit(solution)/shard_map/ppermute | solution.py:277

commit v5 on v4

--- a/solution.py
+++ b/solution.py
@@ -1,3 +1,5 @@
+import functools
+
 import jax
 import jax.numpy as jnp
 from jax import lax
@@ -16,6 +18,7 @@
 AXES = ("seq", "head")
 STAT = 2 * BLOCK
 PIECE = STAT + 16
+HEAVY = 20_000_000_000
 F32 = jnp.float32
 BF16 = jnp.bfloat16
 
@@ -32,52 +35,67 @@
     return jnp.dot(left, right, preferred_element_type=F32)
 
 
-def pack(
-    queries, outputs, grads, norms, keys, values,
-    kv0, kv1, kv2, kv3, piece0, piece1, piece2, piece3, held, sems,
-):
+def pack(shifts, queries, outputs, grads, norms, *rest):
     place = lax.rem(lax.axis_index("head"), ROW)
-    pieces = (piece0, piece1, piece2, piece3)
-    early = []
+    count = len(shifts)
+    rest = list(rest)
     copies = []
-    for shift, (piece, kv) in enumerate(zip(pieces, (kv0, kv1, kv2, kv3))):
+    held_outputs, held_grads, stats, held_norms, sems = rest[-5:]
+    if count < len(rest) - 5:
+        keys, values = rest[:2]
+        kv_pieces = rest[2 : 2 + ROW]
+        pieces = rest[2 + ROW : 2 + ROW + count]
+    else:
+        kv_pieces = []
+        pieces = rest[:count]
+    norm_copy = pltpu.make_async_copy(norms, held_norms, sems.at[0, 5])
+    norm_copy.start()
+    loads = []
+    for slot, shift in enumerate(shifts):
         group = lax.rem(place + shift, ROW)
         span = pl.ds(pl.multiple_of(group * WIDE, WIDE), WIDE)
-        columns = pl.ds(pl.multiple_of(group * DH, DH), DH)
-        for part, (source, target) in enumerate(
-            ((keys, kv.at[:, pl.ds(0, DH)]), (values, kv.at[:, pl.ds(DH, DH)]))
-        ):
-            early.append(
-                pltpu.make_async_copy(source.at[:, columns], target, sems.at[shift, 3 + part])
+        load = [
+            pltpu.make_async_copy(source.at[:, span], target.at[slot], sems.at[slot, part])
+            for part, (source, target) in enumerate(
+                ((grads, held_grads), (outputs, held_outputs))
             )
-        copies.append(
-            [
-                pltpu.make_async_copy(source.at[:, span], target, sems.at[shift, part])
-                for part, (source, target) in enumerate(
-                    (
-                        (grads, piece.at[pl.ds(BLOCK, BLOCK), :]),
-                        (outputs, held.at[shift]),
-                        (queries, piece.at[pl.ds(0, BLOCK), :]),
-                    )
-                )
-            ]
+        ]
+        for copy in load:
+            copy.start()
+        loads.append(load)
+    for shift, kv in enumerate(kv_pieces):
+        columns = pl.ds(pl.multiple_of(lax.rem(place + shift, ROW) * DH, DH), DH)
+        for part, source in enumerate((keys, values)):
+            copy = pltpu.make_async_copy(
+                source.at[:, columns], kv.at[:, pl.ds(part * DH, DH)], sems.at[shift, 6 + part]
+            )
+            copy.start()
+            copies.append(copy)
+    for slot, (shift, piece) in enumerate(zip(shifts, pieces)):
+        group = lax.rem(place + shift, ROW)
+        span = pl.ds(pl.multiple_of(group * WIDE, WIDE), WIDE)
+        copy = pltpu.make_async_copy(
+            queries.at[:, span], piece.at[pl.ds(0, BLOCK), :], sems.at[slot, 2]
         )
-    for part in range(3):
-        for copy in copies:
-            copy[part].start()
-    for copy in early:
         copy.start()
-    turned = norms[...].astype(F32)
+        copies.append(copy)
+    norm_copy.wait()
+    turned = held_norms[...].astype(F32)
     ones = jnp.ones((16, DH), BF16)
     row_id = lax.broadcasted_iota(jnp.int32, (16, BLOCK), 0)
     head_id = lax.broadcasted_iota(jnp.int32, (H, BLOCK), 0)
-    for shift, piece in enumerate(pieces):
+    for slot, (shift, piece) in enumerate(zip(shifts, pieces)):
         group = lax.rem(place + shift, ROW)
-        copies[shift][0].wait()
-        copies[shift][1].wait()
+        for copy in loads[slot]:
+            copy.wait()
+        copy = pltpu.make_async_copy(
+            held_grads.at[slot], piece.at[pl.ds(BLOCK, BLOCK), :], sems.at[slot, 3]
+        )
+        copy.start()
+        copies.append(copy)
         for head in range(GQ):
             cut = slice(head * DH, (head + 1) * DH)
-            product = piece[BLOCK:STAT, cut].astype(F32) * held[shift, :, cut].astype(F32)
+            product = held_grads[slot, :, cut].astype(F32) * held_outputs[slot, :, cut].astype(F32)
             high = product.astype(BF16)
             low = (product - high.astype(F32)).astype(BF16)
             dots = nt(ones, high) + nt(ones, low)
@@ -87,15 +105,18 @@
             norm = jnp.sum(
                 jnp.where(head_id == group * GQ + head, turned, 0.0), axis=0, keepdims=True
             )
-            stats = jnp.where(
+            both = jnp.where(
                 row_id == 0,
                 norm,
                 jnp.where(row_id == 1, first, jnp.where(row_id == 2, second, third)),
             )
-            piece[STAT:, cut] = stats.astype(BF16)
+            stats[slot, :, cut] = both.astype(BF16)
+        copy = pltpu.make_async_copy(
+            stats.at[slot], piece.at[pl.ds(STAT, PIECE - STAT), :], sems.at[slot, 4]
+        )
+        copy.start()
+        copies.append(copy)
     for copy in copies:
-        copy[2].wait()
-    for copy in early:
         copy.wait()
 
 
@@ -251,7 +272,7 @@
         copy.wait()
 
 
-def kernel(body, name, in_specs, shapes, scratch=(), out_spec=VMEM, grant=24, cost=200_000_000_000):
+def kernel(body, name, in_specs, shapes, scratch=(), out_spec=VMEM, grant=24, cost=0):
     return pl.pallas_call(
         body,
         in_specs=in_specs,
@@ -278,39 +299,59 @@
 
     def along_rows(value, rows):
         by = rows * ROW
-        return lax.ppermute(
-            value, AXES, [(b, b + by) for b in range(total) if 0 <= b + by < total]
-        )
+        return lax.ppermute(value, AXES, [(b, (b + by) % total) for b in range(total)])
 
     kv_shape = (ROW, BLOCK, 2 * DH)
     late_shape = (ROW - 1, BLOCK, 2 * DH)
+    dq_shape = ((ROW, DH, WIDE), F32)
+    piece_shape = ((PIECE, WIDE), BF16)
+    turned = log_norms.T
+
+    def pack_scratch(count):
+        return [
+            pltpu.VMEM((count, BLOCK, WIDE), BF16),
+            pltpu.VMEM((count, BLOCK, WIDE), BF16),
+            pltpu.VMEM((count, PIECE - STAT, WIDE), BF16),
+            pltpu.VMEM((H, BLOCK), BF16),
+            sems((ROW, 8)),
+        ]
+
     packed = kernel(
-        pack,
-        "pack",
-        [HBM] * 3 + [VMEM] + [HBM] * 2,
-        [((BLOCK, 2 * DH), BF16)] * ROW + [((PIECE, WIDE), BF16)] * ROW,
-        [pltpu.VMEM((ROW, BLOCK, WIDE), BF16), sems((ROW, 5))],
-        grant=52,
-    )(queries, outputs, out_grads, log_norms.T, keys, values)
+        functools.partial(pack, (1, 3)),
+        "pack_near",
+        [HBM] * 6,
+        [((BLOCK, 2 * DH), BF16)] * ROW + [piece_shape] * 2,
+        pack_scratch(2),
+        HBM,
+        grant=56,
+    )(queries, outputs, out_grads, turned, keys, values)
     kv_pieces = [along_row(packed[shift], shift) for shift in range(ROW)]
-    kv_pieces, sent = lax.optimization_barrier((kv_pieces, packed[ROW:]))
-    piece0 = sent[0]
-    piece1 = along_row(sent[1], 1)
-    piece3 = along_row(sent[3], 3)
+    kv_pieces, near = lax.optimization_barrier((kv_pieces, packed[ROW:]))
+    piece1 = along_row(near[0], 1)
+    piece3 = along_row(near[1], 3)
     kv_own, kv_late = kernel(
         in_order, "in_order", [VMEM] * ROW, [(kv_shape, BF16), (late_shape, BF16)]
     )(*kv_pieces)
     kv_one = along_rows(kv_own, 1)
+    kv_late, turned = lax.optimization_barrier((kv_late, turned))
+    piece0, far = kernel(
+        functools.partial(pack, (0, 2)),
+        "pack_rest",
+        [HBM] * 4,
+        [piece_shape] * 2,
+        pack_scratch(2),
+        HBM,
+        grant=56,
+    )(queries, outputs, out_grads, turned)
+    far, kv_late = lax.optimization_barrier((far, kv_late))
+    piece2 = along_row(far, 2)
     kv_two = along_rows(kv_late, 2)
-    piece1, piece3, far = lax.optimization_barrier((piece1, piece3, sent[2]))
-    piece2 = along_row(far, 2)
-
-    dq_shape = ((ROW, DH, WIDE), F32)
+
     dkv_own, dq = kernel(
-        begin_own, "begin_own", [SMEM] + [VMEM] * 4, [(kv_shape, F32), dq_shape]
+        begin_own, "begin_own", [SMEM] + [VMEM] * 4, [(kv_shape, F32), dq_shape], cost=HEAVY
     )(doc_start, piece0, piece1, piece3, kv_own)
     dkv_one, dq = kernel(
-        begin_one, "begin_one", [SMEM] + [VMEM] * 5, [(kv_shape, F32), dq_shape]
+        begin_one, "begin_one", [SMEM] + [VMEM] * 5, [(kv_shape, F32), dq_shape], cost=HEAVY
     )(doc_start, piece0, piece1, piece3, kv_one, dq)
     dkv_two, dkv_one, dq = kernel(
         finish_earlier,
@@ -318,6 +359,7 @@
         [SMEM] + [VMEM] * 8,
         [(late_shape, BF16), (kv_shape, BF16), dq_shape],
         [pltpu.VMEM(late_shape, F32), pltpu.VMEM(kv_shape, F32)],
+        cost=HEAVY,
     )(doc_start, piece0, piece1, piece2, piece3, kv_two, kv_one, dkv_one, dq)
     back_two = along_rows(dkv_two, -2)
     back_one = along_rows(dkv_one, -1)
@@ -327,6 +369,7 @@
         [SMEM] + [VMEM] * 4,
         [(kv_shape, F32)] + [((BLOCK, WIDE), BF16)] * ROW,
         [pltpu.VMEM((1, DH, WIDE), F32)],
+        cost=HEAVY,
     )(doc_start, piece2, kv_own, dkv_own, dq)
     dq_pieces = [along_row(dq_sent[slot], -slot) for slot in range(ROW)]
     (query_out,) = kernel(
@@ -337,7 +380,9 @@
         [sems((ROW,))],
         HBM,
     )(*dq_pieces)
-    dkv_sent = kernel(add_up, "add_up", [VMEM] * 3, [((BLOCK, 2 * DH), BF16)] * ROW)(
+    dkv_sent = kernel(
+        add_up, "add_up", [VMEM] * 3, [((BLOCK, 2 * DH), BF16)] * ROW, cost=HEAVY
+    )(
         dkv_own, back_one, back_two
     )
     dkv_pieces = [along_row(dkv_sent[slot], -slot) for slot in range(ROW)]

time: 95.6 us -> 115 us (1.20)
  the two profiles are of different devices: /device:TPU:67 before, /device:TPU:34 now
where the time goes in v5:
time: 115 us; the launch traced here: 114 us
  Pallas kernels  60.5 us (53%)
  starting transfers between devices  33.7 us (29%)
  waiting for transfers between devices  16.7 us (15%)
  local copies, waits for them, and re-layouts  1.89 us (2%)
    pallas_call x1, Pallas kernels, per_device(): kernel(functools.partial(pack, (1, 3)), 'pack_near', [HBM] * 6, [((BLOCK,...  25.2 us
    ppermute x12, starting transfers between devices, along_row(): return lax.ppermute(value, AXES, pairs)  23.1 us
    pallas_call x1, Pallas kernels, per_device(): kernel(functools.partial(pack, (0, 2)), 'pack_rest', [HBM] * 4, [piece_sh...  17.3 us
    ppermute x4, starting transfers between devices, along_rows(): lax.ppermute(value, AXES, [(b, (b + by) % total) for b in range(total)])  10.6 us
    ppermute x4, waiting for transfers between devices, along_rows(): lax.ppermute(value, AXES, [(b, (b + by) % total) for b in range(total)])  9.24 us
    ppermute x12, waiting for transfers between devices, along_row(): return lax.ppermute(value, AXES, pairs)  7.45 us
    pallas_call x1, Pallas kernels, per_device(): kernel(begin_one, 'begin_one', [SMEM] + [VMEM] * 5, [(kv_shape, F32), dq_...  5.48 us
    pallas_call x1, Pallas kernels, per_device(): kernel(begin_own, 'begin_own', [SMEM] + [VMEM] * 4, [(kv_shape, F32), dq_...  5 us
  transfers between devices with their start and end apart: 16, of which 7 were waited for; matrix products, arithmetic and copies ran while one was open for 0% of the time, Pallas kernels for 28%

profile of v5, /device:TPU:34, one launch (start us, length us, event | category | flops | bytes accessed | tf_op | source)
XLA Modules:
  0.0 113.7 jit_solution(11012762392785667929)
XLA Ops:
  0.6 25.2 %pack_near.1 = (bf16[128,256]{1,0:T(8,128)(2,1)}, bf16[128,256]{1,0:T(8,128)(2,1)}, bf16[128,256]{1,0:T(8,128)(2,1)}, bf16[128,256]{1,0:T(8,128)(2,1)}, bf16[272...) custom-call(bf16[128,4096]{1,0:T(8,128)(2,1)} %queries.3, bf16[128,4096]{1,0:T(8,128)(2,1)} %outputs.3, ...), custom_call_target="tpu_custom_call" | custom-call | tf_op jit(solution)/shard_map/pack_near/pallas_call | solution.py:319
  25.9 0.0 copy-start.2
  25.9 1.7 %collective-permute-start = (bf16[128,256]{1,0:T(8,128)(2,1)}, bf16[128,256]{1,0:T(8,128)(2,1)S(1)}, u32[]{:S(2)}, u32[]{:S(2)}) collective-permute-start(bf16[128,256]{1,0:T(8,128)(2,1)} %get-tuple-element.42), channel_id=1, source_target_pairs={{0,1},{1,2},{2,3},{3,0},{4,5},{5,6},{6,7},{7,4},{8,9},{9,10},{10,1... | collective-permute-start | bytes 196616 | tf_op jit(solution)/shard_map/ppermute | solution.py:298
  27.6 2.9 %collective-permute-start.1 = (bf16[128,256]{1,0:T(8,128)(2,1)}, bf16[128,256]{1,0:T(8,128)(2,1)S(1)}, u32[]{:S(2)}, u32[]{:S(2)}) collective-permute-start(bf16[128,256]{1,0:T(8,128)(2,1)} %get-tuple-element.43), channel_id=1, source_target_pairs={{0,2},{1,3},{2,0},{3,1},{4,6},{5,7},{6,4},{7,5},{8,10},{9,11},{10,... | collective-permute-start | bytes 196616 | tf_op jit(solution)/shard_map/ppermute | solution.py:298
  30.5 1.3 %collective-permute-start.2 = (bf16[128,256]{1,0:T(8,128)(2,1)}, bf16[128,256]{1,0:T(8,128)(2,1)S(1)}, u32[]{:S(2)}, u32[]{:S(2)}) collective-permute-start(bf16[128,256]{1,0:T(8,128)(2,1)} %get-tuple-element.44), channel_id=1, source_target_pairs={{0,3},{1,0},{2,1},{3,2},{4,7},{5,4},{6,5},{7,6},{8,11},{9,8},{10,9... | collective-permute-start | bytes 196616 | tf_op jit(solution)/shard_map/ppermute | solution.py:298
  31.8 0.0 collective-permute-done.piece1
  31.8 2.1 %collective-permute-done.1.piece2 = bf16[128,256]{1,0:T(8,128)(2,1)S(1)} collective-permute-done((bf16[128,256]{1,0:T(8,128)(2,1)}, bf16[128,256]{1,0:T(8,128)(2,1)S(1)}, u32[]{:S(2)}, u32[]{:S(2)}) %collective-permute-start.1) | collective-permute-done | bytes 65568 | tf_op jit(solution)/shard_map/ppermute | solution.py:298
  33.9 1.1 collective-permute-done.2.piece3
  34.9 0.3 collective-permute-start.4
  35.2 2.9 %collective-permute-start.5 = (bf16[272,1024]{1,0:T(8,128)(2,1)}, bf16[272,1024]{1,0:T(8,128)(2,1)S(1)}, u32[]{:S(2)}, u32[]{:S(2)}) collective-permute-start(bf16[272,1024]{1,0:T(8,128)(2,1)} %get-tuple-element.59), channel_id=1, source_target_pairs={{0,3},{1,0},{2,1},{3,2},{4,7},{5,4},{6,5},{7,6},{8,11},{9,8},{10,9... | collective-permute-start | bytes 1671176 | tf_op jit(solution)/shard_map/ppermute | solution.py:298
  38.2 0.0 copy-start
  38.2 0.8 copy-done
  39.1 3.3 %collective-permute-start.7 = (bf16[4,128,256]{2,1,0:T(8,128)(2,1)S(1)}, bf16[4,128,256]{2,1,0:T(8,128)(2,1)S(1)}, u32[]{:S(2)}, u32[]{:S(2)}) collective-permute-start(bf16[4,128,256]{2,1,0:T(8,128)(2,1)S(1)} %get-tuple-element.56.kv), channel_id=1, source_target_pairs={{0,4},{1,5},{2,6},{3,7},{4,8},{5,9},{6,10},{7,11},{8,12},{9,13},{1... | collective-permute-start | bytes 786440 | tf_op jit(solution)/shard_map/ppermute | solution.py:302
  42.4 17.3 %pack_rest.1 = (bf16[272,1024]{1,0:T(8,128)(2,1)}, bf16[272,1024]{1,0:T(8,128)(2,1)}) custom-call(bf16[128,4096]{1,0:T(8,128)(2,1)} %queries.3, bf16[128,4096]{1,0:T(8,128)(2,1)} %outputs.3, bf16[128,4096]{1,0:T(8,128)(2,1)} %grads.3, bf16[32,128]{1,0:T(8,128)(2,1)} %bitcast.2), custom_call_target="tpu_custom_call" | custom-call | tf_op jit(solution)/shard_map/pack_rest/pallas_call | solution.py:337
  59.7 4.6 %collective-permute-start.6 = (bf16[3,128,256]{2,1,0:T(8,128)(2,1)S(1)}, bf16[3,128,256]{2,1,0:T(8,128)(2,1)S(1)}, u32[]{:S(2)}, u32[]{:S(2)}) collective-permute-start(bf16[3,128,256]{2,1,0:T(8,128)(2,1)S(1)} %get-tuple-element.61), channel_id=1, source_target_pairs={{0,8},{1,9},{2,10},{3,11},{4,12},{5,13},{6,14},{7,15},{8,16},{9,17... | collective-permute-start | bytes 589832 | tf_op jit(solution)/shard_map/ppermute | solution.py:302
  64.3 0.8 collective-permute-start.3
  65.1 0.0 collective-permute-done.4.piece1
  65.1 0.0 collective-permute-done.5.piece3
  65.1 0.0 copy-done.2
  65.1 0.0 copy-start.1
  65.1 1.0 copy-done.1
  66.1 5.0 %begin_own.1 = (f32[4,128,256]{2,1,0:T(8,128)S(1)}, f32[4,128,1024]{2,1,0:T(8,128)S(1)}) custom-call(s32[16]{0:T(128)S(1)} %copy-done.2, bf16[272,1024]{1,0:T(8,128)(2,1)S(1)} %copy-done.1, bf16[272,1024]{1,0:T(8,128)(2,1)S(1)} %collective-permute-done.4.piece1, bf16[272,1024]{1,0:T(8,128)(2,1)S(1)} %collective-permute-done.5.piece3, ...), custom_call_target="tpu_custom_call" | custom-call | flops 20000000000 | bytes 20000000000 | tf_op jit(solution)/shard_map/begin_own/pallas_call | solution.py:350
  71.1 0.0 collective-permute-done.7.kv.kv_one
  71.2 5.5 %begin_one.1 = (f32[4,128,256]{2,1,0:T(8,128)S(1)}, f32[4,128,1024]{2,1,0:T(8,128)S(1)}) custom-call(s32[16]{0:T(128)S(1)} %copy-done.2, bf16[272,1024]{1,0:T(8,128)(2,1)S(1)} %copy-done.1, bf16[272,1024]{1,0:T(8,128)(2,1)S(1)} %collective-permute-done.4.piece1, bf16[272,1024]{1,0:T(8,128)(2,1)S(1)} %collective-permute-done.5.piece3, ...), custom_call_target="tpu_custom_call" | custom-call | flops 20000000000 | bytes 20000000000 | tf_op jit(solution)/shard_map/begin_one/pallas_call | solution.py:353
  76.6 0.0 collective-permute-done.6.kv_two
  76.7 1.2 %collective-permute-done.3.piece2 = bf16[272,1024]{1,0:T(8,128)(2,1)S(1)} collective-permute-done((bf16[272,1024]{1,0:T(8,128)(2,1)}, bf16[272,1024]{1,0:T(8,128)(2,1)S(1)}, u32[]{:S(2)}, u32[]{:S(2)}) %collective-permute-start.3) | collective-permute-done | bytes 557088 | tf_op jit(solution)/shard_map/ppermute | solution.py:298
  77.8 2.5 %finish_earlier.1 = (bf16[3,128,256]{2,1,0:T(8,128)(2,1)S(1)}, bf16[4,128,256]{2,1,0:T(8,128)(2,1)S(1)}, f32[4,128,1024]{2,1,0:T(8,128)S(1)}) custom-call(s32[16]{0:T(128)S(1)} %copy-done.2, bf16[272,1024]{1,0:T(8,128)(2,1)S(1)} %copy-done.1, bf16[272,1024]{1,0:T(8,128)(2,1)S(1)} %collective-permute-done.4.piece1, ...), custom_call_target="tpu_custom_call" | custom-call | flops 20000000000 | bytes 20000000000 | tf_op jit(solution)/shard_map/finish_earlier/pallas_call | solution.py:356
  80.4 1.9 %collective-permute-start.12 = (bf16[3,128,256]{2,1,0:T(8,128)(2,1)S(1)}, bf16[3,128,256]{2,1,0:T(8,128)(2,1)S(1)}, u32[]{:S(2)}, u32[]{:S(2)}) collective-permute-start(bf16[3,128,256]{2,1,0:T(8,128)(2,1)S(1)} %get-tuple-element.72), channel_id=1, source_target_pairs={{0,248},{1,249},{2,250},{3,251},{4,252},{5,253},{6,254},{7,255},{8... | collective-permute-start | bytes 589832 | tf_op jit(solution)/shard_map/ppermute | solution.py:302
  82.3 0.8 collective-permute-start.11
  83.0 3.0 %finish_own.1 = (f32[4,128,256]{2,1,0:T(8,128)S(1)}, bf16[128,1024]{1,0:T(8,128)(2,1)S(1)}, bf16[128,1024]{1,0:T(8,128)(2,1)S(1)}, bf16[128,1024]{1,0:T(8,128)(2,1)S(1)}, bf16[128,1024]{1,0:T(8,128)(2,1)S(1)}) custom-call(s32[16]{0:T(128)S(1)} %copy-done.2, bf16[272,1024]{1,0:T(8,128)(2,1)S(1)} %collective-permute-done.3.piece2, ...), custom_call_target="tpu_custom_call" | custom-call | flops 20000000000 | bytes 20000000000 | tf_op jit(solution)/shard_map/finish_own/pallas_call | solution.py:366
  86.1 0.8 collective-permute-start.8
  86.9 1.0 collective-permute-start.9
  87.9 1.3 %collective-permute-start.10 = (bf16[128,1024]{1,0:T(8,128)(2,1)S(1)}, bf16[128,1024]{1,0:T(8,128)(2,1)S(1)}, u32[]{:S(2)}, u32[]{:S(2)}) collective-permute-start(bf16[128,1024]{1,0:T(8,128)(2,1)S(1)} %get-tuple-element.69), channel_id=1, source_target_pairs={{0,1},{1,2},{2,3},{3,0},{4,5},{5,6},{6,7},{7,4},{8,9},{9,10},{10,1... | collective-permute-start | bytes 786440 | tf_op jit(solution)/shard_map/ppermute | solution.py:298
  89.3 4.7 %collective-permute-done.12.two = bf16[3,128,256]{2,1,0:T(8,128)(2,1)S(1)} collective-permute-done((bf16[3,128,256]{2,1,0:T(8,128)(2,1)S(1)}, bf16[3,128,256]{2,1,0:T(8,128)(2,1)S(1)}, u32[]{:S(2)}, u32[]{:S(2)}) %collective-permute-start.12) | collective-permute-done | bytes 196640 | tf_op jit(solution)/shard_map/ppermute | solution.py:302
  94.0 4.5 %collective-permute-done.11.one = bf16[4,128,256]{2,1,0:T(8,128)(2,1)S(1)} collective-permute-done((bf16[4,128,256]{2,1,0:T(8,128)(2,1)S(1)}, bf16[4,128,256]{2,1,0:T(8,128)(2,1)S(1)}, u32[]{:S(2)}, u32[]{:S(2)}) %collective-permute-start.11) | collective-permute-done | bytes 262176 | tf_op jit(solution)/shard_map/ppermute | solution.py:302
  98.5 0.1 add_up.1
  98.6 1.1 collective-permute-start.13
  99.7 7.5 %collective-permute-start.14 = (bf16[128,256]{1,0:T(8,128)(2,1)S(1)}, bf16[128,256]{1,0:T(8,128)(2,1)S(1)}, u32[]{:S(2)}, u32[]{:S(2)}) collective-permute-start(bf16[128,256]{1,0:T(8,128)(2,1)S(1)} %get-tuple-element.75), channel_id=1, source_target_pairs={{0,2},{1,3},{2,0},{3,1},{4,6},{5,7},{6,4},{7,5},{8,10},{9,11},{10,... | collective-permute-start | bytes 196616 | tf_op jit(solution)/shard_map/ppermute | solution.py:298
  107.3 0.0 collective-permute-done.8.piece1
  107.3 1.3 %collective-permute-start.15 = (bf16[128,256]{1,0:T(8,128)(2,1)S(1)}, bf16[128,256]{1,0:T(8,128)(2,1)S(1)}, u32[]{:S(2)}, u32[]{:S(2)}) collective-permute-start(bf16[128,256]{1,0:T(8,128)(2,1)S(1)} %get-tuple-element.76), channel_id=1, source_target_pairs={{0,1},{1,2},{2,3},{3,0},{4,5},{5,6},{6,7},{7,4},{8,9},{9,10},{10,1... | collective-permute-start | bytes 196616 | tf_op jit(solution)/shard_map/ppermute | solution.py:298
  108.6 0.0 collective-permute-done.9.piece2
  108.6 0.0 collective-permute-done.10.piece3
  108.6 1.0 join_queries.1
  109.6 0.0 collective-permute-done.13.piece1
  109.6 0.4 collective-permute-done.14.piece2
  110.0 2.7 %collective-permute-done.15.piece3 = bf16[128,256]{1,0:T(8,128)(2,1)S(1)} collective-permute-done((bf16[128,256]{1,0:T(8,128)(2,1)S(1)}, bf16[128,256]{1,0:T(8,128)(2,1)S(1)}, u32[]{:S(2)}, u32[]{:S(2)}) %collective-permute-start.15) | collective-permute-done | bytes 65568 | tf_op jit(solution)/shard_map/ppermute | solution.py:298
  112.7 0.8 join_kv.1
  (1 shorter events, 0.0 us)
Async XLA Ops:
  25.9 39.2 %copy-start.2 = (s32[16]{0:T(128)S(1)}, s32[16]{0:T(128)}, u32[]{:S(2)}) copy-start(s32[16]{0:T(128)} %doc_start.7) | copy-start | bytes 196
  25.9 5.9 %collective-permute-start = (bf16[128,256]{1,0:T(8,128)(2,1)}, bf16[128,256]{1,0:T(8,128)(2,1)S(1)}, u32[]{:S(2)}, u32[]{:S(2)}) collective-permute-start(bf16[128,256]{1,0:T(8,128)(2,1)} %get-tuple-element.42), channel_id=1, source_target_pairs={{0,1},{1,2},{2,3},{3,0},{4,5},{5,6},{6,7},{7,4},{8,9},{9,10},{10,1... | collective-permute-start | bytes 196616 | tf_op jit(solution)/shard_map/ppermute | solution.py:298
  27.6 6.3 %collective-permute-start.1 = (bf16[128,256]{1,0:T(8,128)(2,1)}, bf16[128,256]{1,0:T(8,128)(2,1)S(1)}, u32[]{:S(2)}, u32[]{:S(2)}) collective-permute-start(bf16[128,256]{1,0:T(8,128)(2,1)} %get-tuple-element.43), channel_id=1, source_target_pairs={{0,2},{1,3},{2,0},{3,1},{4,6},{5,7},{6,4},{7,5},{8,10},{9,11},{10,... | collective-permute-start | bytes 196616 | tf_op jit(solution)/shard_map/ppermute | solution.py:298
  30.5 4.5 %collective-permute-start.2 = (bf16[128,256]{1,0:T(8,128)(2,1)}, bf16[128,256]{1,0:T(8,128)(2,1)S(1)}, u32[]{:S(2)}, u32[]{:S(2)}) collective-permute-start(bf16[128,256]{1,0:T(8,128)(2,1)} %get-tuple-element.44), channel_id=1, source_target_pairs={{0,3},{1,0},{2,1},{3,2},{4,7},{5,4},{6,5},{7,6},{8,11},{9,8},{10,9... | collective-permute-start | bytes 196616 | tf_op jit(solution)/shard_map/ppermute | solution.py:298
  34.9 30.1 %collective-permute-start.4 = (bf16[272,1024]{1,0:T(8,128)(2,1)}, bf16[272,1024]{1,0:T(8,128)(2,1)S(1)}, u32[]{:S(2)}, u32[]{:S(2)}) collective-permute-start(bf16[272,1024]{1,0:T(8,128)(2,1)} %get-tuple-element.58), channel_id=1, source_target_pairs={{0,1},{1,2},{2,3},{3,0},{4,5},{5,6},{6,7},{7,4},{8,9},{9,10},{10,1... | collective-permute-start | bytes 1671176 | tf_op jit(solution)/shard_map/ppermute | solution.py:298
  35.2 29.8 %collective-permute-start.5 = (bf16[272,1024]{1,0:T(8,128)(2,1)}, bf16[272,1024]{1,0:T(8,128)(2,1)S(1)}, u32[]{:S(2)}, u32[]{:S(2)}) collective-permute-start(bf16[272,1024]{1,0:T(8,128)(2,1)} %get-tuple-element.59), channel_id=1, source_target_pairs={{0,3},{1,0},{2,1},{3,2},{4,7},{5,4},{6,5},{7,6},{8,11},{9,8},{10,9... | collective-permute-start | bytes 1671176 | tf_op jit(solution)/shard_map/ppermute | solution.py:298
  38.2 0.8 copy-start
  39.1 32.1 %collective-permute-start.7 = (bf16[4,128,256]{2,1,0:T(8,128)(2,1)S(1)}, bf16[4,128,256]{2,1,0:T(8,128)(2,1)S(1)}, u32[]{:S(2)}, u32[]{:S(2)}) collective-permute-start(bf16[4,128,256]{2,1,0:T(8,128)(2,1)S(1)} %get-tuple-element.56.kv), channel_id=1, source_target_pairs={{0,4},{1,5},{2,6},{3,7},{4,8},{5,9},{6,10},{7,11},{8,12},{9,13},{1... | collective-permute-start | bytes 786440 | tf_op jit(solution)/shard_map/ppermute | solution.py:302
  59.7 17.0 %collective-permute-start.6 = (bf16[3,128,256]{2,1,0:T(8,128)(2,1)S(1)}, bf16[3,128,256]{2,1,0:T(8,128)(2,1)S(1)}, u32[]{:S(2)}, u32[]{:S(2)}) collective-permute-start(bf16[3,128,256]{2,1,0:T(8,128)(2,1)S(1)} %get-tuple-element.61), channel_id=1, source_target_pairs={{0,8},{1,9},{2,10},{3,11},{4,12},{5,13},{6,14},{7,15},{8,16},{9,17... | collective-permute-start | bytes 589832 | tf_op jit(solution)/shard_map/ppermute | solution.py:302
  64.3 13.5 %collective-permute-start.3 = (bf16[272,1024]{1,0:T(8,128)(2,1)}, bf16[272,1024]{1,0:T(8,128)(2,1)S(1)}, u32[]{:S(2)}, u32[]{:S(2)}) collective-permute-start(bf16[272,1024]{1,0:T(8,128)(2,1)} %get-tuple-element.55), channel_id=1, source_target_pairs={{0,2},{1,3},{2,0},{3,1},{4,6},{5,7},{6,4},{7,5},{8,10},{9,11},{10,... | collective-permute-start | bytes 1671176 | tf_op jit(solution)/shard_map/ppermute | solution.py:298
  65.1 1.1 copy-start.1
  80.4 13.6 %collective-permute-start.12 = (bf16[3,128,256]{2,1,0:T(8,128)(2,1)S(1)}, bf16[3,128,256]{2,1,0:T(8,128)(2,1)S(1)}, u32[]{:S(2)}, u32[]{:S(2)}) collective-permute-start(bf16[3,128,256]{2,1,0:T(8,128)(2,1)S(1)} %get-tuple-element.72), channel_id=1, source_target_pairs={{0,248},{1,249},{2,250},{3,251},{4,252},{5,253},{6,254},{7,255},{8... | collective-permute-start | bytes 589832 | tf_op jit(solution)/shard_map/ppermute | solution.py:302
  82.3 16.2 %collective-permute-start.11 = (bf16[4,128,256]{2,1,0:T(8,128)(2,1)S(1)}, bf16[4,128,256]{2,1,0:T(8,128)(2,1)S(1)}, u32[]{:S(2)}, u32[]{:S(2)}) collective-permute-start(bf16[4,128,256]{2,1,0:T(8,128)(2,1)S(1)} %get-tuple-element.71), channel_id=1, source_target_pairs={{0,252},{1,253},{2,254},{3,255},{4,0},{5,1},{6,2},{7,3},{8,4},{9,5... | collective-permute-start | bytes 786440 | tf_op jit(solution)/shard_map/ppermute | solution.py:302
  86.1 21.2 %collective-permute-start.8 = (bf16[128,1024]{1,0:T(8,128)(2,1)S(1)}, bf16[128,1024]{1,0:T(8,128)(2,1)S(1)}, u32[]{:S(2)}, u32[]{:S(2)}) collective-permute-start(bf16[128,1024]{1,0:T(8,128)(2,1)S(1)} %get-tuple-element.67), channel_id=1, source_target_pairs={{0,3},{1,0},{2,1},{3,2},{4,7},{5,4},{6,5},{7,6},{8,11},{9,8},{10,9... | collective-permute-start | bytes 786440 | tf_op jit(solution)/shard_map/ppermute | solution.py:298
  86.9 21.7 %collective-permute-start.9 = (bf16[128,1024]{1,0:T(8,128)(2,1)S(1)}, bf16[128,1024]{1,0:T(8,128)(2,1)S(1)}, u32[]{:S(2)}, u32[]{:S(2)}) collective-permute-start(bf16[128,1024]{1,0:T(8,128)(2,1)S(1)} %get-tuple-element.68), channel_id=1, source_target_pairs={{0,2},{1,3},{2,0},{3,1},{4,6},{5,7},{6,4},{7,5},{8,10},{9,11},{10,... | collective-permute-start | bytes 786440 | tf_op jit(solution)/shard_map/ppermute | solution.py:298
  87.9 20.6 %collective-permute-start.10 = (bf16[128,1024]{1,0:T(8,128)(2,1)S(1)}, bf16[128,1024]{1,0:T(8,128)(2,1)S(1)}, u32[]{:S(2)}, u32[]{:S(2)}) collective-permute-start(bf16[128,1024]{1,0:T(8,128)(2,1)S(1)} %get-tuple-element.69), channel_id=1, source_target_pairs={{0,1},{1,2},{2,3},{3,0},{4,5},{5,6},{6,7},{7,4},{8,9},{9,10},{10,1... | collective-permute-start | bytes 786440 | tf_op jit(solution)/shard_map/ppermute | solution.py:298
  98.6 11.0 %collective-permute-start.13 = (bf16[128,256]{1,0:T(8,128)(2,1)S(1)}, bf16[128,256]{1,0:T(8,128)(2,1)S(1)}, u32[]{:S(2)}, u32[]{:S(2)}) collective-permute-start(bf16[128,256]{1,0:T(8,128)(2,1)S(1)} %get-tuple-element.74), channel_id=1, source_target_pairs={{0,3},{1,0},{2,1},{3,2},{4,7},{5,4},{6,5},{7,6},{8,11},{9,8},{10,9... | collective-permute-start | bytes 196616 | tf_op jit(solution)/shard_map/ppermute | solution.py:298
  99.7 10.3 %collective-permute-start.14 = (bf16[128,256]{1,0:T(8,128)(2,1)S(1)}, bf16[128,256]{1,0:T(8,128)(2,1)S(1)}, u32[]{:S(2)}, u32[]{:S(2)}) collective-permute-start(bf16[128,256]{1,0:T(8,128)(2,1)S(1)} %get-tuple-element.75), channel_id=1, source_target_pairs={{0,2},{1,3},{2,0},{3,1},{4,6},{5,7},{6,4},{7,5},{8,10},{9,11},{10,... | collective-permute-start | bytes 196616 | tf_op jit(solution)/shard_map/ppermute | solution.py:298
  107.3 5.5 %collective-permute-start.15 = (bf16[128,256]{1,0:T(8,128)(2,1)S(1)}, bf16[128,256]{1,0:T(8,128)(2,1)S(1)}, u32[]{:S(2)}, u32[]{:S(2)}) collective-permute-start(bf16[128,256]{1,0:T(8,128)(2,1)S(1)} %get-tuple-element.76), channel_id=1, source_target_pairs={{0,1},{1,2},{2,3},{3,0},{4,5},{5,6},{6,7},{7,4},{8,9},{9,10},{10,1... | collective-permute-start | bytes 196616 | tf_op jit(solution)/shard_map/ppermute | solution.py:298

commit v6 on v5

--- a/solution.py
+++ b/solution.py
@@ -38,47 +38,44 @@
 def pack(shifts, queries, outputs, grads, norms, *rest):
     place = lax.rem(lax.axis_index("head"), ROW)
     count = len(shifts)
-    rest = list(rest)
-    copies = []
-    held_outputs, held_grads, stats, held_norms, sems = rest[-5:]
-    if count < len(rest) - 5:
-        keys, values = rest[:2]
-        kv_pieces = rest[2 : 2 + ROW]
-        pieces = rest[2 + ROW : 2 + ROW + count]
-    else:
-        kv_pieces = []
-        pieces = rest[:count]
-    norm_copy = pltpu.make_async_copy(norms, held_norms, sems.at[0, 5])
-    norm_copy.start()
+    held_outputs, held_norms, sems = rest[-3:]
+    pieces = rest[-3 - count : -3]
     loads = []
-    for slot, shift in enumerate(shifts):
-        group = lax.rem(place + shift, ROW)
-        span = pl.ds(pl.multiple_of(group * WIDE, WIDE), WIDE)
-        load = [
-            pltpu.make_async_copy(source.at[:, span], target.at[slot], sems.at[slot, part])
-            for part, (source, target) in enumerate(
-                ((grads, held_grads), (outputs, held_outputs))
-            )
-        ]
-        for copy in load:
-            copy.start()
-        loads.append(load)
-    for shift, kv in enumerate(kv_pieces):
-        columns = pl.ds(pl.multiple_of(lax.rem(place + shift, ROW) * DH, DH), DH)
-        for part, source in enumerate((keys, values)):
-            copy = pltpu.make_async_copy(
-                source.at[:, columns], kv.at[:, pl.ds(part * DH, DH)], sems.at[shift, 6 + part]
-            )
-            copy.start()
-            copies.append(copy)
     for slot, (shift, piece) in enumerate(zip(shifts, pieces)):
         group = lax.rem(place + shift, ROW)
         span = pl.ds(pl.multiple_of(group * WIDE, WIDE), WIDE)
-        copy = pltpu.make_async_copy(
-            queries.at[:, span], piece.at[pl.ds(0, BLOCK), :], sems.at[slot, 2]
+        loads.append(
+            [
+                pltpu.make_async_copy(source.at[:, span], target, sems.at[slot, part])
+                for part, (source, target) in enumerate(
+                    (
+                        (grads, piece.at[pl.ds(BLOCK, BLOCK), :]),
+                        (outputs, held_outputs.at[slot]),
+                        (queries, piece.at[pl.ds(0, BLOCK), :]),
+                    )
+                )
+            ]
         )
+    late = [load[2] for load in loads]
+    if len(rest) > 3 + count:
+        keys, values = rest[:2]
+        for shift, kv in enumerate(rest[2 : 2 + ROW]):
+            columns = pl.ds(pl.multiple_of(lax.rem(place + shift, ROW) * DH, DH), DH)
+            for part, source in enumerate((keys, values)):
+                late.append(
+                    pltpu.make_async_copy(
+                        source.at[:, columns],
+                        kv.at[:, pl.ds(part * DH, DH)],
+                        sems.at[shift, 4 + part],
+                    )
+                )
+    norm_copy = pltpu.make_async_copy(norms, held_norms, sems.at[0, 3])
+    norm_copy.start()
+    for load in loads:
+        load[0].start()
+        load[1].start()
+    for copy in late:
         copy.start()
-        copies.append(copy)
     norm_copy.wait()
     turned = held_norms[...].astype(F32)
     ones = jnp.ones((16, DH), BF16)
@@ -86,16 +83,11 @@
     head_id = lax.broadcasted_iota(jnp.int32, (H, BLOCK), 0)
     for slot, (shift, piece) in enumerate(zip(shifts, pieces)):
         group = lax.rem(place + shift, ROW)
-        for copy in loads[slot]:
-            copy.wait()
-        copy = pltpu.make_async_copy(
-            held_grads.at[slot], piece.at[pl.ds(BLOCK, BLOCK), :], sems.at[slot, 3]
-        )
-        copy.start()
-        copies.append(copy)
+        loads[slot][0].wait()
+        loads[slot][1].wait()
         for head in range(GQ):
             cut = slice(head * DH, (head + 1) * DH)
-            product = held_grads[slot, :, cut].astype(F32) * held_outputs[slot, :, cut].astype(F32)
+            product = piece[BLOCK:STAT, cut].astype(F32) * held_outputs[slot, :, cut].astype(F32)
             high = product.astype(BF16)
             low = (product - high.astype(F32)).astype(BF16)
             dots = nt(ones, high) + nt(ones, low)
@@ -105,18 +97,13 @@
             norm = jnp.sum(
                 jnp.where(head_id == group * GQ + head, turned, 0.0), axis=0, keepdims=True
             )
-            both = jnp.where(
+            stats = jnp.where(
                 row_id == 0,
                 norm,
                 jnp.where(row_id == 1, first, jnp.where(row_id == 2, second, third)),
             )
-            stats[slot, :, cut] = both.astype(BF16)
-        copy = pltpu.make_async_copy(
-            stats.at[slot], piece.at[pl.ds(STAT, PIECE - STAT), :], sems.at[slot, 4]
-        )
-        copy.start()
-        copies.append(copy)
-    for copy in copies:
+            piece[STAT:, cut] = stats.astype(BF16)
+    for copy in late:
         copy.wait()
 
 
@@ -310,10 +297,8 @@
     def pack_scratch(count):
         return [
             pltpu.VMEM((count, BLOCK, WIDE), BF16),
-            pltpu.VMEM((count, BLOCK, WIDE), BF16),
-            pltpu.VMEM((count, PIECE - STAT, WIDE), BF16),
             pltpu.VMEM((H, BLOCK), BF16),
-            sems((ROW, 8)),
+            sems((ROW, 6)),
         ]
 
     packed = kernel(
@@ -322,7 +307,6 @@
         [HBM] * 6,
         [((BLOCK, 2 * DH), BF16)] * ROW + [piece_shape] * 2,
         pack_scratch(2),
-        HBM,
         grant=56,
     )(queries, outputs, out_grads, turned, keys, values)
     kv_pieces = [along_row(packed[shift], shift) for shift in range(ROW)]
@@ -340,8 +324,7 @@
         [HBM] * 4,
         [piece_shape] * 2,
         pack_scratch(2),
-        HBM,
-        grant=56,
+        grant=52,
     )(queries, outputs, out_grads, turned)
     far, kv_late = lax.optimization_barrier((far, kv_late))
     piece2 = along_row(far, 2)

time: 115 us -> 82.5 us (0.72)
  the two profiles are of different devices: /device:TPU:34 before, /device:TPU:1 now
where the time goes in v6:
time: 82.5 us; the launch traced here: 82.1 us
  starting transfers between devices  40.3 us (49%)
  waiting for transfers between devices  22.4 us (27%)
  Pallas kernels  17.6 us (21%)
  between operations  0.9 us (1%)
  local copies, waits for them, and re-layouts  0.85 us (1%)
    ppermute x4, starting transfers between devices, along_rows(): lax.ppermute(value, AXES, [(b, (b + by) % total) for b in range(total)])  23.5 us
    ppermute x12, starting transfers between devices, along_row(): return lax.ppermute(value, AXES, pairs)  16.8 us
    ppermute x4, waiting for transfers between devices, along_rows(): lax.ppermute(value, AXES, [(b, (b + by) % total) for b in range(total)])  16.2 us
    ppermute x12, waiting for transfers between devices, along_row(): return lax.ppermute(value, AXES, pairs)  6.21 us
    pallas_call x1, Pallas kernels, per_device(): kernel(functools.partial(pack, (1, 3)), 'pack_near', [HBM] * 6, [((BLOCK,...  3.16 us
    pallas_call x1, Pallas kernels, per_device(): kernel(begin_one, 'begin_one', [SMEM] + [VMEM] * 5, [(kv_shape, F32), dq_...  2.89 us
    pallas_call x1, Pallas kernels, per_device(): kernel(begin_own, 'begin_own', [SMEM] + [VMEM] * 4, [(kv_shape, F32), dq_...  2.61 us
    pallas_call x1, Pallas kernels, per_device(): kernel(finish_earlier, 'finish_earlier', [SMEM] + [VMEM] * 8, [(late_shap...  2.55 us
  transfers between devices with their start and end apart: 16, of which 7 were waited for; matrix products, arithmetic and copies ran while one was open for 0% of the time, Pallas kernels for 14%

profile of v6, /device:TPU:1, one launch (start us, length us, event | category | flops | bytes accessed | tf_op | source)
XLA Modules:
  0.0 82.1 jit_solution(10176650204403500920)
XLA Ops:
  0.6 0.0 copy-start.1
  0.6 3.2 %pack_near.1 = (bf16[128,256]{1,0:T(8,128)(2,1)}, bf16[128,256]{1,0:T(8,128)(2,1)}, bf16[128,256]{1,0:T(8,128)(2,1)}, bf16[128,256]{1,0:T(8,128)(2,1)}, bf16[272...) custom-call(bf16[128,4096]{1,0:T(8,128)(2,1)} %queries.3, bf16[128,4096]{1,0:T(8,128)(2,1)} %outputs.3, ...), custom_call_target="tpu_custom_call" | custom-call | tf_op jit(solution)/shard_map/pack_near/pallas_call | solution.py:304
  3.8 0.0 copy-start.2
  3.8 2.2 %collective-permute-start = (bf16[128,256]{1,0:T(8,128)(2,1)}, bf16[128,256]{1,0:T(8,128)(2,1)S(1)}, u32[]{:S(2)}, u32[]{:S(2)}) collective-permute-start(bf16[128,256]{1,0:T(8,128)(2,1)} %get-tuple-element.42), channel_id=1, source_target_pairs={{0,1},{1,2},{2,3},{3,0},{4,5},{5,6},{6,7},{7,4},{8,9},{9,10},{10,1... | collective-permute-start | bytes 196616 | tf_op jit(solution)/shard_map/ppermute | solution.py:285
  6.0 2.6 %collective-permute-start.1 = (bf16[128,256]{1,0:T(8,128)(2,1)}, bf16[128,256]{1,0:T(8,128)(2,1)S(1)}, u32[]{:S(2)}, u32[]{:S(2)}) collective-permute-start(bf16[128,256]{1,0:T(8,128)(2,1)} %get-tuple-element.43), channel_id=1, source_target_pairs={{0,2},{1,3},{2,0},{3,1},{4,6},{5,7},{6,4},{7,5},{8,10},{9,11},{10,... | collective-permute-start | bytes 196616 | tf_op jit(solution)/shard_map/ppermute | solution.py:285
  8.6 1.1 %collective-permute-start.2 = (bf16[128,256]{1,0:T(8,128)(2,1)}, bf16[128,256]{1,0:T(8,128)(2,1)S(1)}, u32[]{:S(2)}, u32[]{:S(2)}) collective-permute-start(bf16[128,256]{1,0:T(8,128)(2,1)} %get-tuple-element.44), channel_id=1, source_target_pairs={{0,3},{1,0},{2,1},{3,2},{4,7},{5,4},{6,5},{7,6},{8,11},{9,8},{10,9... | collective-permute-start | bytes 196616 | tf_op jit(solution)/shard_map/ppermute | solution.py:285
  9.7 0.0 collective-permute-done.piece1
  9.7 1.7 %collective-permute-done.1.piece2 = bf16[128,256]{1,0:T(8,128)(2,1)S(1)} collective-permute-done((bf16[128,256]{1,0:T(8,128)(2,1)}, bf16[128,256]{1,0:T(8,128)(2,1)S(1)}, u32[]{:S(2)}, u32[]{:S(2)}) %collective-permute-start.1) | collective-permute-done | bytes 65568 | tf_op jit(solution)/shard_map/ppermute | solution.py:285
  11.5 0.8 collective-permute-done.2.piece3
  12.3 0.0 collective-permute-start.4
  12.3 2.7 %collective-permute-start.5 = (bf16[272,1024]{1,0:T(8,128)(2,1)}, bf16[272,1024]{1,0:T(8,128)(2,1)S(1)}, u32[]{:S(2)}, u32[]{:S(2)}) collective-permute-start(bf16[272,1024]{1,0:T(8,128)(2,1)} %get-tuple-element.59), channel_id=1, source_target_pairs={{0,3},{1,0},{2,1},{3,2},{4,7},{5,4},{6,5},{7,6},{8,11},{9,8},{10,9... | collective-permute-start | bytes 1671176 | tf_op jit(solution)/shard_map/ppermute | solution.py:285
  14.9 0.0 copy-start
  15.0 0.8 %copy-done = bf16[128,256]{1,0:T(8,128)(2,1)S(1)} copy-done((bf16[128,256]{1,0:T(8,128)(2,1)S(1)}, bf16[128,256]{1,0:T(8,128)(2,1)}, u32[]{:S(2)}) %copy-start) | copy-done | bytes 65560
  15.8 3.1 %collective-permute-start.7 = (bf16[4,128,256]{2,1,0:T(8,128)(2,1)S(1)}, bf16[4,128,256]{2,1,0:T(8,128)(2,1)S(1)}, u32[]{:S(2)}, u32[]{:S(2)}) collective-permute-start(bf16[4,128,256]{2,1,0:T(8,128)(2,1)S(1)} %get-tuple-element.56.kv), channel_id=1, source_target_pairs={{0,4},{1,5},{2,6},{3,7},{4,8},{5,9},{6,10},{7,11},{8,12},{9,13},{1... | collective-permute-start | bytes 786440 | tf_op jit(solution)/shard_map/ppermute | solution.py:289
  18.9 0.0 copy-done.1
  18.9 2.1 %pack_rest.1 = (bf16[272,1024]{1,0:T(8,128)(2,1)S(1)}, bf16[272,1024]{1,0:T(8,128)(2,1)S(1)}) custom-call(bf16[128,4096]{1,0:T(8,128)(2,1)} %queries.3, bf16[128,4096]{1,0:T(8,128)(2,1)} %outputs.3, bf16[128,4096]{1,0:T(8,128)(2,1)} %grads.3, bf16[32,128]{1,0:T(8,128)(2,1)S(1)} %bitcast.2), custom_call_target="tpu_custom_call" | custom-call | tf_op jit(solution)/shard_map/pack_rest/pallas_call | solution.py:321
  21.0 5.2 %collective-permute-start.6 = (bf16[3,128,256]{2,1,0:T(8,128)(2,1)S(1)}, bf16[3,128,256]{2,1,0:T(8,128)(2,1)S(1)}, u32[]{:S(2)}, u32[]{:S(2)}) collective-permute-start(bf16[3,128,256]{2,1,0:T(8,128)(2,1)S(1)} %get-tuple-element.61), channel_id=1, source_target_pairs={{0,8},{1,9},{2,10},{3,11},{4,12},{5,13},{6,14},{7,15},{8,16},{9,17... | collective-permute-start | bytes 589832 | tf_op jit(solution)/shard_map/ppermute | solution.py:289
  26.2 0.6 collective-permute-start.3
  26.8 0.0 collective-permute-done.4.piece1
  26.8 0.0 collective-permute-done.5.piece3
  26.8 0.0 copy-done.2
  26.8 2.6 %begin_own.1 = (f32[4,128,256]{2,1,0:T(8,128)S(1)}, f32[4,128,1024]{2,1,0:T(8,128)S(1)}) custom-call(s32[16]{0:T(128)S(1)} %copy-done.2, bf16[272,1024]{1,0:T(8,128)(2,1)S(1)} %get-tuple-element.57.piece0, bf16[272,1024]{1,0:T(8,128)(2,1)S(1)} %collective-permute-done.4.piece1, bf16[272,1024]{1,0:T(8,128)(2,1)S(1)} %collective-permute-done.5.piece3, ...), custom_call_target="tpu_custom_call" | custom-call | flops 20000000000 | bytes 20000000000 | tf_op jit(solution)/shard_map/begin_own/pallas_call | solution.py:333
  29.4 2.2 %collective-permute-done.7.kv.kv_one = bf16[4,128,256]{2,1,0:T(8,128)(2,1)S(1)} collective-permute-done((bf16[4,128,256]{2,1,0:T(8,128)(2,1)S(1)}, bf16[4,128,256]{2,1,0:T(8,128)(2,1)S(1)}, u32[]{:S(2)}, u32[]{:S(2)}) %collective-permute-start.7) | collective-permute-done | bytes 262176 | tf_op jit(solution)/shard_map/ppermute | solution.py:289
  31.7 2.9 %begin_one.1 = (f32[4,128,256]{2,1,0:T(8,128)S(1)}, f32[4,128,1024]{2,1,0:T(8,128)S(1)}) custom-call(s32[16]{0:T(128)S(1)} %copy-done.2, bf16[272,1024]{1,0:T(8,128)(2,1)S(1)} %get-tuple-element.57.piece0, bf16[272,1024]{1,0:T(8,128)(2,1)S(1)} %collective-permute-done.4.piece1, bf16[272,1024]{1,0:T(8,128)(2,1)S(1)} %collective-permute-done.5.piece3, ...), custom_call_target="tpu_custom_call" | custom-call | flops 20000000000 | bytes 20000000000 | tf_op jit(solution)/shard_map/begin_one/pallas_call | solution.py:336
  34.6 6.9 %collective-permute-done.6.kv_two = bf16[3,128,256]{2,1,0:T(8,128)(2,1)S(1)} collective-permute-done((bf16[3,128,256]{2,1,0:T(8,128)(2,1)S(1)}, bf16[3,128,256]{2,1,0:T(8,128)(2,1)S(1)}, u32[]{:S(2)}, u32[]{:S(2)}) %collective-permute-start.6) | collective-permute-done | bytes 196640 | tf_op jit(solution)/shard_map/ppermute | solution.py:289
  41.4 0.0 collective-permute-done.3.piece2
  41.4 2.5 %finish_earlier.1 = (bf16[3,128,256]{2,1,0:T(8,128)(2,1)S(1)}, bf16[4,128,256]{2,1,0:T(8,128)(2,1)S(1)}, f32[4,128,1024]{2,1,0:T(8,128)S(1)}) custom-call(s32[16]{0:T(128)S(1)} %copy-done.2, bf16[272,1024]{1,0:T(8,128)(2,1)S(1)} %get-tuple-element.57.piece0, bf16[272,1024]{1,0:T(8,128)(2,1)S(1)} %collective-permute-done.4.piece1, ...), custom_call_target="tpu_custom_call" | custom-call | flops 20000000000 | bytes 20000000000 | tf_op jit(solution)/shard_map/finish_earlier/pallas_call | solution.py:339
  44.0 10.2 %collective-permute-start.12 = (bf16[3,128,256]{2,1,0:T(8,128)(2,1)S(1)}, bf16[3,128,256]{2,1,0:T(8,128)(2,1)S(1)}, u32[]{:S(2)}, u32[]{:S(2)}) collective-permute-start(bf16[3,128,256]{2,1,0:T(8,128)(2,1)S(1)} %get-tuple-element.72), channel_id=1, source_target_pairs={{0,248},{1,249},{2,250},{3,251},{4,252},{5,253},{6,254},{7,255},{8... | collective-permute-start | bytes 589832 | tf_op jit(solution)/shard_map/ppermute | solution.py:289
  54.2 5.1 %collective-permute-start.11 = (bf16[4,128,256]{2,1,0:T(8,128)(2,1)S(1)}, bf16[4,128,256]{2,1,0:T(8,128)(2,1)S(1)}, u32[]{:S(2)}, u32[]{:S(2)}) collective-permute-start(bf16[4,128,256]{2,1,0:T(8,128)(2,1)S(1)} %get-tuple-element.71), channel_id=1, source_target_pairs={{0,252},{1,253},{2,254},{3,255},{4,0},{5,1},{6,2},{7,3},{8,4},{9,5... | collective-permute-start | bytes 786440 | tf_op jit(solution)/shard_map/ppermute | solution.py:289
  59.2 2.4 %finish_own.1 = (f32[4,128,256]{2,1,0:T(8,128)S(1)}, bf16[128,1024]{1,0:T(8,128)(2,1)S(1)}, bf16[128,1024]{1,0:T(8,128)(2,1)S(1)}, bf16[128,1024]{1,0:T(8,128)(2,1)S(1)}, bf16[128,1024]{1,0:T(8,128)(2,1)S(1)}) custom-call(s32[16]{0:T(128)S(1)} %copy-done.2, bf16[272,1024]{1,0:T(8,128)(2,1)S(1)} %collective-permute-done.3.piece2, ...), custom_call_target="tpu_custom_call" | custom-call | flops 20000000000 | bytes 20000000000 | tf_op jit(solution)/shard_map/finish_own/pallas_call | solution.py:349
  61.7 3.4 %collective-permute-start.8 = (bf16[128,1024]{1,0:T(8,128)(2,1)S(1)}, bf16[128,1024]{1,0:T(8,128)(2,1)S(1)}, u32[]{:S(2)}, u32[]{:S(2)}) collective-permute-start(bf16[128,1024]{1,0:T(8,128)(2,1)S(1)} %get-tuple-element.67), channel_id=1, source_target_pairs={{0,3},{1,0},{2,1},{3,2},{4,7},{5,4},{6,5},{7,6},{8,11},{9,8},{10,9... | collective-permute-start | bytes 786440 | tf_op jit(solution)/shard_map/ppermute | solution.py:285
  65.1 0.0 collective-permute-start.9
  65.1 0.7 collective-permute-start.10
  65.7 0.0 collective-permute-done.12.two
  65.8 7.1 %collective-permute-done.11.one = bf16[4,128,256]{2,1,0:T(8,128)(2,1)S(1)} collective-permute-done((bf16[4,128,256]{2,1,0:T(8,128)(2,1)S(1)}, bf16[4,128,256]{2,1,0:T(8,128)(2,1)S(1)}, u32[]{:S(2)}, u32[]{:S(2)}) %collective-permute-start.11) | collective-permute-done | bytes 262176 | tf_op jit(solution)/shard_map/ppermute | solution.py:289
  72.9 0.1 add_up.1
  73.0 2.9 %collective-permute-start.13 = (bf16[128,256]{1,0:T(8,128)(2,1)S(1)}, bf16[128,256]{1,0:T(8,128)(2,1)S(1)}, u32[]{:S(2)}, u32[]{:S(2)}) collective-permute-start(bf16[128,256]{1,0:T(8,128)(2,1)S(1)} %get-tuple-element.74), channel_id=1, source_target_pairs={{0,3},{1,0},{2,1},{3,2},{4,7},{5,4},{6,5},{7,6},{8,11},{9,8},{10,9... | collective-permute-start | bytes 196616 | tf_op jit(solution)/shard_map/ppermute | solution.py:285
  75.8 0.0 collective-permute-start.14
  75.8 0.0 collective-permute-done.8.piece1
  75.8 0.7 collective-permute-start.15
  76.5 0.0 collective-permute-done.9.piece2
  76.5 0.0 collective-permute-done.10.piece3
  76.5 1.0 %join_queries.1 = bf16[128,4096]{1,0:T(8,128)(2,1)} custom-call(bf16[128,1024]{1,0:T(8,128)(2,1)S(1)} %get-tuple-element.66.piece0, bf16[128,1024]{1,0:T(8,128)(2,1)S(1)} %collective-permute-done.8.piece1, bf16[128,1024]{1,0:T(8,128)(2,1)S(1)} %collective-permute-done.9.piece2, bf16[128,1024]{1,0:T(8,128)(2,1)S(1)} %collective-permute-done.10.piece3), custom_call_target="tpu_custom_call" | custom-call | tf_op jit(solution)/shard_map/join_queries/pallas_call | solution.py:358
  77.5 0.0 collective-permute-done.13.piece1
  77.5 3.0 %collective-permute-done.14.piece2 = bf16[128,256]{1,0:T(8,128)(2,1)S(1)} collective-permute-done((bf16[128,256]{1,0:T(8,128)(2,1)S(1)}, bf16[128,256]{1,0:T(8,128)(2,1)S(1)}, u32[]{:S(2)}, u32[]{:S(2)}) %collective-permute-start.14) | collective-permute-done | bytes 65568 | tf_op jit(solution)/shard_map/ppermute | solution.py:285
  80.6 0.6 collective-permute-done.15.piece3
  81.2 0.8 join_kv.1
  (1 shorter events, 0.0 us)
Async XLA Ops:
  0.6 18.3 %copy-start.1 = (bf16[128,32]{0,1:T(8,128)(2,1)S(1)}, bf16[128,32]{0,1:T(8,128)(2,1)}, u32[]{:S(2)}) copy-start(bf16[128,32]{0,1:T(8,128)(2,1)} %param.10) | copy-start | bytes 24580
  3.8 23.0 %copy-start.2 = (s32[16]{0:T(128)S(1)}, s32[16]{0:T(128)}, u32[]{:S(2)}) copy-start(s32[16]{0:T(128)} %doc_start.7) | copy-start | bytes 196
  3.8 5.9 %collective-permute-start = (bf16[128,256]{1,0:T(8,128)(2,1)}, bf16[128,256]{1,0:T(8,128)(2,1)S(1)}, u32[]{:S(2)}, u32[]{:S(2)}) collective-permute-start(bf16[128,256]{1,0:T(8,128)(2,1)} %get-tuple-element.42), channel_id=1, source_target_pairs={{0,1},{1,2},{2,3},{3,0},{4,5},{5,6},{6,7},{7,4},{8,9},{9,10},{10,1... | collective-permute-start | bytes 196616 | tf_op jit(solution)/shard_map/ppermute | solution.py:285
  6.0 5.4 %collective-permute-start.1 = (bf16[128,256]{1,0:T(8,128)(2,1)}, bf16[128,256]{1,0:T(8,128)(2,1)S(1)}, u32[]{:S(2)}, u32[]{:S(2)}) collective-permute-start(bf16[128,256]{1,0:T(8,128)(2,1)} %get-tuple-element.43), channel_id=1, source_target_pairs={{0,2},{1,3},{2,0},{3,1},{4,6},{5,7},{6,4},{7,5},{8,10},{9,11},{10,... | collective-permute-start | bytes 196616 | tf_op jit(solution)/shard_map/ppermute | solution.py:285
  8.6 3.6 %collective-permute-start.2 = (bf16[128,256]{1,0:T(8,128)(2,1)}, bf16[128,256]{1,0:T(8,128)(2,1)S(1)}, u32[]{:S(2)}, u32[]{:S(2)}) collective-permute-start(bf16[128,256]{1,0:T(8,128)(2,1)} %get-tuple-element.44), channel_id=1, source_target_pairs={{0,3},{1,0},{2,1},{3,2},{4,7},{5,4},{6,5},{7,6},{8,11},{9,8},{10,9... | collective-permute-start | bytes 196616 | tf_op jit(solution)/shard_map/ppermute | solution.py:285
  12.3 14.5 %collective-permute-start.4 = (bf16[272,1024]{1,0:T(8,128)(2,1)}, bf16[272,1024]{1,0:T(8,128)(2,1)S(1)}, u32[]{:S(2)}, u32[]{:S(2)}) collective-permute-start(bf16[272,1024]{1,0:T(8,128)(2,1)} %get-tuple-element.58), channel_id=1, source_target_pairs={{0,1},{1,2},{2,3},{3,0},{4,5},{5,6},{6,7},{7,4},{8,9},{9,10},{10,1... | collective-permute-start | bytes 1671176 | tf_op jit(solution)/shard_map/ppermute | solution.py:285
  12.3 14.5 %collective-permute-start.5 = (bf16[272,1024]{1,0:T(8,128)(2,1)}, bf16[272,1024]{1,0:T(8,128)(2,1)S(1)}, u32[]{:S(2)}, u32[]{:S(2)}) collective-permute-start(bf16[272,1024]{1,0:T(8,128)(2,1)} %get-tuple-element.59), channel_id=1, source_target_pairs={{0,3},{1,0},{2,1},{3,2},{4,7},{5,4},{6,5},{7,6},{8,11},{9,8},{10,9... | collective-permute-start | bytes 1671176 | tf_op jit(solution)/shard_map/ppermute | solution.py:285
  14.9 0.8 %copy-start = (bf16[128,256]{1,0:T(8,128)(2,1)S(1)}, bf16[128,256]{1,0:T(8,128)(2,1)}, u32[]{:S(2)}) copy-start(bf16[128,256]{1,0:T(8,128)(2,1)} %get-tuple-element.47.piece0) | copy-start | bytes 196612
  15.8 15.8 %collective-permute-start.7 = (bf16[4,128,256]{2,1,0:T(8,128)(2,1)S(1)}, bf16[4,128,256]{2,1,0:T(8,128)(2,1)S(1)}, u32[]{:S(2)}, u32[]{:S(2)}) collective-permute-start(bf16[4,128,256]{2,1,0:T(8,128)(2,1)S(1)} %get-tuple-element.56.kv), channel_id=1, source_target_pairs={{0,4},{1,5},{2,6},{3,7},{4,8},{5,9},{6,10},{7,11},{8,12},{9,13},{1... | collective-permute-start | bytes 786440 | tf_op jit(solution)/shard_map/ppermute | solution.py:289
  21.0 20.5 %collective-permute-start.6 = (bf16[3,128,256]{2,1,0:T(8,128)(2,1)S(1)}, bf16[3,128,256]{2,1,0:T(8,128)(2,1)S(1)}, u32[]{:S(2)}, u32[]{:S(2)}) collective-permute-start(bf16[3,128,256]{2,1,0:T(8,128)(2,1)S(1)} %get-tuple-element.61), channel_id=1, source_target_pairs={{0,8},{1,9},{2,10},{3,11},{4,12},{5,13},{6,14},{7,15},{8,16},{9,17... | collective-permute-start | bytes 589832 | tf_op jit(solution)/shard_map/ppermute | solution.py:289
  26.2 15.2 %collective-permute-start.3 = (bf16[272,1024]{1,0:T(8,128)(2,1)S(1)}, bf16[272,1024]{1,0:T(8,128)(2,1)S(1)}, u32[]{:S(2)}, u32[]{:S(2)}) collective-permute-start(bf16[272,1024]{1,0:T(8,128)(2,1)S(1)} %get-tuple-element.55), channel_id=1, source_target_pairs={{0,2},{1,3},{2,0},{3,1},{4,6},{5,7},{6,4},{7,5},{8,10},{9,11},{10,... | collective-permute-start | bytes 1671176 | tf_op jit(solution)/shard_map/ppermute | solution.py:285
  44.0 21.8 %collective-permute-start.12 = (bf16[3,128,256]{2,1,0:T(8,128)(2,1)S(1)}, bf16[3,128,256]{2,1,0:T(8,128)(2,1)S(1)}, u32[]{:S(2)}, u32[]{:S(2)}) collective-permute-start(bf16[3,128,256]{2,1,0:T(8,128)(2,1)S(1)} %get-tuple-element.72), channel_id=1, source_target_pairs={{0,248},{1,249},{2,250},{3,251},{4,252},{5,253},{6,254},{7,255},{8... | collective-permute-start | bytes 589832 | tf_op jit(solution)/shard_map/ppermute | solution.py:289
  54.2 18.7 %collective-permute-start.11 = (bf16[4,128,256]{2,1,0:T(8,128)(2,1)S(1)}, bf16[4,128,256]{2,1,0:T(8,128)(2,1)S(1)}, u32[]{:S(2)}, u32[]{:S(2)}) collective-permute-start(bf16[4,128,256]{2,1,0:T(8,128)(2,1)S(1)} %get-tuple-element.71), channel_id=1, source_target_pairs={{0,252},{1,253},{2,254},{3,255},{4,0},{5,1},{6,2},{7,3},{8,4},{9,5... | collective-permute-start | bytes 786440 | tf_op jit(solution)/shard_map/ppermute | solution.py:289
  61.7 14.2 %collective-permute-start.8 = (bf16[128,1024]{1,0:T(8,128)(2,1)S(1)}, bf16[128,1024]{1,0:T(8,128)(2,1)S(1)}, u32[]{:S(2)}, u32[]{:S(2)}) collective-permute-start(bf16[128,1024]{1,0:T(8,128)(2,1)S(1)} %get-tuple-element.67), channel_id=1, source_target_pairs={{0,3},{1,0},{2,1},{3,2},{4,7},{5,4},{6,5},{7,6},{8,11},{9,8},{10,9... | collective-permute-start | bytes 786440 | tf_op jit(solution)/shard_map/ppermute | solution.py:285
  65.1 11.5 %collective-permute-start.9 = (bf16[128,1024]{1,0:T(8,128)(2,1)S(1)}, bf16[128,1024]{1,0:T(8,128)(2,1)S(1)}, u32[]{:S(2)}, u32[]{:S(2)}) collective-permute-start(bf16[128,1024]{1,0:T(8,128)(2,1)S(1)} %get-tuple-element.68), channel_id=1, source_target_pairs={{0,2},{1,3},{2,0},{3,1},{4,6},{5,7},{6,4},{7,5},{8,10},{9,11},{10,... | collective-permute-start | bytes 786440 | tf_op jit(solution)/shard_map/ppermute | solution.py:285
  65.1 11.5 %collective-permute-start.10 = (bf16[128,1024]{1,0:T(8,128)(2,1)S(1)}, bf16[128,1024]{1,0:T(8,128)(2,1)S(1)}, u32[]{:S(2)}, u32[]{:S(2)}) collective-permute-start(bf16[128,1024]{1,0:T(8,128)(2,1)S(1)} %get-tuple-element.69), channel_id=1, source_target_pairs={{0,1},{1,2},{2,3},{3,0},{4,5},{5,6},{6,7},{7,4},{8,9},{9,10},{10,1... | collective-permute-start | bytes 786440 | tf_op jit(solution)/shard_map/ppermute | solution.py:285
  73.0 4.6 %collective-permute-start.13 = (bf16[128,256]{1,0:T(8,128)(2,1)S(1)}, bf16[128,256]{1,0:T(8,128)(2,1)S(1)}, u32[]{:S(2)}, u32[]{:S(2)}) collective-permute-start(bf16[128,256]{1,0:T(8,128)(2,1)S(1)} %get-tuple-element.74), channel_id=1, source_target_pairs={{0,3},{1,0},{2,1},{3,2},{4,7},{5,4},{6,5},{7,6},{8,11},{9,8},{10,9... | collective-permute-start | bytes 196616 | tf_op jit(solution)/shard_map/ppermute | solution.py:285
  75.8 4.7 %collective-permute-start.14 = (bf16[128,256]{1,0:T(8,128)(2,1)S(1)}, bf16[128,256]{1,0:T(8,128)(2,1)S(1)}, u32[]{:S(2)}, u32[]{:S(2)}) collective-permute-start(bf16[128,256]{1,0:T(8,128)(2,1)S(1)} %get-tuple-element.75), channel_id=1, source_target_pairs={{0,2},{1,3},{2,0},{3,1},{4,6},{5,7},{6,4},{7,5},{8,10},{9,11},{10,... | collective-permute-start | bytes 196616 | tf_op jit(solution)/shard_map/ppermute | solution.py:285
  75.8 5.3 %collective-permute-start.15 = (bf16[128,256]{1,0:T(8,128)(2,1)S(1)}, bf16[128,256]{1,0:T(8,128)(2,1)S(1)}, u32[]{:S(2)}, u32[]{:S(2)}) collective-permute-start(bf16[128,256]{1,0:T(8,128)(2,1)S(1)} %get-tuple-element.76), channel_id=1, source_target_pairs={{0,1},{1,2},{2,3},{3,0},{4,5},{5,6},{6,7},{7,4},{8,9},{9,10},{10,1... | collective-permute-start | bytes 196616 | tf_op jit(solution)/shard_map/ppermute | solution.py:285

commit v7 on v6

--- a/solution.py
+++ b/solution.py
@@ -179,29 +179,35 @@
     sweep(1, doc_start, {0: piece0, 1: piece1, 3: piece3}, kv, dq, dkv)
 
 
+def begin_two(doc_start, piece0, piece1, piece3, kv, dq_in, dkv, dq):
+    dkv[...] = jnp.zeros_like(dkv)
+    for slot in (0, 1, 3):
+        dq[slot] = dq_in[slot]
+    sweep(2, doc_start, {0: piece0, 1: piece1, 3: piece3}, kv, dq, dkv)
+
+
 def round_kv(dkv, out):
     out[:, :, :DH] = (dkv[:, :, :DH] * SCALE).astype(BF16)
     out[:, :, DH:] = dkv[:, :, DH:].astype(BF16)
 
 
 def finish_earlier(
-    doc_start, piece0, piece1, piece2, piece3, kv_two, kv_one, dkv_in, dq_in,
-    two_out, one_out, dq, dkv_two, dkv,
+    doc_start, piece2, kv_two, kv_one, two_in, one_in, two_out, one_out, late, two, one
 ):
-    for slot in (0, 1, 3):
-        dq[slot] = dq_in[slot]
-    dq[2] = jnp.zeros((DH, WIDE), F32)
-    dkv_two[...] = jnp.zeros_like(dkv_two)
-    sweep(2, doc_start, {0: piece0, 1: piece1, 2: piece2, 3: piece3}, kv_two, dq, dkv_two)
-    round_kv(dkv_two, two_out)
+    late[...] = jnp.zeros_like(late)
+    two[...] = two_in[...]
+    one[...] = one_in[...]
+    sweep(2, doc_start, {2: piece2}, kv_two, Shifted(late), two)
+    round_kv(two, two_out)
+    sweep(1, doc_start, {2: piece2}, kv_one, Shifted(late), one)
+    round_kv(one, one_out)
+
+
+def finish_own(
+    doc_start, piece2, kv, dkv_in, dq_in, late_in, dkv, out0, out1, out2, out3, late
+):
     dkv[...] = dkv_in[...]
-    sweep(1, doc_start, {2: piece2}, kv_one, dq, dkv)
-    round_kv(dkv, one_out)
-
-
-def finish_own(doc_start, piece2, kv, dkv_in, dq_in, dkv, out0, out1, out2, out3, late):
-    dkv[...] = dkv_in[...]
-    late[0] = dq_in[2]
+    late[...] = late_in[...]
     sweep(0, doc_start, {2: piece2}, kv, Shifted(late), dkv)
     dkv[:, :, :DH] = dkv[:, :, :DH] * SCALE
     for slot, out in enumerate((out0, out1, out2, out3)):
@@ -327,8 +333,9 @@
         grant=52,
     )(queries, outputs, out_grads, turned)
     far, kv_late = lax.optimization_barrier((far, kv_late))
+    kv_two = along_rows(kv_late, 2)
+    piece1, piece3, far = lax.optimization_barrier((piece1, piece3, far))
     piece2 = along_row(far, 2)
-    kv_two = along_rows(kv_late, 2)
 
     dkv_own, dq = kernel(
         begin_own, "begin_own", [SMEM] + [VMEM] * 4, [(kv_shape, F32), dq_shape], cost=HEAVY
@@ -336,24 +343,32 @@
     dkv_one, dq = kernel(
         begin_one, "begin_one", [SMEM] + [VMEM] * 5, [(kv_shape, F32), dq_shape], cost=HEAVY
     )(doc_start, piece0, piece1, piece3, kv_one, dq)
-    dkv_two, dkv_one, dq = kernel(
+    dkv_two, dq = kernel(
+        begin_two,
+        "begin_two",
+        [SMEM] + [VMEM] * 5,
+        [(late_shape, F32), dq_shape],
+        cost=HEAVY,
+    )(doc_start, piece0, piece1, piece3, kv_two, dq)
+    far_shape = ((1, DH, WIDE), F32)
+    dkv_two, dkv_one, dq_far = kernel(
         finish_earlier,
         "finish_earlier",
-        [SMEM] + [VMEM] * 8,
-        [(late_shape, BF16), (kv_shape, BF16), dq_shape],
+        [SMEM] + [VMEM] * 5,
+        [(late_shape, BF16), (kv_shape, BF16), far_shape],
         [pltpu.VMEM(late_shape, F32), pltpu.VMEM(kv_shape, F32)],
         cost=HEAVY,
-    )(doc_start, piece0, piece1, piece2, piece3, kv_two, kv_one, dkv_one, dq)
+    )(doc_start, piece2, kv_two, kv_one, dkv_two, dkv_one)
     back_two = along_rows(dkv_two, -2)
     back_one = along_rows(dkv_one, -1)
     dkv_own, *dq_sent = kernel(
         finish_own,
         "finish_own",
-        [SMEM] + [VMEM] * 4,
+        [SMEM] + [VMEM] * 5,
         [(kv_shape, F32)] + [((BLOCK, WIDE), BF16)] * ROW,
-        [pltpu.VMEM((1, DH, WIDE), F32)],
+        [pltpu.VMEM(*far_shape)],
         cost=HEAVY,
-    )(doc_start, piece2, kv_own, dkv_own, dq)
+    )(doc_start, piece2, kv_own, dkv_own, dq, dq_far)
     dq_pieces = [along_row(dq_sent[slot], -slot) for slot in range(ROW)]
     (query_out,) = kernel(
         join_queries,

time: 82.5 us -> 79.6 us (0.965)
  starting transfers between devices: 40.3 us -> 30.9 us
  waiting for transfers between devices: 22.4 us -> 28.2 us
    ppermute x4, starting transfers between devices: 23.5 us -> 15.9 us  [along_rows(): lax.ppermute(value, AXES, [(b, (b + by) % total) for b in range(total)])]
    ppermute x4, waiting for transfers between devices: 16.2 us -> 22.3 us  [along_rows(): lax.ppermute(value, AXES, [(b, (b + by) % total) for b in range(total)])]
    ppermute x12, starting transfers between devices: 16.8 us -> 15 us  [along_row(): return lax.ppermute(value, AXES, pairs)]
    pallas_call x2 -> x3, Pallas kernels: 4.99 us -> 5.57 us  [the longest x1 2.46 us: per_device(): kernel(finish_own, 'finish_own', [SMEM] + [VMEM] * 5, [(kv_shape, F32)] +...]
  transfers between devices with their start and end apart: 16 -> 16, of which waited for: 7 -> 7; matrix products, arithmetic and copies ran while one was open for 0% -> 0% of each run, Pallas kernels for 14% -> 17%
where the time goes in v7:
time: 79.6 us; the launch traced here: 79.1 us
  starting transfers between devices  30.9 us (39%)
  waiting for transfers between devices  28.2 us (35%)
  Pallas kernels  18.2 us (23%)
  between operations  0.91 us (1%)
  local copies, waits for them, and re-layouts  0.85 us (1%)
    ppermute x4, waiting for transfers between devices, along_rows(): lax.ppermute(value, AXES, [(b, (b + by) % total) for b in range(total)])  22.3 us
    ppermute x4, starting transfers between devices, along_rows(): lax.ppermute(value, AXES, [(b, (b + by) % total) for b in range(total)])  15.9 us
    ppermute x12, starting transfers between devices, along_row(): return lax.ppermute(value, AXES, pairs)  15 us
    ppermute x12, waiting for transfers between devices, along_row(): return lax.ppermute(value, AXES, pairs)  5.9 us
    pallas_call x1, Pallas kernels, per_device(): kernel(functools.partial(pack, (1, 3)), 'pack_near', [HBM] * 6, [((BLOCK,...  3.16 us
    pallas_call x1, Pallas kernels, per_device(): kernel(begin_one, 'begin_one', [SMEM] + [VMEM] * 5, [(kv_shape, F32), dq_...  2.89 us
    pallas_call x1, Pallas kernels, per_device(): kernel(begin_own, 'begin_own', [SMEM] + [VMEM] * 4, [(kv_shape, F32), dq_...  2.61 us
    pallas_call x1, Pallas kernels, per_device(): kernel(finish_own, 'finish_own', [SMEM] + [VMEM] * 5, [(kv_shape, F32)] +...  2.46 us
  transfers between devices with their start and end apart: 16, of which 7 were waited for; matrix products, arithmetic and copies ran while one was open for 0% of the time, Pallas kernels for 17%

profile of v7, /device:TPU:1, one launch (start us, length us, event | category | flops | bytes accessed | tf_op | source)
XLA Modules:
  0.0 79.1 jit_solution(223418747214486382)
XLA Ops:
  0.6 0.0 copy-start.1
  0.6 3.2 %pack_near.1 = (bf16[128,256]{1,0:T(8,128)(2,1)}, bf16[128,256]{1,0:T(8,128)(2,1)}, bf16[128,256]{1,0:T(8,128)(2,1)}, bf16[128,256]{1,0:T(8,128)(2,1)}, bf16[272...) custom-call(bf16[128,4096]{1,0:T(8,128)(2,1)} %queries.3, bf16[128,4096]{1,0:T(8,128)(2,1)} %outputs.3, ...), custom_call_target="tpu_custom_call" | custom-call | tf_op jit(solution)/shard_map/pack_near/pallas_call | solution.py:310
  3.8 0.0 copy-start.2
  3.8 2.2 %collective-permute-start = (bf16[128,256]{1,0:T(8,128)(2,1)}, bf16[128,256]{1,0:T(8,128)(2,1)S(1)}, u32[]{:S(2)}, u32[]{:S(2)}) collective-permute-start(bf16[128,256]{1,0:T(8,128)(2,1)} %get-tuple-element.47), channel_id=1, source_target_pairs={{0,1},{1,2},{2,3},{3,0},{4,5},{5,6},{6,7},{7,4},{8,9},{9,10},{10,1... | collective-permute-start | bytes 196616 | tf_op jit(solution)/shard_map/ppermute | solution.py:291
  6.0 2.6 %collective-permute-start.1 = (bf16[128,256]{1,0:T(8,128)(2,1)}, bf16[128,256]{1,0:T(8,128)(2,1)S(1)}, u32[]{:S(2)}, u32[]{:S(2)}) collective-permute-start(bf16[128,256]{1,0:T(8,128)(2,1)} %get-tuple-element.48), channel_id=1, source_target_pairs={{0,2},{1,3},{2,0},{3,1},{4,6},{5,7},{6,4},{7,5},{8,10},{9,11},{10,... | collective-permute-start | bytes 196616 | tf_op jit(solution)/shard_map/ppermute | solution.py:291
  8.6 1.1 %collective-permute-start.2 = (bf16[128,256]{1,0:T(8,128)(2,1)}, bf16[128,256]{1,0:T(8,128)(2,1)S(1)}, u32[]{:S(2)}, u32[]{:S(2)}) collective-permute-start(bf16[128,256]{1,0:T(8,128)(2,1)} %get-tuple-element.49), channel_id=1, source_target_pairs={{0,3},{1,0},{2,1},{3,2},{4,7},{5,4},{6,5},{7,6},{8,11},{9,8},{10,9... | collective-permute-start | bytes 196616 | tf_op jit(solution)/shard_map/ppermute | solution.py:291
  9.7 0.0 collective-permute-done.piece1
  9.7 1.7 %collective-permute-done.1.piece2 = bf16[128,256]{1,0:T(8,128)(2,1)S(1)} collective-permute-done((bf16[128,256]{1,0:T(8,128)(2,1)}, bf16[128,256]{1,0:T(8,128)(2,1)S(1)}, u32[]{:S(2)}, u32[]{:S(2)}) %collective-permute-start.1) | collective-permute-done | bytes 65568 | tf_op jit(solution)/shard_map/ppermute | solution.py:291
  11.5 0.8 %collective-permute-done.2.piece3 = bf16[128,256]{1,0:T(8,128)(2,1)S(1)} collective-permute-done((bf16[128,256]{1,0:T(8,128)(2,1)}, bf16[128,256]{1,0:T(8,128)(2,1)S(1)}, u32[]{:S(2)}, u32[]{:S(2)}) %collective-permute-start.2) | collective-permute-done | bytes 65568 | tf_op jit(solution)/shard_map/ppermute | solution.py:291
  12.3 0.0 collective-permute-start.3
  12.3 2.7 %collective-permute-start.4 = (bf16[272,1024]{1,0:T(8,128)(2,1)}, bf16[272,1024]{1,0:T(8,128)(2,1)S(1)}, u32[]{:S(2)}, u32[]{:S(2)}) collective-permute-start(bf16[272,1024]{1,0:T(8,128)(2,1)} %get-tuple-element.53), channel_id=1, source_target_pairs={{0,3},{1,0},{2,1},{3,2},{4,7},{5,4},{6,5},{7,6},{8,11},{9,8},{10,9... | collective-permute-start | bytes 1671176 | tf_op jit(solution)/shard_map/ppermute | solution.py:291
  14.9 0.0 copy-start
  15.0 0.8 %copy-done = bf16[128,256]{1,0:T(8,128)(2,1)S(1)} copy-done((bf16[128,256]{1,0:T(8,128)(2,1)S(1)}, bf16[128,256]{1,0:T(8,128)(2,1)}, u32[]{:S(2)}) %copy-start) | copy-done | bytes 65560
  15.8 3.1 %collective-permute-start.7 = (bf16[4,128,256]{2,1,0:T(8,128)(2,1)S(1)}, bf16[4,128,256]{2,1,0:T(8,128)(2,1)S(1)}, u32[]{:S(2)}, u32[]{:S(2)}) collective-permute-start(bf16[4,128,256]{2,1,0:T(8,128)(2,1)S(1)} %get-tuple-element.64.kv), channel_id=1, source_target_pairs={{0,4},{1,5},{2,6},{3,7},{4,8},{5,9},{6,10},{7,11},{8,12},{9,13},{1... | collective-permute-start | bytes 786440 | tf_op jit(solution)/shard_map/ppermute | solution.py:295
  18.9 0.0 copy-done.1
  18.9 2.1 %pack_rest.1 = (bf16[272,1024]{1,0:T(8,128)(2,1)S(1)}, bf16[272,1024]{1,0:T(8,128)(2,1)S(1)}) custom-call(bf16[128,4096]{1,0:T(8,128)(2,1)} %queries.3, bf16[128,4096]{1,0:T(8,128)(2,1)} %outputs.3, bf16[128,4096]{1,0:T(8,128)(2,1)} %grads.3, bf16[32,128]{1,0:T(8,128)(2,1)S(1)} %bitcast.2), custom_call_target="tpu_custom_call" | custom-call | tf_op jit(solution)/shard_map/pack_rest/pallas_call | solution.py:327
  21.0 5.2 %collective-permute-start.6 = (bf16[3,128,256]{2,1,0:T(8,128)(2,1)S(1)}, bf16[3,128,256]{2,1,0:T(8,128)(2,1)S(1)}, u32[]{:S(2)}, u32[]{:S(2)}) collective-permute-start(bf16[3,128,256]{2,1,0:T(8,128)(2,1)S(1)} %get-tuple-element.69), channel_id=1, source_target_pairs={{0,8},{1,9},{2,10},{3,11},{4,12},{5,13},{6,14},{7,15},{8,16},{9,17... | collective-permute-start | bytes 589832 | tf_op jit(solution)/shard_map/ppermute | solution.py:295
  26.2 0.0 collective-permute-done.3.piece1
  26.2 0.0 collective-permute-done.4.piece3
  26.2 0.8 collective-permute-start.5
  27.0 0.0 copy-done.2
  27.0 2.6 %begin_own.1 = (f32[4,128,256]{2,1,0:T(8,128)S(1)}, f32[4,128,1024]{2,1,0:T(8,128)S(1)}) custom-call(s32[16]{0:T(128)S(1)} %copy-done.2, bf16[272,1024]{1,0:T(8,128)(2,1)S(1)} %get-tuple-element.65.piece0, bf16[272,1024]{1,0:T(8,128)(2,1)S(1)} %collective-permute-done.3.piece1, bf16[272,1024]{1,0:T(8,128)(2,1)S(1)} %collective-permute-done.4.piece3, ...), custom_call_target="tpu_custom_call" | custom-call | flops 20000000000 | bytes 20000000000 | tf_op jit(solution)/shard_map/begin_own/pallas_call | solution.py:340
  29.6 2.1 %collective-permute-done.7.kv.kv_one = bf16[4,128,256]{2,1,0:T(8,128)(2,1)S(1)} collective-permute-done((bf16[4,128,256]{2,1,0:T(8,128)(2,1)S(1)}, bf16[4,128,256]{2,1,0:T(8,128)(2,1)S(1)}, u32[]{:S(2)}, u32[]{:S(2)}) %collective-permute-start.7) | collective-permute-done | bytes 262176 | tf_op jit(solution)/shard_map/ppermute | solution.py:295
  31.7 2.9 %begin_one.1 = (f32[4,128,256]{2,1,0:T(8,128)S(1)}, f32[4,128,1024]{2,1,0:T(8,128)S(1)}) custom-call(s32[16]{0:T(128)S(1)} %copy-done.2, bf16[272,1024]{1,0:T(8,128)(2,1)S(1)} %get-tuple-element.65.piece0, bf16[272,1024]{1,0:T(8,128)(2,1)S(1)} %collective-permute-done.3.piece1, bf16[272,1024]{1,0:T(8,128)(2,1)S(1)} %collective-permute-done.4.piece3, ...), custom_call_target="tpu_custom_call" | custom-call | flops 20000000000 | bytes 20000000000 | tf_op jit(solution)/shard_map/begin_one/pallas_call | solution.py:343
  34.6 6.9 %collective-permute-done.6.kv.kv_two = bf16[3,128,256]{2,1,0:T(8,128)(2,1)S(1)} collective-permute-done((bf16[3,128,256]{2,1,0:T(8,128)(2,1)S(1)}, bf16[3,128,256]{2,1,0:T(8,128)(2,1)S(1)}, u32[]{:S(2)}, u32[]{:S(2)}) %collective-permute-start.6) | collective-permute-done | bytes 196640 | tf_op jit(solution)/shard_map/ppermute | solution.py:295
  41.4 2.3 %begin_two.1 = (f32[3,128,256]{2,1,0:T(8,128)S(1)}, f32[4,128,1024]{2,1,0:T(8,128)S(1)}) custom-call(s32[16]{0:T(128)S(1)} %copy-done.2, bf16[272,1024]{1,0:T(8,128)(2,1)S(1)} %get-tuple-element.65.piece0, bf16[272,1024]{1,0:T(8,128)(2,1)S(1)} %collective-permute-done.3.piece1, bf16[272,1024]{1,0:T(8,128)(2,1)S(1)} %collective-permute-done.4.piece3, ...), custom_call_target="tpu_custom_call" | custom-call | flops 20000000000 | bytes 20000000000 | tf_op jit(solution)/shard_map/begin_two/pallas_call | solution.py:346
  43.8 0.0 collective-permute-done.5.piece2
  43.8 0.8 finish_earlier.1
  44.6 5.4 %collective-permute-start.12 = (bf16[3,128,256]{2,1,0:T(8,128)(2,1)S(1)}, bf16[3,128,256]{2,1,0:T(8,128)(2,1)S(1)}, u32[]{:S(2)}, u32[]{:S(2)}) collective-permute-start(bf16[3,128,256]{2,1,0:T(8,128)(2,1)S(1)} %get-tuple-element.82), channel_id=1, source_target_pairs={{0,248},{1,249},{2,250},{3,251},{4,252},{5,253},{6,254},{7,255},{8... | collective-permute-start | bytes 589832 | tf_op jit(solution)/shard_map/ppermute | solution.py:295
  49.9 2.3 %collective-permute-start.11 = (bf16[4,128,256]{2,1,0:T(8,128)(2,1)S(1)}, bf16[4,128,256]{2,1,0:T(8,128)(2,1)S(1)}, u32[]{:S(2)}, u32[]{:S(2)}) collective-permute-start(bf16[4,128,256]{2,1,0:T(8,128)(2,1)S(1)} %get-tuple-element.81), channel_id=1, source_target_pairs={{0,252},{1,253},{2,254},{3,255},{4,0},{5,1},{6,2},{7,3},{8,4},{9,5... | collective-permute-start | bytes 786440 | tf_op jit(solution)/shard_map/ppermute | solution.py:295
  52.2 2.5 %finish_own.1 = (f32[4,128,256]{2,1,0:T(8,128)S(1)}, bf16[128,1024]{1,0:T(8,128)(2,1)S(1)}, bf16[128,1024]{1,0:T(8,128)(2,1)S(1)}, bf16[128,1024]{1,0:T(8,128)(2,1)S(1)}, bf16[128,1024]{1,0:T(8,128)(2,1)S(1)}) custom-call(s32[16]{0:T(128)S(1)} %copy-done.2, bf16[272,1024]{1,0:T(8,128)(2,1)S(1)} %collective-permute-done.5.piece2, ...), custom_call_target="tpu_custom_call" | custom-call | flops 20000000000 | bytes 20000000000 | tf_op jit(solution)/shard_map/finish_own/pallas_call | solution.py:364
  54.7 0.4 collective-permute-start.8
  55.0 1.9 %collective-permute-start.9 = (bf16[128,1024]{1,0:T(8,128)(2,1)S(1)}, bf16[128,1024]{1,0:T(8,128)(2,1)S(1)}, u32[]{:S(2)}, u32[]{:S(2)}) collective-permute-start(bf16[128,1024]{1,0:T(8,128)(2,1)S(1)} %get-tuple-element.78), channel_id=1, source_target_pairs={{0,2},{1,3},{2,0},{3,1},{4,6},{5,7},{6,4},{7,5},{8,10},{9,11},{10,... | collective-permute-start | bytes 786440 | tf_op jit(solution)/shard_map/ppermute | solution.py:291
  56.9 0.8 collective-permute-start.10
  57.7 0.0 collective-permute-done.12.two
  57.7 13.4 %collective-permute-done.11.one = bf16[4,128,256]{2,1,0:T(8,128)(2,1)S(1)} collective-permute-done((bf16[4,128,256]{2,1,0:T(8,128)(2,1)S(1)}, bf16[4,128,256]{2,1,0:T(8,128)(2,1)S(1)}, u32[]{:S(2)}, u32[]{:S(2)}) %collective-permute-start.11) | collective-permute-done | bytes 262176 | tf_op jit(solution)/shard_map/ppermute | solution.py:295
  71.0 0.1 add_up.1
  71.1 2.0 %collective-permute-start.13 = (bf16[128,256]{1,0:T(8,128)(2,1)S(1)}, bf16[128,256]{1,0:T(8,128)(2,1)S(1)}, u32[]{:S(2)}, u32[]{:S(2)}) collective-permute-start(bf16[128,256]{1,0:T(8,128)(2,1)S(1)} %get-tuple-element.84), channel_id=1, source_target_pairs={{0,3},{1,0},{2,1},{3,2},{4,7},{5,4},{6,5},{7,6},{8,11},{9,8},{10,9... | collective-permute-start | bytes 196616 | tf_op jit(solution)/shard_map/ppermute | solution.py:291
  73.1 0.0 collective-permute-start.14
  73.1 0.0 collective-permute-done.8.piece1
  73.1 0.7 collective-permute-start.15
  73.8 0.0 collective-permute-done.9.piece2
  73.8 0.0 collective-permute-done.10.piece3
  73.8 1.0 %join_queries.1 = bf16[128,4096]{1,0:T(8,128)(2,1)} custom-call(bf16[128,1024]{1,0:T(8,128)(2,1)S(1)} %get-tuple-element.76.piece0, bf16[128,1024]{1,0:T(8,128)(2,1)S(1)} %collective-permute-done.8.piece1, bf16[128,1024]{1,0:T(8,128)(2,1)S(1)} %collective-permute-done.9.piece2, bf16[128,1024]{1,0:T(8,128)(2,1)S(1)} %collective-permute-done.10.piece3), custom_call_target="tpu_custom_call" | custom-call | tf_op jit(solution)/shard_map/join_queries/pallas_call | solution.py:373
  74.8 0.0 collective-permute-done.13.piece1
  74.8 3.0 %collective-permute-done.14.piece2 = bf16[128,256]{1,0:T(8,128)(2,1)S(1)} collective-permute-done((bf16[128,256]{1,0:T(8,128)(2,1)S(1)}, bf16[128,256]{1,0:T(8,128)(2,1)S(1)}, u32[]{:S(2)}, u32[]{:S(2)}) %collective-permute-start.14) | collective-permute-done | bytes 65568 | tf_op jit(solution)/shard_map/ppermute | solution.py:291
  77.9 0.3 collective-permute-done.15.piece3
  78.2 0.8 join_kv.1
  (1 shorter events, 0.0 us)
Async XLA Ops:
  0.6 18.3 %copy-start.1 = (bf16[128,32]{0,1:T(8,128)(2,1)S(1)}, bf16[128,32]{0,1:T(8,128)(2,1)}, u32[]{:S(2)}) copy-start(bf16[128,32]{0,1:T(8,128)(2,1)} %param.10) | copy-start | bytes 24580
  3.8 23.2 %copy-start.2 = (s32[16]{0:T(128)S(1)}, s32[16]{0:T(128)}, u32[]{:S(2)}) copy-start(s32[16]{0:T(128)} %doc_start.9) | copy-start | bytes 196
  3.8 5.9 %collective-permute-start = (bf16[128,256]{1,0:T(8,128)(2,1)}, bf16[128,256]{1,0:T(8,128)(2,1)S(1)}, u32[]{:S(2)}, u32[]{:S(2)}) collective-permute-start(bf16[128,256]{1,0:T(8,128)(2,1)} %get-tuple-element.47), channel_id=1, source_target_pairs={{0,1},{1,2},{2,3},{3,0},{4,5},{5,6},{6,7},{7,4},{8,9},{9,10},{10,1... | collective-permute-start | bytes 196616 | tf_op jit(solution)/shard_map/ppermute | solution.py:291
  6.0 5.4 %collective-permute-start.1 = (bf16[128,256]{1,0:T(8,128)(2,1)}, bf16[128,256]{1,0:T(8,128)(2,1)S(1)}, u32[]{:S(2)}, u32[]{:S(2)}) collective-permute-start(bf16[128,256]{1,0:T(8,128)(2,1)} %get-tuple-element.48), channel_id=1, source_target_pairs={{0,2},{1,3},{2,0},{3,1},{4,6},{5,7},{6,4},{7,5},{8,10},{9,11},{10,... | collective-permute-start | bytes 196616 | tf_op jit(solution)/shard_map/ppermute | solution.py:291
  8.6 3.6 %collective-permute-start.2 = (bf16[128,256]{1,0:T(8,128)(2,1)}, bf16[128,256]{1,0:T(8,128)(2,1)S(1)}, u32[]{:S(2)}, u32[]{:S(2)}) collective-permute-start(bf16[128,256]{1,0:T(8,128)(2,1)} %get-tuple-element.49), channel_id=1, source_target_pairs={{0,3},{1,0},{2,1},{3,2},{4,7},{5,4},{6,5},{7,6},{8,11},{9,8},{10,9... | collective-permute-start | bytes 196616 | tf_op jit(solution)/shard_map/ppermute | solution.py:291
  12.3 13.9 %collective-permute-start.3 = (bf16[272,1024]{1,0:T(8,128)(2,1)}, bf16[272,1024]{1,0:T(8,128)(2,1)S(1)}, u32[]{:S(2)}, u32[]{:S(2)}) collective-permute-start(bf16[272,1024]{1,0:T(8,128)(2,1)} %get-tuple-element.52), channel_id=1, source_target_pairs={{0,1},{1,2},{2,3},{3,0},{4,5},{5,6},{6,7},{7,4},{8,9},{9,10},{10,1... | collective-permute-start | bytes 1671176 | tf_op jit(solution)/shard_map/ppermute | solution.py:291
  12.3 13.9 %collective-permute-start.4 = (bf16[272,1024]{1,0:T(8,128)(2,1)}, bf16[272,1024]{1,0:T(8,128)(2,1)S(1)}, u32[]{:S(2)}, u32[]{:S(2)}) collective-permute-start(bf16[272,1024]{1,0:T(8,128)(2,1)} %get-tuple-element.53), channel_id=1, source_target_pairs={{0,3},{1,0},{2,1},{3,2},{4,7},{5,4},{6,5},{7,6},{8,11},{9,8},{10,9... | collective-permute-start | bytes 1671176 | tf_op jit(solution)/shard_map/ppermute | solution.py:291
  14.9 0.8 %copy-start = (bf16[128,256]{1,0:T(8,128)(2,1)S(1)}, bf16[128,256]{1,0:T(8,128)(2,1)}, u32[]{:S(2)}) copy-start(bf16[128,256]{1,0:T(8,128)(2,1)} %get-tuple-element.54.piece0) | copy-start | bytes 196612
  15.8 15.8 %collective-permute-start.7 = (bf16[4,128,256]{2,1,0:T(8,128)(2,1)S(1)}, bf16[4,128,256]{2,1,0:T(8,128)(2,1)S(1)}, u32[]{:S(2)}, u32[]{:S(2)}) collective-permute-start(bf16[4,128,256]{2,1,0:T(8,128)(2,1)S(1)} %get-tuple-element.64.kv), channel_id=1, source_target_pairs={{0,4},{1,5},{2,6},{3,7},{4,8},{5,9},{6,10},{7,11},{8,12},{9,13},{1... | collective-permute-start | bytes 786440 | tf_op jit(solution)/shard_map/ppermute | solution.py:295
  21.0 20.5 %collective-permute-start.6 = (bf16[3,128,256]{2,1,0:T(8,128)(2,1)S(1)}, bf16[3,128,256]{2,1,0:T(8,128)(2,1)S(1)}, u32[]{:S(2)}, u32[]{:S(2)}) collective-permute-start(bf16[3,128,256]{2,1,0:T(8,128)(2,1)S(1)} %get-tuple-element.69), channel_id=1, source_target_pairs={{0,8},{1,9},{2,10},{3,11},{4,12},{5,13},{6,14},{7,15},{8,16},{9,17... | collective-permute-start | bytes 589832 | tf_op jit(solution)/shard_map/ppermute | solution.py:295
  26.2 17.6 %collective-permute-start.5 = (bf16[272,1024]{1,0:T(8,128)(2,1)S(1)}, bf16[272,1024]{1,0:T(8,128)(2,1)S(1)}, u32[]{:S(2)}, u32[]{:S(2)}) collective-permute-start(bf16[272,1024]{1,0:T(8,128)(2,1)S(1)} %get-tuple-element.63), channel_id=1, source_target_pairs={{0,2},{1,3},{2,0},{3,1},{4,6},{5,7},{6,4},{7,5},{8,10},{9,11},{10,... | collective-permute-start | bytes 1671176 | tf_op jit(solution)/shard_map/ppermute | solution.py:291
  44.6 13.1 %collective-permute-start.12 = (bf16[3,128,256]{2,1,0:T(8,128)(2,1)S(1)}, bf16[3,128,256]{2,1,0:T(8,128)(2,1)S(1)}, u32[]{:S(2)}, u32[]{:S(2)}) collective-permute-start(bf16[3,128,256]{2,1,0:T(8,128)(2,1)S(1)} %get-tuple-element.82), channel_id=1, source_target_pairs={{0,248},{1,249},{2,250},{3,251},{4,252},{5,253},{6,254},{7,255},{8... | collective-permute-start | bytes 589832 | tf_op jit(solution)/shard_map/ppermute | solution.py:295
  49.9 21.1 %collective-permute-start.11 = (bf16[4,128,256]{2,1,0:T(8,128)(2,1)S(1)}, bf16[4,128,256]{2,1,0:T(8,128)(2,1)S(1)}, u32[]{:S(2)}, u32[]{:S(2)}) collective-permute-start(bf16[4,128,256]{2,1,0:T(8,128)(2,1)S(1)} %get-tuple-element.81), channel_id=1, source_target_pairs={{0,252},{1,253},{2,254},{3,255},{4,0},{5,1},{6,2},{7,3},{8,4},{9,5... | collective-permute-start | bytes 786440 | tf_op jit(solution)/shard_map/ppermute | solution.py:295
  54.7 18.5 %collective-permute-start.8 = (bf16[128,1024]{1,0:T(8,128)(2,1)S(1)}, bf16[128,1024]{1,0:T(8,128)(2,1)S(1)}, u32[]{:S(2)}, u32[]{:S(2)}) collective-permute-start(bf16[128,1024]{1,0:T(8,128)(2,1)S(1)} %get-tuple-element.77), channel_id=1, source_target_pairs={{0,3},{1,0},{2,1},{3,2},{4,7},{5,4},{6,5},{7,6},{8,11},{9,8},{10,9... | collective-permute-start | bytes 786440 | tf_op jit(solution)/shard_map/ppermute | solution.py:291
  55.0 18.8 %collective-permute-start.9 = (bf16[128,1024]{1,0:T(8,128)(2,1)S(1)}, bf16[128,1024]{1,0:T(8,128)(2,1)S(1)}, u32[]{:S(2)}, u32[]{:S(2)}) collective-permute-start(bf16[128,1024]{1,0:T(8,128)(2,1)S(1)} %get-tuple-element.78), channel_id=1, source_target_pairs={{0,2},{1,3},{2,0},{3,1},{4,6},{5,7},{6,4},{7,5},{8,10},{9,11},{10,... | collective-permute-start | bytes 786440 | tf_op jit(solution)/shard_map/ppermute | solution.py:291
  56.9 16.9 %collective-permute-start.10 = (bf16[128,1024]{1,0:T(8,128)(2,1)S(1)}, bf16[128,1024]{1,0:T(8,128)(2,1)S(1)}, u32[]{:S(2)}, u32[]{:S(2)}) collective-permute-start(bf16[128,1024]{1,0:T(8,128)(2,1)S(1)} %get-tuple-element.79), channel_id=1, source_target_pairs={{0,1},{1,2},{2,3},{3,0},{4,5},{5,6},{6,7},{7,4},{8,9},{9,10},{10,1... | collective-permute-start | bytes 786440 | tf_op jit(solution)/shard_map/ppermute | solution.py:291
  71.1 3.7 %collective-permute-start.13 = (bf16[128,256]{1,0:T(8,128)(2,1)S(1)}, bf16[128,256]{1,0:T(8,128)(2,1)S(1)}, u32[]{:S(2)}, u32[]{:S(2)}) collective-permute-start(bf16[128,256]{1,0:T(8,128)(2,1)S(1)} %get-tuple-element.84), channel_id=1, source_target_pairs={{0,3},{1,0},{2,1},{3,2},{4,7},{5,4},{6,5},{7,6},{8,11},{9,8},{10,9... | collective-permute-start | bytes 196616 | tf_op jit(solution)/shard_map/ppermute | solution.py:291
  73.1 4.7 %collective-permute-start.14 = (bf16[128,256]{1,0:T(8,128)(2,1)S(1)}, bf16[128,256]{1,0:T(8,128)(2,1)S(1)}, u32[]{:S(2)}, u32[]{:S(2)}) collective-permute-start(bf16[128,256]{1,0:T(8,128)(2,1)S(1)} %get-tuple-element.85), channel_id=1, source_target_pairs={{0,2},{1,3},{2,0},{3,1},{4,6},{5,7},{6,4},{7,5},{8,10},{9,11},{10,... | collective-permute-start | bytes 196616 | tf_op jit(solution)/shard_map/ppermute | solution.py:291
  73.1 5.0 %collective-permute-start.15 = (bf16[128,256]{1,0:T(8,128)(2,1)S(1)}, bf16[128,256]{1,0:T(8,128)(2,1)S(1)}, u32[]{:S(2)}, u32[]{:S(2)}) collective-permute-start(bf16[128,256]{1,0:T(8,128)(2,1)S(1)} %get-tuple-element.86), channel_id=1, source_target_pairs={{0,1},{1,2},{2,3},{3,0},{4,5},{5,6},{6,7},{7,4},{8,9},{9,10},{10,1... | collective-permute-start | bytes 196616 | tf_op jit(solution)/shard_map/ppermute | solution.py:291
